TPU v7x, 32 devices: a whole 2x2x4 slice. The times are simulated.
32 devices in a mesh: cond: 2 (over core), pair: 4 (over z), dp: 4 (over y, x).
Axes of the slice: x: 2, y: 2, z: 4, core: 2. Of those that a mesh axis runs over, the one named last changes fastest.
Arguments:
- latents: float32 [8, 24, 24, 1536], P(('cond', 'dp'), 'pair'), may hold values from -6 to 6
- ratio_embed: float32 [8, 64], P(('cond', 'dp')), may hold values from -6 to 6
- clip_tokens: float32 [8, 76, 1280], P(('cond', 'dp'), 'pair'), may hold values from -6 to 6
- cotangent: float32 [8, 24, 24, 1536], P(('cond', 'dp'), 'pair'), may hold values from -6 to 6
- conv_kernel: float32 [3, 3, 1536], P(None, None, 'dp'), may hold values from -2 to 2
- conv_bias: float32 [1536], P('dp'), may hold values from -1.75 to 1.75
- expand_weight: float32 [1536, 6144], P('dp'), may hold values from -0.15625 to 0.15625
- expand_bias: float32 [6144], P('dp'), may hold values from -1.75 to 1.75
- response_gain: float32 [6144], P('dp'), may hold values from -3 to 3
- response_bias: float32 [6144], P('dp'), may hold values from -1.75 to 1.75
- reduce_weight: float32 [6144, 1536], P('dp'), may hold values from -0.078125 to 0.078125
- reduce_bias: float32 [1536], P('dp'), may hold values from -1.75 to 1.75
- ratio_weight: float32 [64, 3072], P('dp'), may hold values from -0.375 to 0.375
- ratio_bias: float32 [3072], P('dp'), may hold values from -1.75 to 1.75
- text_weight: float32 [1280, 1536], P('dp'), may hold values from -0.15625 to 0.15625
- text_bias: float32 [1536], P('dp'), may hold values from -1.75 to 1.75
- attend_weight: float32 [1536, 4608], P('dp'), may hold values from -0.15625 to 0.15625
- query_bias: float32 [1536], P('dp'), may hold values from -1.75 to 1.75
- value_bias: float32 [1536], P('dp'), may hold values from -1.75 to 1.75
- output_weight: float32 [1536, 1536], P('dp'), may hold values from -1.25 to 1.25
- output_bias: float32 [1536], P('dp'), may hold values from -1.75 to 1.75
Outputs:
- layer_output: float32 [8, 24, 24, 1536], P(('cond', 'dp'), 'pair')
- latent_grad: float32 [8, 24, 24, 1536], P(('cond', 'dp'), 'pair')
- tokens_grad: float32 [8, 76, 1280], P(('cond', 'dp'), 'pair')
- kernel_grad: float32 [3, 3, 1536], P(None, None, 'dp')
- convbias_grad: float32 [1536], P('dp')
- expand_grad: float32 [1536, 6144], P('dp')
- expbias_grad: float32 [6144], P('dp')
- gain_grad: float32 [6144], P('dp')
- respbias_grad: float32 [6144], P('dp')
- reduce_grad: float32 [6144, 1536], P('dp')
- redbias_grad: float32 [1536], P('dp')
- ratio_grad: float32 [64, 3072], P('dp')
- ratiobias_grad: float32 [3072], P('dp')
- mapper_grad: float32 [1280, 1536], P('dp')
- mapbias_grad: float32 [1536], P('dp')
- attend_grad: float32 [1536, 4608], P('dp')
- querybias_grad: float32 [1536], P('dp')
- valuebias_grad: float32 [1536], P('dp')
- output_grad: float32 [1536, 1536], P('dp')
- outbias_grad: float32 [1536], P('dp')
All inputs are finite; a program needn't handle non-finite values.
Results may differ from a plain program's by a relative error of at most 0.0003.
Values sent between devices are 32-bit elements; how exact they have to be, the bound alone decides.
A program may use at most 448 MiB of HBM per device.

v0:
```python
import functools

import jax
import jax.numpy as jnp
from jax import lax
from jax.sharding import PartitionSpec as P

HEADS = 24
HEAD_CHANNELS = 64


HIGHEST_ACCURACY = lax.Precision.HIGHEST
EPSILON = 1e-06


def extended(block, sides, width):
    for axis, dim in sides:
        count = lax.axis_size(axis)
        forward = [(i, i + 1) for i in range(count - 1)]
        backward = [(target, source) for source, target in forward]
        low = lax.ppermute(
            lax.slice_in_dim(block, block.shape[dim] - width, None, axis=dim), axis, forward
        )
        high = lax.ppermute(lax.slice_in_dim(block, 0, width, axis=dim), axis, backward)
        block = jnp.concatenate([low, block, high], axis=dim)
    return block


def layer_norm(values):
    centered = values - jnp.mean(values, axis=-1, keepdims=True)
    variance = jnp.mean(centered * centered, axis=-1, keepdims=True)
    return centered * lax.rsqrt(variance + EPSILON)


def matmul(left, right):
    return jnp.einsum("...k,kn->...n", left, right, precision=HIGHEST_ACCURACY)


def depthwise(row_padded, kernel, conv_shift):
    row_count = row_padded.shape[1] - 2
    col_count = row_padded.shape[2]
    padded = jnp.pad(row_padded, ((0, 0), (0, 0), (1, 1), (0, 0)))
    total_conv = conv_shift
    for row_off in range(3):
        for col_off in range(3):
            total_conv = (
                total_conv
                + padded[:, row_off : row_off + row_count, col_off : col_off + col_count, :]
                * kernel[row_off, col_off]
            )
    return total_conv


def front(row_padded, kernel, conv_shift, expand_w, expand_b):
    normed = layer_norm(depthwise(row_padded, kernel, conv_shift))
    flat = normed.reshape(normed.shape[0], normed.shape[1] * normed.shape[2], normed.shape[3])
    return jax.nn.gelu(matmul(flat, expand_w) + expand_b, approximate=False)


def response_mlp(activated, totals, resp_gain, resp_bias, reduce_w, reduce_b, residual):
    norms = jnp.sqrt(totals + EPSILON)
    scaled = norms / (jnp.mean(norms, axis=-1, keepdims=True) + EPSILON)
    response = resp_gain * (activated * scaled[:, None, :]) + resp_bias + activated
    return residual + matmul(response, reduce_w) + reduce_b


def modulate(hidden_one, ratio_w, ratio_b, embed):
    modulation = jnp.dot(embed, ratio_w, precision=HIGHEST_ACCURACY) + ratio_b
    chan_count = hidden_one.shape[-1]
    return hidden_one * (1.0 + modulation[:, None, :chan_count]) + modulation[:, None, chan_count:]


def project(hidden_two, tokens, map_w, map_b, attend_w, query_b, value_b):
    chan_count = hidden_two.shape[-1]
    normed = layer_norm(hidden_two)
    mapped = matmul(jax.nn.silu(tokens), map_w) + map_b
    source = jnp.concatenate([normed, mapped], axis=1)
    query_matrix = matmul(normed, attend_w[:, :chan_count]) + query_b
    key_value = matmul(source, attend_w[:, chan_count:])
    return (query_matrix, key_value[..., :chan_count], key_value[..., chan_count:] + value_b)


def divide_into_heads(values):
    return values.reshape(values.shape[:-1] + (HEADS, HEAD_CHANNELS))


def attend_single(triple):
    query_matrix, key_matrix, value_matrix = triple
    attention_scores = jnp.einsum(
        "iuy,ouy->uio",
        divide_into_heads(query_matrix),
        divide_into_heads(key_matrix),
        precision=HIGHEST_ACCURACY,
    ) * HEAD_CHANNELS ** (-0.5)
    top_score = jnp.max(attention_scores, axis=-1, keepdims=True)
    expo_terms = jnp.exp(attention_scores - top_score)
    expo_total = jnp.sum(expo_terms, axis=-1, keepdims=True)
    attention_probabilities = expo_terms / expo_total
    attended_output = jnp.einsum(
        "fvb,bfq->vfq",
        attention_probabilities,
        divide_into_heads(value_matrix),
        precision=HIGHEST_ACCURACY,
    )
    log_total = top_score + jnp.log(expo_total)
    return (attended_output.reshape(query_matrix.shape), log_total)


def attend_back_single(items):
    query_matrix, key_matrix, value_matrix, attended_output, log_total, grad_mix = items
    query_per_head = divide_into_heads(query_matrix)
    key_per_head = divide_into_heads(key_matrix)
    value_per_head = divide_into_heads(value_matrix)
    gradient_per_head = divide_into_heads(grad_mix)
    attention_scores = jnp.einsum(
        "iuy,ouy->uio", query_per_head, key_per_head, precision=HIGHEST_ACCURACY
    ) * HEAD_CHANNELS ** (-0.5)
    attention_probabilities = jnp.exp(attention_scores - log_total)
    probability_gradient = jnp.einsum(
        "iuy,ouy->uio", gradient_per_head, value_per_head, precision=HIGHEST_ACCURACY
    )
    delta_rows = jnp.einsum(
        "phd,phd->hp",
        gradient_per_head,
        divide_into_heads(attended_output),
        precision=HIGHEST_ACCURACY,
    )
    score_gradient = (
        attention_probabilities
        * (probability_gradient - delta_rows[..., None])
        * HEAD_CHANNELS ** (-0.5)
    )
    query_gradient = jnp.einsum(
        "fvb,bfq->vfq", score_gradient, key_per_head, precision=HIGHEST_ACCURACY
    )
    key_gradient = jnp.einsum(
        "gyu,ygx->ugx", score_gradient, query_per_head, precision=HIGHEST_ACCURACY
    )
    value_gradient = jnp.einsum(
        "gyu,ygx->ugx", attention_probabilities, gradient_per_head, precision=HIGHEST_ACCURACY
    )
    return (
        query_gradient.reshape(query_matrix.shape),
        key_gradient.reshape(key_matrix.shape),
        value_gradient.reshape(value_matrix.shape),
    )


def body(
    latents,
    ratio_embed,
    clip_tokens,
    cotangent,
    conv_kernel,
    conv_bias,
    expand_weight,
    expand_bias,
    response_gain,
    response_bias,
    reduce_weight,
    reduce_bias,
    ratio_weight,
    ratio_bias,
    text_weight,
    text_bias,
    attend_weight,
    query_bias,
    value_bias,
    output_weight,
    output_bias,
):
    gathered = (
        lax.all_gather(conv_kernel, "dp", axis=2, tiled=True),
        lax.all_gather(conv_bias, "dp", axis=0, tiled=True),
        lax.all_gather(expand_weight, "dp", axis=0, tiled=True),
        lax.all_gather(expand_bias, "dp", axis=0, tiled=True),
        lax.all_gather(response_gain, "dp", axis=0, tiled=True),
        lax.all_gather(response_bias, "dp", axis=0, tiled=True),
        lax.all_gather(reduce_weight, "dp", axis=0, tiled=True),
        lax.all_gather(reduce_bias, "dp", axis=0, tiled=True),
        lax.all_gather(ratio_weight, "dp", axis=0, tiled=True),
        lax.all_gather(ratio_bias, "dp", axis=0, tiled=True),
        lax.all_gather(text_weight, "dp", axis=0, tiled=True),
        lax.all_gather(text_bias, "dp", axis=0, tiled=True),
        lax.all_gather(attend_weight, "dp", axis=0, tiled=True),
        lax.all_gather(query_bias, "dp", axis=0, tiled=True),
        lax.all_gather(value_bias, "dp", axis=0, tiled=True),
        lax.all_gather(output_weight, "dp", axis=0, tiled=True),
        lax.all_gather(output_bias, "dp", axis=0, tiled=True),
    )
    (
        kernel,
        conv_shift,
        expand_w,
        expand_b,
        resp_gain,
        resp_bias,
        reduce_w,
        reduce_b,
        ratio_w,
        ratio_b,
        map_w,
        map_b,
        attend_w,
        query_b,
        value_b,
        out_w,
        out_b,
    ) = gathered
    lat_count, row_count, col_count, chan_count = latents.shape
    pixel_count = row_count * col_count
    row_padded = extended(latents, (("pair", 1),), 1)
    activated, front_pull = jax.vjp(front, row_padded, kernel, conv_shift, expand_w, expand_b)
    totals = lax.psum(jnp.sum(activated * activated, axis=1), "pair")
    residual = latents.reshape(lat_count, pixel_count, chan_count)
    hidden_one, mlp_pull = jax.vjp(
        response_mlp, activated, totals, resp_gain, resp_bias, reduce_w, reduce_b, residual
    )
    hidden_two, mod_pull = jax.vjp(
        functools.partial(modulate, embed=ratio_embed), hidden_one, ratio_w, ratio_b
    )
    (query_matrix, key_local, value_local), proj_pull = jax.vjp(
        project, hidden_two, clip_tokens, map_w, map_b, attend_w, query_b, value_b
    )
    key_matrix, value_matrix = (
        lax.all_gather(key_local, "pair", axis=1, tiled=True),
        lax.all_gather(value_local, "pair", axis=1, tiled=True),
    )
    attended_output, log_total = lax.map(attend_single, (query_matrix, key_matrix, value_matrix))
    result = hidden_two + matmul(attended_output, out_w) + out_b
    layer_output = result.reshape(latents.shape)
    grad_out = cotangent.reshape(lat_count, pixel_count, chan_count)
    out_w_grad = jnp.einsum("lpc,lpn->cn", attended_output, grad_out, precision=HIGHEST_ACCURACY)
    out_b_grad = jnp.sum(grad_out, axis=(0, 1))
    grad_mix = jnp.einsum("lpn,cn->lpc", grad_out, out_w, precision=HIGHEST_ACCURACY)
    query_gradient, key_gradient, value_gradient = lax.map(
        attend_back_single,
        (query_matrix, key_matrix, value_matrix, attended_output, log_total, grad_mix),
    )
    key_share, value_share = (
        lax.psum_scatter(key_gradient, "pair", scatter_dimension=1, tiled=True),
        lax.psum_scatter(value_gradient, "pair", scatter_dimension=1, tiled=True),
    )
    grad_two, tokens_grad, map_w_grad, map_b_grad, attend_w_grad, query_b_grad, value_b_grad = (
        proj_pull((query_gradient, key_share, value_share))
    )
    grad_two = grad_two + grad_out
    attend_shards = (
        lax.psum_scatter(map_w_grad, "dp", scatter_dimension=0, tiled=True),
        lax.psum_scatter(map_b_grad, "dp", scatter_dimension=0, tiled=True),
        lax.psum_scatter(attend_w_grad, "dp", scatter_dimension=0, tiled=True),
        lax.psum_scatter(query_b_grad, "dp", scatter_dimension=0, tiled=True),
        lax.psum_scatter(value_b_grad, "dp", scatter_dimension=0, tiled=True),
        lax.psum_scatter(out_w_grad, "dp", scatter_dimension=0, tiled=True),
        lax.psum_scatter(out_b_grad, "dp", scatter_dimension=0, tiled=True),
    )
    grad_one, ratio_w_grad, ratio_b_grad = mod_pull(grad_two)
    grad_act, grad_totals, gain_grad, respb_grad, reduce_w_grad, reduce_b_grad, grad_res = mlp_pull(
        grad_one
    )
    grad_totals = lax.psum(grad_totals, "pair")
    grad_act = grad_act + 2.0 * activated * grad_totals[:, None, :]
    grad_padded, kernel_grad, shift_grad, expand_w_grad, expand_b_grad = front_pull(grad_act)
    rim_rows = jnp.concatenate([grad_padded[:, :1], grad_padded[:, -1:]], axis=1)
    arrived = extended(rim_rows, (("pair", 1),), 1)
    inner_rows = grad_padded[:, 1:-1]
    inner_rows = inner_rows.at[:, 0].add(arrived[:, 0]).at[:, -1].add(arrived[:, 3])
    latent_grad = inner_rows + grad_res.reshape(latents.shape)
    block_shards = (
        lax.psum_scatter(kernel_grad, "dp", scatter_dimension=2, tiled=True),
        lax.psum_scatter(shift_grad, "dp", scatter_dimension=0, tiled=True),
        lax.psum_scatter(expand_w_grad, "dp", scatter_dimension=0, tiled=True),
        lax.psum_scatter(expand_b_grad, "dp", scatter_dimension=0, tiled=True),
        lax.psum_scatter(gain_grad, "dp", scatter_dimension=0, tiled=True),
        lax.psum_scatter(respb_grad, "dp", scatter_dimension=0, tiled=True),
        lax.psum_scatter(reduce_w_grad, "dp", scatter_dimension=0, tiled=True),
        lax.psum_scatter(reduce_b_grad, "dp", scatter_dimension=0, tiled=True),
        lax.psum_scatter(ratio_w_grad, "dp", scatter_dimension=0, tiled=True),
        lax.psum_scatter(ratio_b_grad, "dp", scatter_dimension=0, tiled=True),
    )
    shards = tuple(block_shards) + tuple(attend_shards)
    summed = lax.psum(shards, ("cond", "pair"))
    return (layer_output, latent_grad, tokens_grad) + tuple(summed)


def solution(mesh):
    return jax.shard_map(
        body,
        mesh=mesh,
        in_specs=(
            P(("cond", "dp"), "pair", None, None),
            P(("cond", "dp"), None),
            P(("cond", "dp"), "pair", None),
            P(("cond", "dp"), "pair", None, None),
            P(None, None, "dp"),
            P("dp"),
            P("dp", None),
            P("dp"),
            P("dp"),
            P("dp"),
            P("dp", None),
            P("dp"),
            P("dp", None),
            P("dp"),
            P("dp", None),
            P("dp"),
            P("dp", None),
            P("dp"),
            P("dp"),
            P("dp", None),
            P("dp"),
        ),
        out_specs=(
            P(("cond", "dp"), "pair", None, None),
            P(("cond", "dp"), "pair", None, None),
            P(("cond", "dp"), "pair", None),
            P(None, None, "dp"),
            P("dp"),
            P("dp", None),
            P("dp"),
            P("dp"),
            P("dp"),
            P("dp", None),
            P("dp"),
            P("dp", None),
            P("dp"),
            P("dp", None),
            P("dp"),
            P("dp", None),
            P("dp"),
            P("dp"),
            P("dp", None),
            P("dp"),
        ),
        check_vma=False,
    )
```

profile of v0, /device:TPU:16, one launch (start us, length us, event | category | flops | bytes accessed | tf_op | source)
XLA Modules:
  0.0 3507.4 jit_solution(2042247593550592681)
XLA Ops:
  40.3 12.6 all_gather.65
  109.9 324.6 %all-gather.18.cloned.1.call-done = f32[1536,6144]{1,0:T(8,128)} async-done(((f32[384,6144]{1,0:T(8,128)}), f32[1536,6144]{1,0:T(8,128)}) %all-gather.18.cloned.1.call-update) | async-done | bytes 37748752 | tf_op jit(solution)/shard_map/all_gather | solution.py:175
  434.5 33.8 multiply_reduce_fusion.3
  468.3 17.4 psum.133
  487.2 282.3 %all-gather.20.cloned.1.call-done = f32[6144,1536]{1,0:T(8,128)} async-done(((f32[1536,1536]{1,0:T(8,128)}), f32[6144,1536]{1,0:T(8,128)}) %all-gather.20.cloned.1.call-update) | async-done | bytes 37748752 | tf_op jit(solution)/shard_map/all_gather | solution.py:179
  769.4 28.4 fusion.68
  798.3 226.5 %all-gather.24.cloned.1.call-done = f32[1536,4608]{1,0:T(8,128)} async-done(((f32[384,4608]{1,0:T(8,128)}), f32[1536,4608]{1,0:T(8,128)}) %all-gather.24.cloned.1.call-update) | async-done | bytes 28311568 | tf_op jit(solution)/shard_map/all_gather | solution.py:185
  1024.8 15.0 fusion.19
  1052.2 70.6 %all-gather.30.cloned.1.call-done = f32[1536,1536]{1,0:T(8,128)} async-done(((f32[384,1536]{1,0:T(8,128)}), f32[1536,1536]{1,0:T(8,128)}) %all-gather.30.cloned.1.call-update) | async-done | bytes 9437200 | tf_op jit(solution)/shard_map/all_gather | solution.py:188
  1122.9 11.3 fusion.113
  1144.8 56.3 %all-gather.28.cloned.1.call-done = f32[1,652,1536]{2,0,1:T(1,128)} async-done(((f32[1,163,1536]{2,0,1:T(1,128)}), f32[1,652,1536]{2,0,1:T(1,128)}) %all-gather.28.cloned.1.call-update) | async-done | bytes 4005904 | tf_op jit(solution)/shard_map/all_gather | solution.py:226
  1225.5 54.0 %all-gather.26.cloned.1.call-done = f32[1,652,1536]{2,0,1:T(1,128)} async-done(((f32[1,163,1536]{2,0,1:T(1,128)}), f32[1,652,1536]{2,0,1:T(1,128)}) %all-gather.26.cloned.1.call-update) | async-done | bytes 4005904 | tf_op jit(solution)/shard_map/all_gather | solution.py:227
  1288.8 17.2 fusion.57
  1315.2 13.4 multiply_multiply_fusion
  1358.3 15.6 bitcast_reduce_fusion
  1373.9 261.6 %all-reduce.49.cloned.1.call-done = (f32[1,652,1536]{2,0,1:T(1,128)}, f32[1,652,1536]{2,0,1:T(1,128)}) async-done(((f32[1,652,1536]{2,0,1:T(1,128)}, f32[1,652,1536]{2,0,1:T(1,128)}), (f32[1,652,1536]{2,0,1:T(1,128)}, f32[1,652,1536]{2,0,1:T(1,128)})) %all-reduce.49.cloned.1.call-update) | async-done | bytes 8011792
  1640.7 22.4 fusion.30
  1663.2 19.0 fusion.63
  1685.1 11.3 fusion.117
  1706.5 17.3 fusion.64
  1723.8 16.9 fusion.46
  1752.6 46.4 %multiply_reduce_fusion.1 = (f32[6144]{0:T(1024)}, f32[6144]{0:T(1024)S(1)}, f32[6144]{0:T(1024)}, f32[144,6144]{1,0:T(8,128)}) fusion(f32[144,6144]{1,0:T(8,128)} %get-tuple-element.240, f32[6144]{0:T(1024)S(1)} %bitcast.176, f32[6144]{0:T(1024)S(1)} %bitcast.180, f32[6144,1536]{1,0:T(8,128)} %all-gather.20.cloned.1.call-done, ...), kind=kOutput, calls=%fused_computation.28 | convolution fusion | flops 16313628672 | bytes 45834240 | tf_op jit(solution)/shard_map/transpose(jvp(...k,kn->...n))/dot_general | solution.py:36
  1800.5 15.3 psum.134
  1825.2 34.3 fusion.116
  1860.2 35.4 %fusion.28 = f32[6144,1536]{1,0:T(8,128)} fusion(f32[144,6144]{1,0:T(8,128)} %get-tuple-element.240, f32[6144]{0:T(1024)S(1)} %bitcast.184, f32[6144]{0:T(1024)S(1)} %bitcast.178, f32[6144]{0:T(1024)S(1)} %bitcast.182, f32[1,144,1536]{2,1,0:T(8,128)S(1)} %get-tuple-element.235), kind=kOutput, calls=%fused_computation.47 | convolution fusion | flops 16310992896 | bytes 42246144 | tf_op jit(solution)/shard_map/transpose(jvp(...k,kn->...n))/dot_general | solution.py:36
  1898.1 43.0 %fusion.115 = f32[144,1536]{1,0:T(8,128)S(1)} fusion(f32[144,6144]{1,0:T(8,128)} %copy-done.4, f32[1536,6144]{1,0:T(8,128)} %all-gather.18.cloned.1.call-done), kind=kOutput, calls=%fused_computation.205 | convolution fusion | flops 16307453952 | bytes 42172416 | tf_op jit(solution)/shard_map/transpose(jvp(...k,kn->...n))/dot_general | solution.py:36
  1953.4 193.9 %reduce-scatter.18.cloned.1.call-done = f32[384,4608]{1,0:T(8,128)} async-done(((f32[1536,4608]{1,0:T(8,128)}), f32[384,4608]{1,0:T(8,128)}) %reduce-scatter.18.cloned.1.call-update) | async-done | bytes 7077904 | tf_op jit(solution)/shard_map/reduce_scatter | solution.py:251
  2147.3 326.0 %reduce-scatter.10.cloned.1.call-done = f32[384,6144]{1,0:T(8,128)} async-done(((f32[1536,6144]{1,0:T(8,128)}), f32[384,6144]{1,0:T(8,128)}) %reduce-scatter.10.cloned.1.call-update) | async-done | bytes 9437200 | tf_op jit(solution)/shard_map/reduce_scatter | solution.py:272
  2473.2 325.5 %reduce-scatter.12.cloned.1.call-done = f32[1536,1536]{1,0:T(8,128)} async-done(((f32[6144,1536]{1,0:T(8,128)}), f32[1536,1536]{1,0:T(8,128)}) %reduce-scatter.12.cloned.1.call-update) | async-done | bytes 9437200 | tf_op jit(solution)/shard_map/reduce_scatter | solution.py:276
  2842.1 36.2 %all-reduce.47.cloned.1.call-done = (f32[1536]{0:T(1024)}, f32[6144]{0:T(1024)}, f32[6144]{0:T(1024)}, f32[6144]{0:T(1024)}, f32[1536]{0:T(1024)}, /*index=5*/f3...) async-done(((f32[1536]{0:T(1024)}, f32[6144]{0:T(1024)}, f32[6144]{0:T(1024)}, f32[6144]{0:T(1024)}, f32[1536]{0:T(1024)}, ...) | async-done | bytes 122896
  2886.0 32.2 all-reduce.37
  2921.1 558.4 %all-reduce.45.cloned.1.call-done = (f32[384,6144]{1,0:T(8,128)}, f32[1536,1536]{1,0:T(8,128)}, f32[16,3072]{1,0:T(8,128)}, f32[320,1536]{1,0:T(8,128)}, f32[384,4608]{1,0:T(8,128)}, /*index=5*/f32[384,1536]{1,0:T(8,128)}) async-done(((f32[384,6144]{1,0:T(8,128)}, f32[1536,1536]{1,0:T(8,128)}, f32[16,3072]{1,0:T(8,128)}, f32[320,1536]{1,0:T(8,128)}, f32[384,4608]{1,0:T(8,128)}, ...) | async-done | bytes 30474256 | tf_op jit(solution)/shard_map/psum | solution.py:282
  (346 shorter events, 313.7 us)
Async XLA Ops:
  7.2 96.3 %all-gather.22.cloned.1.call-start = ((), (), s32[]{:S(2)}) async-start(), calls=%async_computation.9 | async-start | bytes 9830400 | tf_op jit(solution)/shard_map/all_gather | solution.py:183
  7.9 426.6 %all-gather.18.cloned.1.call-start = ((), (), s32[]{:S(2)}) async-start(), calls=%async_computation.7 | async-start | bytes 47185920 | tf_op jit(solution)/shard_map/all_gather | solution.py:175
  8.7 760.7 %all-gather.20.cloned.1.call-start = ((), (), s32[]{:S(2)}) async-start(), calls=%async_computation.8 | async-start | bytes 47185920 | tf_op jit(solution)/shard_map/all_gather | solution.py:179
  9.5 1015.3 %all-gather.24.cloned.1.call-start = ((), (), s32[]{:S(2)}) async-start(), calls=%async_computation.10 | async-start | bytes 35389440 | tf_op jit(solution)/shard_map/all_gather | solution.py:185
  10.1 50.2 %copy-start.62 = (f32[1536]{0:T(1024)S(1)}, f32[1536]{0:T(1024)}, u32[]{:S(2)}) copy-start(f32[1536]{0:T(1024)} %param.34) | copy-start | bytes 18436
  10.1 50.2 %copy-start.63 = (f32[1536]{0:T(1024)S(1)}, f32[1536]{0:T(1024)}, u32[]{:S(2)}) copy-start(f32[1536]{0:T(1024)} %param.33) | copy-start | bytes 18436
  10.1 50.3 %copy-start.68 = (f32[384]{0:T(512)S(1)}, f32[384]{0:T(512)}, u32[]{:S(2)}) copy-start(f32[384]{0:T(512)} %param.43) | copy-start | bytes 4612
  10.1 81.5 %copy-start.60 = (f32[3,3,384]{2,1,0:T(4,128)S(1)}, f32[3,3,384]{2,1,0:T(4,128)}, u32[]{:S(2)}) copy-start(f32[3,3,384]{2,1,0:T(4,128)} %param.29) | copy-start | bytes 41476
  10.1 1112.8 %all-gather.30.cloned.1.call-start = ((), (), s32[]{:S(2)}) async-start(), calls=%async_computation.13 | async-start | bytes 11796480 | tf_op jit(solution)/shard_map/all_gather | solution.py:188
  10.7 1190.4 %all-gather.28.cloned.1.call-start = ((), (), s32[]{:S(2)}) async-start(), calls=%async_computation.12 | async-start | bytes 5007360 | tf_op jit(solution)/shard_map/all_gather | solution.py:226
  10.8 89.9 %collective-permute-start.1 = (f32[1,1,24,1536]{3,2,1,0:T(8,128)S(1)}, f32[1,1,24,1536]{3,2,1,0:T(8,128)S(1)}, u32[]{:S(2)}, u32[]{:S(2)}) collective-permute-start(f32[1,1,24,1536]{3,2,1,0:T(8,128)S(1)} %get-tuple-element.258), channel_id=1, source_target_pairs={{4,0},{8,4},{12,8},{5,1},{9,5},{13,9},{6,2},{10,6},{14,10},{7,3},{... | collective-permute-start | bytes 442376 | tf_op jit(solution)/shard_map/ppermute | solution.py:24
  13.2 87.6 %collective-permute-start = (f32[1,1,24,1536]{3,2,1,0:T(8,128)S(1)}, f32[1,1,24,1536]{3,2,1,0:T(8,128)S(1)}, u32[]{:S(2)}, u32[]{:S(2)}) collective-permute-start(f32[1,1,24,1536]{3,2,1,0:T(8,128)S(1)} %get-tuple-element.257), channel_id=1, source_target_pairs={{0,4},{4,8},{8,12},{1,5},{5,9},{9,13},{2,6},{6,10},{10,14},{3,7},{... | collective-permute-start | bytes 442376 | tf_op jit(solution)/shard_map/ppermute | solution.py:21
  84.6 684.9 %copy-start.31 = (f32[4,1,1536]{2,1,0:T(1,128)}, f32[4,1,1536]{2,1,0:T(1,128)S(1)}, u32[]{:S(2)}) copy-start(f32[4,1,1536]{2,1,0:T(1,128)S(1)} %all-gather.3) | copy-start | bytes 73732
  103.4 331.1 %copy-start.20 = (f32[1,6,24,1536]{3,2,1,0:T(8,128)}, f32[1,6,24,1536]{3,2,1,0:T(8,128)S(1)}, u32[]{:S(2)}) copy-start(f32[1,6,24,1536]{3,2,1,0:T(8,128)S(1)} %subtract_multiply_fusion) | copy-start | bytes 2654212
  485.8 312.1 %copy-start.29 = (f32[1,6144]{1,0:T(1,128)}, f32[1,6144]{1,0:T(1,128)S(1)}, u32[]{:S(2)}) copy-start(f32[1,6144]{1,0:T(1,128)S(1)} %psum.133) | copy-start | bytes 73732
  798.3 241.5 %copy-start.16 = (f32[1,144,1536]{2,1,0:T(8,128)}, f32[1,144,1536]{2,1,0:T(8,128)S(1)}, u32[]{:S(2)}) copy-start(f32[1,144,1536]{2,1,0:T(8,128)S(1)} %multiply_bitcast_fusion.1) | copy-start | bytes 2654212
  1040.0 82.9 %copy-start.11 = (f32[1,6,24,1536]{3,2,1,0:T(8,128)S(1)}, f32[1,6,24,1536]{3,2,1,0:T(8,128)}, u32[]{:S(2)}) copy-start(f32[1,6,24,1536]{3,2,1,0:T(8,128)} %param.28) | copy-start | bytes 2654212
  1042.0 237.5 %all-gather.26.cloned.1.call-start = ((), (), s32[]{:S(2)}) async-start(), calls=%async_computation.11 | async-start | bytes 5007360 | tf_op jit(solution)/shard_map/all_gather | solution.py:227
  1044.1 591.4 %all-reduce.49.cloned.1.call-start = ((), (), s32[]{:S(2)}) async-start(), calls=%async_computation.23 | async-start | bytes 16023552
  1144.8 65.5 %copy-start.10 = (f32[144,1536]{0,1:T(8,128)}, f32[144,1536]{0,1:T(8,128)S(1)}, u32[]{:S(2)}) copy-start(f32[144,1536]{0,1:T(8,128)S(1)} %copy.91) | copy-start | bytes 2654212
  1356.5 596.9 %reduce-scatter.14.cloned.1.call-start = ((), (), s32[]{:S(2)}) async-start(), calls=%async_computation.16 | async-start | bytes 983040 | tf_op jit(solution)/shard_map/reduce_scatter | solution.py:278
  1685.1 268.3 %reduce-scatter.20.cloned.1.call-start = ((), (), s32[]{:S(2)}) async-start(), calls=%async_computation.19 | async-start | bytes 11796480 | tf_op jit(solution)/shard_map/reduce_scatter | solution.py:254
  1696.5 256.9 %reduce-scatter.16.cloned.1.call-start = ((), (), s32[]{:S(2)}) async-start(), calls=%async_computation.17 | async-start | bytes 9830400 | tf_op jit(solution)/shard_map/reduce_scatter | solution.py:249
  1706.0 441.3 %reduce-scatter.18.cloned.1.call-start = ((), (), s32[]{:S(2)}) async-start(), calls=%async_computation.18 | async-start | bytes 35389440 | tf_op jit(solution)/shard_map/reduce_scatter | solution.py:251
  1750.8 722.5 %reduce-scatter.10.cloned.1.call-start = ((), (), s32[]{:S(2)}) async-start(), calls=%async_computation.14 | async-start | bytes 47185920 | tf_op jit(solution)/shard_map/reduce_scatter | solution.py:272
  1752.6 46.4 %copy-start.30 = (f32[1,6144]{1,0:T(1,128)S(1)}, f32[1,6144]{1,0:T(1,128)}, u32[]{:S(2)}) copy-start(f32[1,6144]{1,0:T(1,128)} %copy-done.29) | copy-start | bytes 73732
  1859.5 939.3 %reduce-scatter.12.cloned.1.call-start = ((), (), s32[]{:S(2)}) async-start(), calls=%async_computation.15 | async-start | bytes 47185920 | tf_op jit(solution)/shard_map/reduce_scatter | solution.py:276
  1895.6 943.0 %reduce-scatter.22.cloned.1.call-start = ((), (), s32[]{:S(2)}) async-start(), calls=%async_computation.20 | async-start | bytes 983040
  1951.6 926.7 %all-reduce.47.cloned.1.call-start = ((), (), s32[]{:S(2)}) async-start(), calls=%async_computation.22 | async-start | bytes 270336
  1953.3 1526.3 %all-reduce.45.cloned.1.call-start = ((), (), s32[]{:S(2)}) async-start(), calls=%async_computation.21 | async-start | bytes 60948480 | tf_op jit(solution)/shard_map/psum | solution.py:282
  2824.3 93.9 %collective-permute-start.2 = (f32[1,1,24,1536]{3,2,1,0:T(8,128)}, f32[1,1,24,1536]{3,2,1,0:T(8,128)}, u32[]{:S(2)}, u32[]{:S(2)}) collective-permute-start(f32[1,1,24,1536]{3,2,1,0:T(8,128)} %get-tuple-element.247), channel_id=1, source_target_pairs={{0,4},{4,8},{8,12},{1,5},{5,9},{9,13},{2,6},{6,10},{10,14},{3,7},{... | collective-permute-start | bytes 442376 | tf_op jit(solution)/shard_map/ppermute | solution.py:21
  2827.7 91.4 %collective-permute-start.3 = (f32[1,1,24,1536]{3,2,1,0:T(8,128)}, f32[1,1,24,1536]{3,2,1,0:T(8,128)}, u32[]{:S(2)}, u32[]{:S(2)}) collective-permute-start(f32[1,1,24,1536]{3,2,1,0:T(8,128)} %get-tuple-element.246), channel_id=1, source_target_pairs={{4,0},{8,4},{12,8},{5,1},{9,5},{13,9},{6,2},{10,6},{14,10},{7,3},{... | collective-permute-start | bytes 442376 | tf_op jit(solution)/shard_map/ppermute | solution.py:24
  (70 other events, 755.5 us)
Sparse Core Ops, SparseCore 0:
  9.9 89.4 all-gather.21
  101.2 333.2 all-gather.17
  436.4 332.9 all-gather.19
  771.1 253.5 all-gather.23
  1026.5 96.3 all-gather.29
  1124.9 76.2 all-gather.27
  1203.3 76.2 all-gather.25
  1356.6 278.9 all-reduce.48
  1685.2 26.0 reduce-scatter.13
  1714.9 94.9 reduce-scatter.19
  1813.5 83.3 reduce-scatter.15
  1899.8 247.3 reduce-scatter.17
  2150.7 322.5 reduce-scatter.9
  2476.2 322.5 reduce-scatter.11
  2802.3 26.0 reduce-scatter.21
  2834.0 44.2 all-reduce.46
  2881.4 598.0 all-reduce.44
where the time goes:
time: 3520 us; the launch traced here: 3510 us
  waiting for transfers between devices  2720 us (77%)
  matrix products  454 us (13%)
  blocking collectives  164 us (5%)
  local copies, waits for them, and re-layouts  93.7 us (3%)
  other arithmetic  42.8 us (1%)
    psum x1, waiting for transfers between devices, body(): summed = lax.psum(shards, ('cond', 'pair'))  558 us
    dot_general x16, matrix products, matmul(): return jnp.einsum('...k,kn->...n', left, right, precision=HIGHEST_ACCURACY)  355 us
    reduce_scatter x1, waiting for transfers between devices, body(): lax.psum_scatter(expand_w_grad, 'dp', scatter_dimension=0, tiled=True)  326 us
    reduce_scatter x1, waiting for transfers between devices, body(): lax.psum_scatter(reduce_w_grad, 'dp', scatter_dimension=0, tiled=True)  326 us
    all_gather x1, waiting for transfers between devices, body(): lax.all_gather(expand_weight, 'dp', axis=0, tiled=True)  325 us
    unnamed x20, waiting for transfers between devices  301 us
    all_gather x1, waiting for transfers between devices, body(): lax.all_gather(reduce_weight, 'dp', axis=0, tiled=True)  282 us
    all_gather x1, waiting for transfers between devices, body(): lax.all_gather(attend_weight, 'dp', axis=0, tiled=True)  226 us
  transfers between devices with their start and end apart: 21, of which 12 were waited for; matrix products, arithmetic and copies ran while one was open for 12% of the time, Pallas kernels for 0%

commit v1 on v0

--- a/solution.py
+++ b/solution.py
@@ -282,10 +282,365 @@
     summed = lax.psum(shards, ("cond", "pair"))
     return (layer_output, latent_grad, tokens_grad) + tuple(summed)
 
+FAST = lax.Precision.HIGH
+
+
+def dot(left, right):
+    return jnp.dot(left, right, precision=FAST)
+
+
+def dot_t(left, right):
+    return lax.dot_general(left, right, (((1,), (1,)), ((), ())), precision=FAST)
+
+
+def t_dot(left, right):
+    return lax.dot_general(left, right, (((0,), (0,)), ((), ())), precision=FAST)
+
+
+def partners(value, step):
+    return lax.ppermute(value, "dp", [(i, i ^ step) for i in range(4)])
+
+
+def gather_near(block):
+    return [block] + [partners(block, step) for step in (1, 2, 3)]
+
+
+def scatter_near(blocks):
+    arrived = [partners(blocks[step], step) for step in (1, 2, 3)]
+    return blocks[0] + arrived[0] + arrived[1] + arrived[2]
+
+
+def exchange_near(blocks, me):
+    near = jnp.stack([blocks[0]] + [partners(blocks[step], step) for step in (1, 2, 3)])
+    order = jnp.bitwise_xor(jnp.arange(4), me)
+    return jnp.take(near, order, axis=0)
+
+
+def other_core(value):
+    return lax.ppermute(value, "cond", [(0, 1), (1, 0)])
+
+
+def norm_stats(values):
+    centered = values - jnp.mean(values, axis=-1, keepdims=True)
+    variance = jnp.mean(centered * centered, axis=-1, keepdims=True)
+    inverse = lax.rsqrt(variance + EPSILON)
+    return centered * inverse, inverse
+
+
+def norm_back(grad, normed, inverse):
+    return inverse * (
+        grad
+        - jnp.mean(grad, axis=-1, keepdims=True)
+        - normed * jnp.mean(grad * normed, axis=-1, keepdims=True)
+    )
+
+
+def to_both_cores(blocks_of, core, me):
+    mine = exchange_near([blocks_of(me ^ step, core) for step in range(4)], me)
+    other = other_core(mine)
+    low = jnp.where(core == 0, mine, other)
+    high = jnp.where(core == 0, other, mine)
+    return jnp.concatenate([low, high], axis=1)
+
+
+def heads_of(values):
+    return values.reshape(values.shape[0], -1, HEAD_CHANNELS)
+
+
+def plane_body(
+    latents,
+    ratio_embed,
+    clip_tokens,
+    cotangent,
+    conv_kernel,
+    conv_bias,
+    expand_weight,
+    expand_bias,
+    response_gain,
+    response_bias,
+    reduce_weight,
+    reduce_bias,
+    ratio_weight,
+    ratio_bias,
+    text_weight,
+    text_bias,
+    attend_weight,
+    query_bias,
+    value_bias,
+    output_weight,
+    output_bias,
+):
+    size = lax.axis_size("dp")
+    core = lax.axis_index("cond")
+    me = lax.axis_index("dp")
+    _, rows, cols, chan = latents.shape
+    pixels = rows * cols
+    part = chan // size
+    hid = size * expand_bias.shape[0]
+    texts = clip_tokens.shape[1]
+    grid = [(z, d) for z in range(size) for d in range(size)]
+    swap_perm = [(z * size + d, d * size + z) for z, d in grid]
+    down_perm = [(z * size + d, d * size + z + 1) for z, d in grid if z + 1 < size]
+    up_perm = [(z * size + d, d * size + z - 1) for z, d in grid if z >= 1]
+
+    def swap(value, perm=swap_perm):
+        return lax.ppermute(value, ("pair", "dp"), perm)
+
+    image = swap(latents[0])
+    above = swap(latents[0, -1:], down_perm)
+    below = swap(latents[0, :1], up_perm)
+    embed = swap(ratio_embed)
+    tokens = swap(clip_tokens[0])
+    cot = swap(cotangent[0].reshape(pixels, chan))
+
+    packed = jnp.concatenate(
+        [
+            conv_kernel.reshape(9, part),
+            conv_bias[None],
+            reduce_bias[None],
+            text_bias[None],
+            output_bias[None],
+            ratio_bias.reshape(2, part),
+        ],
+        axis=0,
+    )
+    every = lax.all_gather(packed, "dp", axis=0)
+    channel_rows = every[:, :13].transpose(1, 0, 2).reshape(13, chan)
+    kernel = channel_rows[:9].reshape(3, 3, chan)
+    conv_shift, reduce_b, text_b, out_b = (channel_rows[9 + i] for i in range(4))
+    ratio_b = every[:, 13:].reshape(2 * chan)
+
+    half = part // 2
+    wide = hid // size
+    expand_w = to_both_cores(
+        lambda to, c: lax.dynamic_slice(expand_weight, (c * half, to * wide), (half, wide)), core, me
+    ).reshape(chan, wide)
+    attend_thirds = attend_weight.reshape(part, 3, chan)
+    attend_w = to_both_cores(
+        lambda to, c: lax.dynamic_slice(
+            attend_thirds, (c * half, 0, to * part), (half, 3, part)
+        ).reshape(half, 3 * part),
+        core,
+        me,
+    ).reshape(chan, 3 * part)
+
+    text_part = text_weight.shape[0]
+    silu_tokens = jax.nn.silu(tokens)
+    token_cols = [
+        lax.dynamic_slice(tokens, (0, (me ^ step) * text_part), (texts, text_part))
+        for step in range(4)
+    ]
+    near_tokens = jnp.concatenate(
+        [token_cols[0]] + [partners(token_cols[step], step) for step in (1, 2, 3)], axis=0
+    )
+    silu_near = jax.nn.silu(near_tokens)
+    mapped_share = dot(silu_near, text_weight)
+    mapped = scatter_near(jnp.split(mapped_share, 4, axis=0)) + text_b
+    mapped_all = jnp.concatenate(gather_near(mapped), axis=0)
+    ratio_part = ratio_weight.shape[0]
+    embed_part = lax.dynamic_slice(embed, (0, me * ratio_part), (1, ratio_part))
+    modulation = (
+        lax.psum(jnp.dot(embed_part, ratio_weight, precision=HIGHEST_ACCURACY), "dp")[0] + ratio_b
+    )
+    mod_scale = 1.0 + modulation[:chan]
+    mod_shift = modulation[chan:]
+
+    row_padded = jnp.concatenate([above, image, below], axis=0)
+    padded = jnp.pad(row_padded, ((0, 0), (1, 1), (0, 0)))
+    total_conv = conv_shift
+    for i in range(3):
+        for j in range(3):
+            total_conv = total_conv + padded[i : i + rows, j : j + cols] * kernel[i, j]
+    normed, inverse = norm_stats(total_conv.reshape(pixels, chan))
+    normed_all = jnp.concatenate(gather_near(normed), axis=0)
+    hidden = dot(normed_all, expand_w) + expand_bias
+    bell = 0.5 * (1.0 + lax.erf(hidden * 0.5**0.5))
+    activated = hidden * bell
+    totals = jnp.sum(activated * activated, axis=0)
+    norms = jnp.sqrt(totals + EPSILON)
+    middle = lax.psum(jnp.sum(norms), "dp") / hid + EPSILON
+    scaled = norms / middle
+    factor = 1.0 + response_gain * scaled
+    response = activated * factor + response_bias
+    one_share = dot(response, reduce_weight)
+    hidden_one = (
+        scatter_near(jnp.split(one_share, 4, axis=0)) + image.reshape(pixels, chan) + reduce_b
+    )
+    hidden_two = hidden_one * mod_scale + mod_shift
+    normed_two, inverse_two = norm_stats(hidden_two)
+    normed_two_all = jnp.concatenate(gather_near(normed_two), axis=0)
+
+    source = jnp.concatenate([normed_two_all, mapped_all], axis=0)
+    query = dot(normed_two_all, attend_w[:, :part]) + query_bias
+    key_value = dot(source, attend_w[:, part:])
+    key = key_value[:, :part]
+    value = key_value[:, part:] + value_bias
+    query_h, key_h, value_h = heads_of(query), heads_of(key), heads_of(value)
+    scores = jnp.einsum("iuy,ouy->uio", query_h, key_h, precision=FAST) * HEAD_CHANNELS ** (-0.5)
+    expo = jnp.exp(scores - jnp.max(scores, axis=-1, keepdims=True))
+    probs = expo / jnp.sum(expo, axis=-1, keepdims=True)
+    mixture_h = jnp.einsum("uio,ouy->iuy", probs, value_h, precision=FAST)
+    mixture = mixture_h.reshape(query.shape)
+    out_share = dot(mixture, output_weight)
+    plane_out = scatter_near(jnp.split(out_share, 4, axis=0)) + hidden_two + out_b
+    layer_output = swap(plane_out).reshape(latents.shape)
+
+    cot_all = jnp.concatenate(gather_near(cot), axis=0)
+    output_grad = t_dot(mixture, cot_all)
+    grad_mix_h = heads_of(dot_t(cot_all, output_weight))
+    grad_probs = jnp.einsum("iuy,ouy->uio", grad_mix_h, value_h, precision=FAST)
+    delta = jnp.sum(grad_mix_h * mixture_h, axis=-1).T
+    grad_scores = probs * (grad_probs - delta[..., None]) * HEAD_CHANNELS ** (-0.5)
+    grad_query = jnp.einsum("uio,ouy->iuy", grad_scores, key_h, precision=FAST).reshape(query.shape)
+    grad_key = jnp.einsum("uio,iuy->ouy", grad_scores, query_h, precision=FAST).reshape(key.shape)
+    grad_value = jnp.einsum("uio,iuy->ouy", probs, grad_mix_h, precision=FAST).reshape(key.shape)
+    spots = size * pixels
+    grad_kv = jnp.concatenate([grad_key, grad_value], axis=1)
+    grad_qkv = jnp.concatenate([grad_query, grad_kv[:spots]], axis=1)
+    two_share = dot_t(grad_qkv, attend_w)
+    text_share = dot_t(grad_kv[spots:], attend_w[:, part:])
+    grad_normed_two = scatter_near(jnp.split(two_share, 4, axis=0))
+    grad_mapped = scatter_near(jnp.split(text_share, 4, axis=0))
+    attend_grad = t_dot(normed_two_all, grad_qkv)
+    attend_grad = attend_grad.at[:, part:].add(t_dot(mapped_all, grad_kv[spots:]))
+    grad_two = cot + norm_back(grad_normed_two, normed_two, inverse_two)
+    grad_one = grad_two * mod_scale
+    grad_one_all = jnp.concatenate(gather_near(grad_one), axis=0)
+    grad_mapped_all = jnp.concatenate(gather_near(grad_mapped), axis=0)
+    mapper_grad = t_dot(silu_near, grad_mapped_all)
+    gate = 1.0 / (1.0 + jnp.exp(-near_tokens))
+    tokens_near = dot_t(grad_mapped_all, text_weight) * (
+        gate * (1.0 + near_tokens * (1.0 - gate))
+    )
+    token_blocks = exchange_near(jnp.split(tokens_near, 4, axis=0), me)
+    tokens_grad = swap(token_blocks.transpose(1, 0, 2).reshape(texts, size * text_part))[None]
+    ratio_sums = lax.psum(
+        jnp.concatenate([jnp.sum(grad_two * hidden_one, axis=0), jnp.sum(grad_two, axis=0)]), "dp"
+    )
+    ratio_grad = embed_part.reshape(ratio_part, 1) * ratio_sums
+
+    reduce_grad = t_dot(response, grad_one_all)
+    grad_response = dot_t(grad_one_all, reduce_weight)
+    gain_sum = jnp.sum(grad_response * activated, axis=0)
+    grad_scaled = gain_sum * response_gain
+    spread = lax.psum(jnp.sum(grad_scaled * norms), "dp") / hid
+    grad_norms = grad_scaled / middle - spread / (middle * middle)
+    grad_totals = grad_norms / (2.0 * norms)
+    grad_activated = grad_response * factor + 2.0 * activated * grad_totals
+    density = jnp.exp(-0.5 * hidden * hidden) * (2.0 * jnp.pi) ** -0.5
+    grad_hidden = grad_activated * (bell + hidden * density)
+    expand_grad = t_dot(normed_all, grad_hidden)
+    front_share = dot_t(grad_hidden, expand_w)
+    grad_normed = scatter_near(jnp.split(front_share, 4, axis=0))
+    grad_conv = norm_back(grad_normed, normed, inverse).reshape(rows, cols, chan)
+    kernel_grad = jnp.stack(
+        [
+            jnp.sum(padded[i : i + rows, j : j + cols] * grad_conv, axis=(0, 1))
+            for i in range(3)
+            for j in range(3)
+        ]
+    )
+    spread_conv = jnp.pad(grad_conv, ((2, 2), (1, 1), (0, 0)))
+    latent_rows = jnp.zeros((rows + 2, cols, chan), jnp.float32)
+    for i in range(3):
+        for j in range(3):
+            latent_rows = (
+                latent_rows
+                + spread_conv[2 - i : 2 - i + rows + 2, 2 - j : 2 - j + cols] * kernel[i, j]
+            )
+    inner = swap(latent_rows[1:-1] + grad_one.reshape(rows, cols, chan))
+    back_up = [(d * size + z, (z - 1) * size + d) for z, d in grid if z >= 1]
+    back_down = [(d * size + z, (z + 1) * size + d) for z, d in grid if z + 1 < size]
+    from_below = swap(latent_rows[:1], back_up)
+    from_above = swap(latent_rows[-1:], back_down)
+    latent_grad = inner.at[-1:].add(from_below).at[:1].add(from_above)[None]
+
+    def over_planes(value, axis):
+        count = value.shape[axis] // 2
+        low = lax.slice_in_dim(value, 0, count, axis=axis)
+        high = lax.slice_in_dim(value, count, None, axis=axis)
+        kept = jnp.where(core == 0, low, high) + other_core(jnp.where(core == 0, high, low))
+        return kept
+
+    def from_both(value, axis):
+        other = other_core(value)
+        return jnp.concatenate(
+            [jnp.where(core == 0, value, other), jnp.where(core == 0, other, value)], axis=axis
+        )
+
+    def columns_home(value):
+        kept = over_planes(value.reshape(size, part, value.shape[1]), 1)
+        blocks = [
+            lax.dynamic_slice(kept, (me ^ step, 0, 0), (1,) + kept.shape[1:])[0]
+            for step in range(4)
+        ]
+        return exchange_near(blocks, me)
+
+    output_sum = from_both(lax.psum(over_planes(output_grad, 0), "pair"), 0)
+    attend_home = columns_home(attend_grad)
+    attend_home = attend_home.reshape(size, half, 3, part).transpose(1, 2, 0, 3)
+    attend_sum = from_both(lax.psum(attend_home.reshape(half, 3 * chan), "pair"), 0)
+    mapper_sum = from_both(lax.psum(over_planes(mapper_grad, 0), "pair"), 0)
+    reduce_sum = from_both(lax.psum(over_planes(reduce_grad, 0), "pair"), 0)
+    expand_home = columns_home(expand_grad).transpose(1, 0, 2).reshape(half, hid)
+    expand_sum = from_both(lax.psum(expand_home, "pair"), 0)
+
+    def mine(value):
+        return lax.dynamic_slice(value, (me * (value.shape[0] // size),), (value.shape[0] // size,))
+
+    small = (
+        jnp.sum(grad_hidden, axis=0),
+        scaled * gain_sum,
+        jnp.sum(grad_response, axis=0),
+        mine(jnp.sum(grad_one_all, axis=0)),
+        mine(jnp.sum(grad_mapped_all, axis=0)),
+        jnp.sum(grad_query, axis=0),
+        jnp.sum(grad_value, axis=0),
+        mine(jnp.sum(cot_all, axis=0)),
+        mine(ratio_sums),
+        ratio_grad.reshape(-1),
+    )
+    lengths = [item.shape[0] for item in small]
+    small_sum = lax.psum(jnp.concatenate(small), ("cond", "pair"))
+    ends = []
+    position = 0
+    for length in lengths:
+        ends.append(small_sum[position : position + length])
+        position += length
+    expb, gain, respb, redb, mapb, queryb, valueb, outb, ratiob, ratio = ends
+    conv_sum = lax.psum(
+        jnp.concatenate([kernel_grad, jnp.sum(grad_conv, axis=(0, 1))[None]], axis=0),
+        ("cond", "pair", "dp"),
+    )
+    conv_mine = lax.dynamic_slice(conv_sum, (0, me * part), (10, part))
+    return (
+        layer_output,
+        latent_grad,
+        tokens_grad,
+        conv_mine[:9].reshape(3, 3, part),
+        conv_mine[9],
+        expand_sum,
+        expb,
+        gain,
+        respb,
+        reduce_sum,
+        redb,
+        ratio.reshape(ratio_part, 2 * chan),
+        ratiob,
+        mapper_sum,
+        mapb,
+        attend_sum,
+        queryb,
+        valueb,
+        output_sum,
+        outb,
+    )
+
 
 def solution(mesh):
+    square = mesh.shape["cond"] == 2 and mesh.shape["pair"] == 4 and mesh.shape["dp"] == 4
     return jax.shard_map(
-        body,
+        plane_body if square else body,
         mesh=mesh,
         in_specs=(
             P(("cond", "dp"), "pair", None, None),

time: 3520 us -> 1710 us (0.49)
  waiting for transfers between devices: 2720 us -> 858 us
  matrix products: 454 us -> 191 us
  starting transfers between devices: 13.8 us -> 176 us
  other arithmetic: 42.8 us -> 176 us
  local copies, waits for them, and re-layouts: 93.7 us -> 150 us
    all_gather x7 -> x0, waiting for transfers between devices: 1010 us -> none  [the longest x1 325 us: body(): lax.all_gather(expand_weight, 'dp', axis=0, tiled=True)]
    reduce_scatter x6 -> x0, waiting for transfers between devices: 845 us -> none  [the longest x1 326 us: body(): lax.psum_scatter(expand_w_grad, 'dp', scatter_dimension=0, tiled=True)]
    ppermute x4 -> x77, waiting for transfers between devices: 0.01 us -> 373 us  [the longest x54 264 us: partners(): return lax.ppermute(value, 'dp', [(i, i ^ step) for i in range(4)])]
    unnamed x20 -> x2, waiting for transfers between devices: 301 us -> 0.03 us
    dot_general x25, matrix products: 454 us -> 191 us  [the longest x6 56.9 us: t_dot(): lax.dot_general(left, right, (((0,), (0,)), ((), ())), precision=FAST)]
    ppermute x4 -> x77, starting transfers between devices: 11.9 us -> 176 us  [the longest x54 133 us: partners(): return lax.ppermute(value, 'dp', [(i, i ^ step) for i in range(4)])]
    psum x1 -> x2, waiting for transfers between devices: 558 us -> 485 us  [the longest x1 485 us: plane_body(): expand_sum = from_both(lax.psum(expand_home, 'pair'), 0)]
    select_n x0 -> x18, other arithmetic: none -> 51.3 us  [the longest x5 18.1 us: from_both(): jnp.where(core == 0, value, other)]
  transfers between devices with their start and end apart: 21 -> 79, of which waited for: 12 -> 24; matrix products, arithmetic and copies ran while one was open for 12% -> 21% of each run, Pallas kernels for 0% -> 0%
where the time goes in v1:
time: 1710 us; the launch traced here: 1700 us
  waiting for transfers between devices  858 us (50%)
  matrix products  191 us (11%)
  starting transfers between devices  176 us (10%)
  other arithmetic  176 us (10%)
  local copies, waits for them, and re-layouts  150 us (9%)
  blocking collectives  129 us (8%)
  between operations  18.1 us (1%)
    psum x1, waiting for transfers between devices, plane_body(): expand_sum = from_both(lax.psum(expand_home, 'pair'), 0)  485 us
    ppermute x54, waiting for transfers between devices, partners(): return lax.ppermute(value, 'dp', [(i, i ^ step) for i in range(4)])  264 us
    ppermute x54, starting transfers between devices, partners(): return lax.ppermute(value, 'dp', [(i, i ^ step) for i in range(4)])  133 us
    ppermute x11, waiting for transfers between devices, swap(): return lax.ppermute(value, ('pair', 'dp'), perm)  108 us
    dot_general x6, matrix products, t_dot(): lax.dot_general(left, right, (((0,), (0,)), ((), ())), precision=FAST)  56.9 us
    all_gather x1, blocking collectives, plane_body(): every = lax.all_gather(packed, 'dp', axis=0)  51.6 us
    dot_general x6, matrix products, dot_t(): lax.dot_general(left, right, (((1,), (1,)), ((), ())), precision=FAST)  49.5 us
    dot_general x6, matrix products, dot(): return jnp.dot(left, right, precision=FAST)  49.2 us
  transfers between devices with their start and end apart: 79, of which 24 were waited for; matrix products, arithmetic and copies ran while one was open for 21% of the time, Pallas kernels for 0%

profile of v1, /device:TPU:16, one launch (start us, length us, event | category | flops | bytes accessed | tf_op | source)
XLA Modules:
  0.0 1698.6 jit_solution(7511074414709197950)
XLA Ops:
  19.7 51.6 %all-gather.1 = f32[4,15,384]{2,1,0:T(8,128)S(1)} all-gather(f32[1,15,384]{2,1,0:T(8,128)S(1)} %bitcast.187), channel_id=2, replica_groups=mesh['cond'=2,'pair'=4,'dp'=4] {'dp'}, dimensions={0}, use_global_device_ids=true | all-gather | bytes 115200 | tf_op jit(solution)/shard_map/all_gather | solution.py:407
  153.0 21.6 %collective-permute-start.23 = (f32[19,1536]{1,0:T(8,128)S(1)}, f32[19,1536]{1,0:T(8,128)S(1)}, u32[]{:S(2)}, u32[]{:S(2)}) collective-permute-start(f32[19,1536]{1,0:T(8,128)S(1)} %get-tuple-element.235), channel_id=1, source_target_pairs={{0,3},{1,2},{2,1},{3,0},{4,7},{5,6},{6,5},{7,4},{8,11},{9,10},{10,... | collective-permute-start | bytes 350216 | tf_op jit(solution)/shard_map/ppermute | solution.py:301
  203.8 39.6 %collective-permute-done.28 = f32[192,1152]{1,0:T(8,128)} collective-permute-done((f32[192,1152]{1,0:T(8,128)}, f32[192,1152]{1,0:T(8,128)}, u32[]{:S(2)}, u32[]{:S(2)}) %collective-permute-start.28) | collective-permute-done | bytes 884768 | tf_op jit(solution)/shard_map/ppermute | solution.py:301
  256.4 19.4 %collective-permute-start.37 = (f32[144,1536]{1,0:T(8,128)}, f32[144,1536]{1,0:T(8,128)S(1)}, u32[]{:S(2)}, u32[]{:S(2)}) collective-permute-start(f32[144,1536]{1,0:T(8,128)} %collective-permute-done.35), channel_id=1, source_target_pairs={{0,2},{1,3},{2,0},{3,1},{4,6},{5,7},{6,4},{7,5},{8,10},{9,11},{10,... | collective-permute-start | bytes 2654216 | tf_op jit(solution)/shard_map/ppermute | solution.py:301
  283.2 21.1 %collective-permute-start.4 = (f32[144,1536]{1,0:T(8,128)}, f32[144,1536]{1,0:T(8,128)S(1)}, u32[]{:S(2)}, u32[]{:S(2)}) collective-permute-start(f32[144,1536]{1,0:T(8,128)} %fusion.59), channel_id=1, source_target_pairs={{0,2},{1,3},{2,0},{3,1},{4,6},{5,7},{6,4},{7,5},{8,10},{9,11},{10,... | collective-permute-start | bytes 2654216 | tf_op jit(solution)/shard_map/ppermute | solution.py:301
  327.6 33.2 %collective-permute-done.4 = f32[144,1536]{1,0:T(8,128)S(1)} collective-permute-done((f32[144,1536]{1,0:T(8,128)}, f32[144,1536]{1,0:T(8,128)S(1)}, u32[]{:S(2)}, u32[]{:S(2)}) %collective-permute-start.4) | collective-permute-done | bytes 884768 | tf_op jit(solution)/shard_map/ppermute | solution.py:301
  360.8 14.8 multiply_reduce_fusion.2
  376.3 18.9 %all-reduce.3 = (f32[]{:T(128)}, f32[3072]{0:T(1024)}) all-reduce(f32[]{:T(128)} %fusion.82, f32[3072]{0:T(1024)} %bitcast.188), channel_id=1, replica_groups=mesh['cond'=2,'pair'=4,'dp'=4] {'dp'}, use_global_device_ids=true, to_apply=%region_4.6 | all-reduce | flops 3073 | bytes 24584 | tf_op jit(solution)/shard_map/psum | solution.py:461
  395.8 12.6 fusion.13
  416.9 14.4 collective-permute-done.10
  431.8 14.5 collective-permute-done.11
  460.2 24.3 %collective-permute-done.26 = f32[19,1536]{1,0:T(8,128)} collective-permute-done((f32[19,1536]{1,0:T(8,128)S(1)}, f32[19,1536]{1,0:T(8,128)}, u32[]{:S(2)}, u32[]{:S(2)}) %collective-permute-start.26) | collective-permute-done | bytes 116768 | tf_op jit(solution)/shard_map/ppermute | solution.py:301
  487.6 18.7 %concatenate.86 = f32[652,1536]{1,0:T(8,128)} concatenate(f32[144,1536]{1,0:T(8,128)} %subtract_multiply_fusion.1, f32[144,1536]{1,0:T(8,128)} %collective-permute-done.14, f32[144,1536]{1,0:T(8,128)} %collective-permute-done.15, f32[144,1536]{1,0:T(8,128)} %collective-permute-done.16, f32[19,1536]{1,0:T(8,128)S(1)} %fusion.79, f32[19,1536]{1,0:T(8,128)S(1)} %collective-permute-done.24, ...), dimensions={0} | concatenate | bytes 8011776 | tf_op jit(solution)/shard_map/concatenate | solution.py:473
  506.3 8.8 fusion.5
  570.1 14.5 fusion.15
  584.7 19.4 %fusion.14 = f32[1536,1152]{1,0:T(8,128)S(1)} fusion(f32[576,768]{0,1:T(8,128)S(1)} %fusion.20, f32[576,384]{0,1:T(8,128)S(1)} %bitcast.179, f32[144,1536]{1,0:T(8,128)} %collective-permute-done.16, f32[144,1536]{1,0:T(8,128)} %collective-permute-done.15, f32[144,1536]{1,0:T(8,128)} %collective-permute-done.14, f32[144,1536]{1,0:T(8,128)} %subtract_multiply_fusion.1), kind=kOutput, calls=%fused_computation.58 | convolution fusion | flops 6118612992 | bytes 13271040 | tf_op jit(solution)/shard_map/dot_general | solution.py:297
  632.9 26.6 %collective-permute-done.54 = f32[19,1536]{1,0:T(8,128)S(1)} collective-permute-done((f32[19,1536]{1,0:T(8,128)}, f32[19,1536]{1,0:T(8,128)S(1)}, u32[]{:S(2)}, u32[]{:S(2)}) %collective-permute-start.54) | collective-permute-done | bytes 116768 | tf_op jit(solution)/shard_map/ppermute | solution.py:301
  691.0 17.0 %collective-permute-done.32 = f32[144,1536]{1,0:T(8,128)} collective-permute-done((f32[144,1536]{1,0:T(8,128)}, f32[144,1536]{1,0:T(8,128)}, u32[]{:S(2)}, u32[]{:S(2)}) %collective-permute-start.32) | collective-permute-done | bytes 884768 | tf_op jit(solution)/shard_map/ppermute | solution.py:301
  711.7 10.2 collective-permute-done.42
  722.0 9.8 collective-permute-done.43
  731.8 13.9 fusion.105
  747.6 15.9 all-reduce.2
  769.7 15.0 fusion.19
  793.9 12.3 fusion.12
  828.0 15.8 collective-permute-done.71
  843.8 18.5 %collective-permute-done.73 = f32[192,1152]{1,0:T(8,128)} collective-permute-done((f32[192,1152]{1,0:T(8,128)}, f32[192,1152]{1,0:T(8,128)}, u32[]{:S(2)}, u32[]{:S(2)}) %collective-permute-start.73) | collective-permute-done | bytes 884768 | tf_op jit(solution)/shard_map/ppermute | solution.py:301
  902.5 9.0 select_add_fusion
  911.4 21.0 %collective-permute-done.63 = f32[192,1536]{1,0:T(8,128)} collective-permute-done((f32[192,1536]{1,0:T(8,128)}, f32[192,1536]{1,0:T(8,128)}, u32[]{:S(2)}, u32[]{:S(2)}) %collective-permute-start.63) | collective-permute-done | bytes 1179680 | tf_op jit(solution)/shard_map/ppermute | solution.py:301
  960.7 12.7 fusion.134
  987.0 96.8 %collective-permute-done.60 = f32[19,1280]{1,0:T(8,128)S(1)} collective-permute-done((f32[19,1280]{1,0:T(8,128)S(1)}, f32[19,1280]{1,0:T(8,128)S(1)}, u32[]{:S(2)}, u32[]{:S(2)}) %collective-permute-start.60) | collective-permute-done | bytes 97312 | tf_op jit(solution)/shard_map/ppermute | solution.py:387
  1102.5 485.5 %all-reduce.10.cloned.1.call-done = (f32[192,6144]{1,0:T(8,128)}, f32[768,1536]{1,0:T(8,128)}, f32[160,1536]{1,0:T(8,128)}, f32[192,4608]{1,0:T(8,128)}, f32[192,1536]{1,0:T(8,128)}) async-done(((f32[192,6144]{1,0:T(8,128)}, f32[768,1536]{1,0:T(8,128)}, f32[160,1536]{1,0:T(8,128)}, f32[192,4608]{1,0:T(8,128)}, f32[192,1536]{1,0:T(8,128)}), (f32[192,6144]{1,0:T(8,128)}, f32[768,1536]{1,0:T(8,128)}, ...) | async-done | bytes 15138832 | tf_op jit(solution)/shard_map/psum | solution.py:586
  1592.4 43.0 %psum.80 = f32[10,1536]{1,0:T(8,128)S(1)} all-reduce(f32[10,1536]{1,0:T(8,128)S(1)} %concatenate.94), channel_id=1, replica_groups=mesh['cond'=2,'pair'=4,'dp'=4] {'cond','pair','dp'}, use_global_device_ids=true, to_apply=%region_28.31 | all-reduce | flops 15360 | bytes 122880 | tf_op jit(solution)/shard_map/psum | solution.py:611
  (598 shorter events, 510.0 us)
Async XLA Ops:
  7.2 1077.3 %all-reduce.8.cloned.1.call-start = ((), (), s32[]{:S(2)}) async-start(), calls=%async_computation | async-start | bytes 458752 | tf_op jit(solution)/shard_map/psum | solution.py:604
  12.1 115.3 %collective-permute-start.6 = (f32[192,1536]{1,0:T(8,128)}, f32[192,1536]{1,0:T(8,128)}, u32[]{:S(2)}, u32[]{:S(2)}) collective-permute-start(f32[192,1536]{1,0:T(8,128)} %get-tuple-element.182), channel_id=1, source_target_pairs={{0,1},{1,0},{2,3},{3,2},{4,5},{5,4},{6,7},{7,6},{8,9},{9,8},{10,11... | collective-permute-start | bytes 3538952 | tf_op jit(solution)/shard_map/ppermute | solution.py:301
  13.6 113.9 %collective-permute-start.7 = (f32[192,1536]{1,0:T(8,128)}, f32[192,1536]{1,0:T(8,128)}, u32[]{:S(2)}, u32[]{:S(2)}) collective-permute-start(f32[192,1536]{1,0:T(8,128)} %get-tuple-element.184), channel_id=1, source_target_pairs={{0,2},{1,3},{2,0},{3,1},{4,6},{5,7},{6,4},{7,5},{8,10},{9,11},{10,... | collective-permute-start | bytes 3538952 | tf_op jit(solution)/shard_map/ppermute | solution.py:301
  15.1 112.3 %collective-permute-start.8 = (f32[192,1536]{1,0:T(8,128)}, f32[192,1536]{1,0:T(8,128)}, u32[]{:S(2)}, u32[]{:S(2)}) collective-permute-start(f32[192,1536]{1,0:T(8,128)} %get-tuple-element.183), channel_id=1, source_target_pairs={{0,3},{1,2},{2,1},{3,0},{4,7},{5,6},{6,5},{7,4},{8,11},{9,10},{10,... | collective-permute-start | bytes 3538952 | tf_op jit(solution)/shard_map/ppermute | solution.py:301
  16.3 73.0 %collective-permute-start.17 = (f32[19,1280]{1,0:T(8,128)}, f32[19,1280]{1,0:T(8,128)}, u32[]{:S(2)}, u32[]{:S(2)}) collective-permute-start(f32[19,1280]{1,0:T(8,128)} %bitcast.137), channel_id=1, source_target_pairs={{0,0},{1,4},{2,8},{3,12},{4,1},{5,5},{6,9},{7,13},{8,2},{9,6},{10,... | collective-permute-start | bytes 291848 | tf_op jit(solution)/shard_map/ppermute | solution.py:387
  116.5 77.6 %collective-permute-start.1 = (f32[6,24,1536]{2,1,0:T(8,128)}, f32[6,24,1536]{2,1,0:T(8,128)S(1)}, u32[]{:S(2)}, u32[]{:S(2)}) collective-permute-start(f32[6,24,1536]{2,1,0:T(8,128)} %bitcast.186), channel_id=1, source_target_pairs={{0,0},{1,4},{2,8},{3,12},{4,1},{5,5},{6,9},{7,13},{8,2},{9,6},{10,... | collective-permute-start | bytes 2654216 | tf_op jit(solution)/shard_map/ppermute | solution.py:387
  143.1 167.4 %collective-permute-start.9 = (f32[4,192,1536]{2,1,0:T(8,128)}, f32[4,192,1536]{2,1,0:T(8,128)}, u32[]{:S(2)}, u32[]{:S(2)}) collective-permute-start(f32[4,192,1536]{2,1,0:T(8,128)} %broadcast_select_fusion), channel_id=1, source_target_pairs={{0,16},{16,0},{1,17},{17,1},{2,18},{18,2},{3,19},{19,3},{4,20},{20... | collective-permute-start | bytes 14155784 | tf_op jit(solution)/shard_map/ppermute | solution.py:320
  180.9 62.5 %collective-permute-start.28 = (f32[192,1152]{1,0:T(8,128)}, f32[192,1152]{1,0:T(8,128)}, u32[]{:S(2)}, u32[]{:S(2)}) collective-permute-start(f32[192,1152]{1,0:T(8,128)} %copy.93), channel_id=1, source_target_pairs={{0,2},{1,3},{2,0},{3,1},{4,6},{5,7},{6,4},{7,5},{8,10},{9,11},{10,... | collective-permute-start | bytes 2654216 | tf_op jit(solution)/shard_map/ppermute | solution.py:301
  186.5 58.9 %collective-permute-start.29 = (f32[192,1152]{1,0:T(8,128)}, f32[192,1152]{1,0:T(8,128)}, u32[]{:S(2)}, u32[]{:S(2)}) collective-permute-start(f32[192,1152]{1,0:T(8,128)} %copy.94), channel_id=1, source_target_pairs={{0,3},{1,2},{2,1},{3,0},{4,7},{5,6},{6,5},{7,4},{8,11},{9,10},{10,... | collective-permute-start | bytes 2654216 | tf_op jit(solution)/shard_map/ppermute | solution.py:301
  203.6 251.7 %collective-permute-start.24 = (f32[19,1536]{1,0:T(8,128)S(1)}, f32[19,1536]{1,0:T(8,128)S(1)}, u32[]{:S(2)}, u32[]{:S(2)}) collective-permute-start(f32[19,1536]{1,0:T(8,128)S(1)} %fusion.79), channel_id=1, source_target_pairs={{0,1},{1,0},{2,3},{3,2},{4,5},{5,4},{6,7},{7,6},{8,9},{9,8},{10,11... | collective-permute-start | bytes 350216 | tf_op jit(solution)/shard_map/ppermute | solution.py:301
  243.4 83.2 %collective-permute-start.3 = (f32[144,1536]{1,0:T(8,128)}, f32[144,1536]{1,0:T(8,128)}, u32[]{:S(2)}, u32[]{:S(2)}) collective-permute-start(f32[144,1536]{1,0:T(8,128)} %fusion.59), channel_id=1, source_target_pairs={{0,1},{1,0},{2,3},{3,2},{4,5},{5,4},{6,7},{7,6},{8,9},{9,8},{10,11... | collective-permute-start | bytes 2654216 | tf_op jit(solution)/shard_map/ppermute | solution.py:301
  283.2 77.6 %collective-permute-start.4 = (f32[144,1536]{1,0:T(8,128)}, f32[144,1536]{1,0:T(8,128)S(1)}, u32[]{:S(2)}, u32[]{:S(2)}) collective-permute-start(f32[144,1536]{1,0:T(8,128)} %fusion.59), channel_id=1, source_target_pairs={{0,2},{1,3},{2,0},{3,1},{4,6},{5,7},{6,4},{7,5},{8,10},{9,11},{10,... | collective-permute-start | bytes 2654216 | tf_op jit(solution)/shard_map/ppermute | solution.py:301
  307.1 53.7 %collective-permute-start.5 = (f32[144,1536]{1,0:T(8,128)}, f32[144,1536]{1,0:T(8,128)S(1)}, u32[]{:S(2)}, u32[]{:S(2)}) collective-permute-start(f32[144,1536]{1,0:T(8,128)} %fusion.59), channel_id=1, source_target_pairs={{0,3},{1,2},{2,1},{3,0},{4,7},{5,6},{6,5},{7,4},{8,11},{9,10},{10,... | collective-permute-start | bytes 2654216 | tf_op jit(solution)/shard_map/ppermute | solution.py:301
  310.6 140.7 %collective-permute-start.30 = (f32[4,192,1152]{2,1,0:T(8,128)}, f32[4,192,1152]{2,1,0:T(8,128)}, u32[]{:S(2)}, u32[]{:S(2)}) collective-permute-start(f32[4,192,1152]{2,1,0:T(8,128)} %broadcast_select_fusion.8), channel_id=1, source_target_pairs={{0,16},{16,0},{1,17},{17,1},{2,18},{18,2},{3,19},{19,3},{4,20},{20... | collective-permute-start | bytes 10616840 | tf_op jit(solution)/shard_map/ppermute | solution.py:320
  326.6 82.8 %collective-permute-start.38 = (f32[144,1536]{1,0:T(8,128)}, f32[144,1536]{1,0:T(8,128)S(1)}, u32[]{:S(2)}, u32[]{:S(2)}) collective-permute-start(f32[144,1536]{1,0:T(8,128)} %collective-permute-done.35), channel_id=1, source_target_pairs={{0,3},{1,2},{2,1},{3,0},{4,7},{5,6},{6,5},{7,4},{8,11},{9,10},{10,... | collective-permute-start | bytes 2654216 | tf_op jit(solution)/shard_map/ppermute | solution.py:301
  617.9 54.1 %collective-permute-start.39 = (f32[144,1536]{1,0:T(8,128)}, f32[144,1536]{1,0:T(8,128)}, u32[]{:S(2)}, u32[]{:S(2)}) collective-permute-start(f32[144,1536]{1,0:T(8,128)} %get-tuple-element.204), channel_id=1, source_target_pairs={{0,1},{1,0},{2,3},{3,2},{4,5},{5,4},{6,7},{7,6},{8,9},{9,8},{10,11... | collective-permute-start | bytes 2654216 | tf_op jit(solution)/shard_map/ppermute | solution.py:301
  619.5 53.1 %collective-permute-start.40 = (f32[144,1536]{1,0:T(8,128)}, f32[144,1536]{1,0:T(8,128)}, u32[]{:S(2)}, u32[]{:S(2)}) collective-permute-start(f32[144,1536]{1,0:T(8,128)} %get-tuple-element.206), channel_id=1, source_target_pairs={{0,2},{1,3},{2,0},{3,1},{4,6},{5,7},{6,4},{7,5},{8,10},{9,11},{10,... | collective-permute-start | bytes 2654216 | tf_op jit(solution)/shard_map/ppermute | solution.py:301
  679.9 51.9 %collective-permute-start.43 = (f32[144,1536]{1,0:T(8,128)S(1)}, f32[144,1536]{1,0:T(8,128)S(1)}, u32[]{:S(2)}, u32[]{:S(2)}) collective-permute-start(f32[144,1536]{1,0:T(8,128)S(1)} %get-tuple-element.163), channel_id=1, source_target_pairs={{0,2},{1,3},{2,0},{3,1},{4,6},{5,7},{6,4},{7,5},{8,10},{9,11},{10,... | collective-permute-start | bytes 2654216 | tf_op jit(solution)/shard_map/ppermute | solution.py:301
  708.0 106.8 %collective-permute-start.70 = (f32[4,192,1152]{2,1,0:T(8,128)}, f32[4,192,1152]{2,1,0:T(8,128)}, u32[]{:S(2)}, u32[]{:S(2)}) collective-permute-start(f32[4,192,1152]{2,1,0:T(8,128)} %slice_select_fusion.2), channel_id=1, source_target_pairs={{0,16},{16,0},{1,17},{17,1},{2,18},{18,2},{3,19},{19,3},{4,20},{20... | collective-permute-start | bytes 10616840 | tf_op jit(solution)/shard_map/ppermute | solution.py:320
  722.0 69.3 %collective-permute-start.68 = (f32[160,1536]{1,0:T(8,128)}, f32[160,1536]{1,0:T(8,128)}, u32[]{:S(2)}, u32[]{:S(2)}) collective-permute-start(f32[160,1536]{1,0:T(8,128)} %slice_select_fusion.4), channel_id=1, source_target_pairs={{0,16},{16,0},{1,17},{17,1},{2,18},{18,2},{3,19},{19,3},{4,20},{20... | collective-permute-start | bytes 2949128 | tf_op jit(solution)/shard_map/ppermute | solution.py:320
  791.3 78.8 %collective-permute-start.61 = (f32[4,192,1536]{2,1,0:T(8,128)}, f32[4,192,1536]{2,1,0:T(8,128)}, u32[]{:S(2)}, u32[]{:S(2)}) collective-permute-start(f32[4,192,1536]{2,1,0:T(8,128)} %slice_select_fusion.1), channel_id=1, source_target_pairs={{0,16},{16,0},{1,17},{17,1},{2,18},{18,2},{3,19},{19,3},{4,20},{20... | collective-permute-start | bytes 14155784 | tf_op jit(solution)/shard_map/ppermute | solution.py:320
  811.5 91.0 %collective-permute-start.66 = (f32[768,1536]{1,0:T(8,128)}, f32[768,1536]{1,0:T(8,128)}, u32[]{:S(2)}, u32[]{:S(2)}) collective-permute-start(f32[768,1536]{1,0:T(8,128)} %slice_select_fusion), channel_id=1, source_target_pairs={{0,16},{16,0},{1,17},{17,1},{2,18},{18,2},{3,19},{19,3},{4,20},{20... | collective-permute-start | bytes 14155784 | tf_op jit(solution)/shard_map/ppermute | solution.py:320
  827.9 760.0 %all-reduce.10.cloned.1.call-start = ((), (), s32[]{:S(2)}) async-start(), calls=%async_computation.1 | async-start | bytes 30277632 | tf_op jit(solution)/shard_map/psum | solution.py:586
  880.1 52.3 %collective-permute-start.63 = (f32[192,1536]{1,0:T(8,128)}, f32[192,1536]{1,0:T(8,128)}, u32[]{:S(2)}, u32[]{:S(2)}) collective-permute-start(f32[192,1536]{1,0:T(8,128)} %get-tuple-element.195), channel_id=1, source_target_pairs={{0,2},{1,3},{2,0},{3,1},{4,6},{5,7},{6,4},{7,5},{8,10},{9,11},{10,... | collective-permute-start | bytes 3538952 | tf_op jit(solution)/shard_map/ppermute | solution.py:301
  955.1 129.5 %collective-permute-start.34 = (f32[144,1536]{1,0:T(8,128)}, f32[144,1536]{1,0:T(8,128)S(1)}, u32[]{:S(2)}, u32[]{:S(2)}) collective-permute-start(f32[144,1536]{1,0:T(8,128)} %get-tuple-element.228), channel_id=1, source_target_pairs={{0,0},{1,4},{2,8},{3,12},{4,1},{5,5},{6,9},{7,13},{8,2},{9,6},{10,... | collective-permute-start | bytes 2654216 | tf_op jit(solution)/shard_map/ppermute | solution.py:387
  976.7 113.9 %collective-permute-start.45 = (f32[144,1536]{1,0:T(8,128)}, f32[144,1536]{1,0:T(8,128)S(1)}, u32[]{:S(2)}, u32[]{:S(2)}) collective-permute-start(f32[144,1536]{1,0:T(8,128)} %get-tuple-element.201), channel_id=1, source_target_pairs={{0,1},{1,0},{2,3},{3,2},{4,5},{5,4},{6,7},{7,6},{8,9},{9,8},{10,11... | collective-permute-start | bytes 2654216 | tf_op jit(solution)/shard_map/ppermute | solution.py:301
  978.0 112.6 %collective-permute-start.46 = (f32[144,1536]{1,0:T(8,128)}, f32[144,1536]{1,0:T(8,128)}, u32[]{:S(2)}, u32[]{:S(2)}) collective-permute-start(f32[144,1536]{1,0:T(8,128)} %get-tuple-element.203), channel_id=1, source_target_pairs={{0,2},{1,3},{2,0},{3,1},{4,6},{5,7},{6,4},{7,5},{8,10},{9,11},{10,... | collective-permute-start | bytes 2654216 | tf_op jit(solution)/shard_map/ppermute | solution.py:301
  980.4 110.2 %collective-permute-start.47 = (f32[144,1536]{1,0:T(8,128)}, f32[144,1536]{1,0:T(8,128)}, u32[]{:S(2)}, u32[]{:S(2)}) collective-permute-start(f32[144,1536]{1,0:T(8,128)} %get-tuple-element.202), channel_id=1, source_target_pairs={{0,3},{1,2},{2,1},{3,0},{4,7},{5,6},{6,5},{7,4},{8,11},{9,10},{10,... | collective-permute-start | bytes 2654216 | tf_op jit(solution)/shard_map/ppermute | solution.py:301
  981.2 102.6 %collective-permute-start.60 = (f32[19,1280]{1,0:T(8,128)S(1)}, f32[19,1280]{1,0:T(8,128)S(1)}, u32[]{:S(2)}, u32[]{:S(2)}) collective-permute-start(f32[19,1280]{1,0:T(8,128)S(1)} %reshape.370), channel_id=1, source_target_pairs={{0,0},{1,4},{2,8},{3,12},{4,1},{5,5},{6,9},{7,13},{8,2},{9,6},{10,... | collective-permute-start | bytes 291848 | tf_op jit(solution)/shard_map/ppermute | solution.py:387
  1095.5 546.1 %collective-permute-start.48 = (f32[6,24,1536]{2,1,0:T(8,128)}, f32[6,24,1536]{2,1,0:T(8,128)}, u32[]{:S(2)}, u32[]{:S(2)}) collective-permute-start(f32[6,24,1536]{2,1,0:T(8,128)} %slice_add_fusion.2), channel_id=1, source_target_pairs={{0,0},{1,4},{2,8},{3,12},{4,1},{5,5},{6,9},{7,13},{8,2},{9,6},{10,... | collective-permute-start | bytes 2654216 | tf_op jit(solution)/shard_map/ppermute | solution.py:387
  1588.0 66.4 %collective-permute-start.74 = (f32[192,4608]{1,0:T(8,128)}, f32[192,4608]{1,0:T(8,128)}, u32[]{:S(2)}, u32[]{:S(2)}) collective-permute-start(f32[192,4608]{1,0:T(8,128)} %get-tuple-element.158), channel_id=1, source_target_pairs={{0,16},{16,0},{1,17},{17,1},{2,18},{18,2},{3,19},{19,3},{4,20},{20... | collective-permute-start | bytes 10616840 | tf_op jit(solution)/shard_map/ppermute | solution.py:320
  1589.0 52.3 %collective-permute-start.49 = (f32[1,24,1536]{2,1,0:T(8,128)S(1)}, f32[1,24,1536]{2,1,0:T(8,128)S(1)}, u32[]{:S(2)}, u32[]{:S(2)}) collective-permute-start(f32[1,24,1536]{2,1,0:T(8,128)S(1)} %get-tuple-element.220), channel_id=1, source_target_pairs={{1,0},{5,1},{9,2},{13,3},{2,4},{6,5},{10,6},{14,7},{3,8},{7,9},{11... | collective-permute-start | bytes 442376 | tf_op jit(solution)/shard_map/ppermute | solution.py:387
  (176 other events, 6215.3 us)
Sparse Core Ops, SparseCore 0:
  828.0 56.5 all-reduce.7
  948.1 639.7 all-reduce.9

commit v2 on v1

--- a/solution.py
+++ b/solution.py
@@ -3,6 +3,8 @@
 import jax
 import jax.numpy as jnp
 from jax import lax
+from jax.experimental import pallas as pl
+from jax.experimental.pallas import tpu as pltpu
 from jax.sharding import PartitionSpec as P
 
 HEADS = 24
@@ -297,29 +299,6 @@
     return lax.dot_general(left, right, (((0,), (0,)), ((), ())), precision=FAST)
 
 
-def partners(value, step):
-    return lax.ppermute(value, "dp", [(i, i ^ step) for i in range(4)])
-
-
-def gather_near(block):
-    return [block] + [partners(block, step) for step in (1, 2, 3)]
-
-
-def scatter_near(blocks):
-    arrived = [partners(blocks[step], step) for step in (1, 2, 3)]
-    return blocks[0] + arrived[0] + arrived[1] + arrived[2]
-
-
-def exchange_near(blocks, me):
-    near = jnp.stack([blocks[0]] + [partners(blocks[step], step) for step in (1, 2, 3)])
-    order = jnp.bitwise_xor(jnp.arange(4), me)
-    return jnp.take(near, order, axis=0)
-
-
-def other_core(value):
-    return lax.ppermute(value, "cond", [(0, 1), (1, 0)])
-
-
 def norm_stats(values):
     centered = values - jnp.mean(values, axis=-1, keepdims=True)
     variance = jnp.mean(centered * centered, axis=-1, keepdims=True)
@@ -335,16 +314,1546 @@
     )
 
 
-def to_both_cores(blocks_of, core, me):
-    mine = exchange_near([blocks_of(me ^ step, core) for step in range(4)], me)
-    other = other_core(mine)
-    low = jnp.where(core == 0, mine, other)
-    high = jnp.where(core == 0, other, mine)
-    return jnp.concatenate([low, high], axis=1)
-
-
 def heads_of(values):
     return values.reshape(values.shape[0], -1, HEAD_CHANNELS)
+
+
+CHUNK = 32
+MESH = pl.DeviceIdType.MESH
+DMA = pltpu.SemaphoreType.DMA
+ANY = pl.BlockSpec(memory_space=pl.ANY)
+
+
+def near_of(me, step):
+    across = lax.rem(lax.rem(me, 2) + lax.rem(step, 2), 2)
+    along = lax.rem(lax.div(me, 2) + lax.div(step, 2), 2)
+    return along * 2 + across
+
+
+def remote(src, dst, send, recv, device):
+    return pltpu.make_async_remote_copy(
+        src_ref=src, dst_ref=dst, send_sem=send, recv_sem=recv, device_id=device,
+        device_id_type=MESH,
+    )
+
+
+def greet(device):
+    barrier = pltpu.get_barrier_semaphore()
+    pl.semaphore_signal(barrier, inc=1, device_id=device, device_id_type=MESH)
+
+
+def relay_begin(full, sems):
+    cross_out, cross_in, mate_out, mate_in = sems
+    core = lax.axis_index("cond")
+    level = lax.axis_index("pair")
+    me = lax.axis_index("dp")
+    unit = full.shape[1] // 4
+    side = lax.rem(level, 2)
+    across = (core, level + 1 - 2 * side, me)
+    mate = (1 - core, level, me)
+
+    def spot(u, step):
+        rows = pl.ds(pl.multiple_of((core * 2 + u) * unit, 8), unit)
+        return full.at[near_of(me, step), rows]
+
+    steps = (1, 2, 3)
+    crosses = [
+        remote(
+            spot(side, step), spot(side, step), cross_out.at[step - 1], cross_in.at[step - 1], across
+        )
+        for step in steps
+    ]
+    mates = [
+        [
+            remote(
+                spot(u, step), spot(u, step), mate_out.at[i, step - 1], mate_in.at[i, step - 1], mate
+            )
+            for step in steps
+        ]
+        for i, u in enumerate((side, 1 - side))
+    ]
+
+    def begin():
+        for copy in crosses + mates[0]:
+            copy.start()
+
+    def end():
+        for cross, far in zip(crosses, mates[1]):
+            cross.wait_recv()
+            far.start()
+        for copy in crosses:
+            copy.wait_send()
+        for copy in mates[0] + mates[1]:
+            copy.wait()
+
+    return begin, end
+
+
+def exchange_body(gather_count, scatter_count, swap_count, relays, *refs):
+    near_count = gather_count + scatter_count
+    count = near_count + swap_count
+    ins = refs[:count]
+    refs = refs[count + relays :]
+    outs = refs[:count]
+    full = refs[count] if relays else None
+    refs = refs[count + relays :]
+    passing, refs = refs[:swap_count], refs[swap_count:]
+    holds = refs[: gather_count + swap_count]
+    send, recv, keep = refs[gather_count + swap_count :][:3]
+    sems = refs[gather_count + swap_count + 3 :]
+    core = lax.axis_index("cond")
+    level = lax.axis_index("pair")
+    me = lax.axis_index("dp")
+    goal = near_of(me, rev(level))
+    quarter = rev(near_of(level, me))
+    shifts = level != 0
+    rises = goal != level
+    final = me == level
+    expected = 3
+    for step in (1, 2, 3):
+        greet((core, level, near_of(me, step)))
+    if relays:
+        greet((1 - core, level, me))
+        greet((core, level + 1 - 2 * lax.rem(level, 2), me))
+        expected = expected + 2
+    if swap_count:
+        pl.when(rises)(lambda: greet((core, quarter, me)))
+        expected = expected + jnp.where(rises, 1, 0)
+    pl.semaphore_wait(pltpu.get_barrier_semaphore(), expected)
+
+    def shift(i, goals):
+        return remote(
+            ins[near_count + i], goals[i], send.at[near_count + i, 0], recv.at[near_count + i, 0],
+            (core, level, goal),
+        )
+
+    def rise(i, sources):
+        return remote(
+            sources[i], outs[near_count + i], send.at[near_count + i, 1],
+            recv.at[near_count + i, 1], (core, goal, me),
+        )
+
+    swap_ins = ins[near_count:]
+    swap_outs = outs[near_count:]
+    near_copies = []
+    if relays:
+        relay_start, relay_end = relay_begin(full, sems)
+        relay_start()
+    for i in range(swap_count):
+        pl.when(jnp.logical_and(shifts, final))(shift(i, swap_outs).start)
+        pl.when(jnp.logical_and(shifts, jnp.logical_not(final)))(shift(i, passing).start)
+        pl.when(jnp.logical_and(jnp.logical_not(shifts), rises))(rise(i, swap_ins).start)
+    for step in (3, 1, 2):
+        for i in range(near_count):
+            if i < gather_count:
+                src, dst = ins[i], outs[i].at[step]
+            else:
+                src, dst = ins[i].at[step], outs[i].at[step - 1]
+            copy = remote(
+                src, dst, send.at[i, step - 1], recv.at[i, step - 1],
+                (core, level, near_of(me, step)),
+            )
+            copy.start()
+            near_copies.append(copy)
+
+    def through(src, hold, dst, sem):
+        load = pltpu.make_async_copy(src, hold, sem)
+        load.start()
+        load.wait()
+        store = pltpu.make_async_copy(hold, dst, sem)
+        store.start()
+        store.wait()
+
+    for i in range(gather_count):
+        through(ins[i], holds[i], outs[i].at[0], keep.at[i])
+    for i in range(swap_count):
+        pl.when(jnp.logical_and(jnp.logical_not(shifts), jnp.logical_not(rises)))(
+            lambda i=i: through(
+                swap_ins[i], holds[gather_count + i], swap_outs[i], keep.at[gather_count + i]
+            )
+        )
+        pl.when(shifts)(shift(i, passing).wait_recv)
+        pl.when(jnp.logical_and(shifts, rises))(rise(i, passing).start)
+    if relays:
+        relay_end()
+    for copy in near_copies:
+        copy.wait()
+    for i in range(swap_count):
+        pl.when(shifts)(shift(i, passing).wait_send)
+        pl.when(rises)(rise(i, swap_ins).wait_send)
+        pl.when(quarter != level)(rise(i, swap_ins).wait_recv)
+
+
+def exchange(collective, gathers=(), scatters=(), swaps=(), relay=()):
+    f32 = jnp.float32
+    shapes = [(4,) + item.shape for item in gathers]
+    shapes += [(3,) + item.shape[1:] for item in scatters]
+    shapes += [item.shape for item in swaps]
+    count = len(shapes)
+    shapes += [item.shape for item in relay]
+    shapes += [item.shape for item in swaps]
+    staged = len(gathers) + len(swaps)
+    scratch = [pltpu.VMEM(item.shape, f32) for item in tuple(gathers) + tuple(swaps)]
+    scratch += [DMA((count, 3)), DMA((count, 3)), DMA((max(staged, 1),))]
+    if relay:
+        scratch += [DMA((3,)), DMA((3,)), DMA((2, 3)), DMA((2, 3))]
+    outs = pl.pallas_call(
+        functools.partial(exchange_body, len(gathers), len(scatters), len(swaps), len(relay)),
+        out_shape=[jax.ShapeDtypeStruct(shape, f32) for shape in shapes],
+        in_specs=[ANY] * (count + len(relay)),
+        out_specs=[ANY] * len(shapes),
+        scratch_shapes=scratch,
+        input_output_aliases={count: count} if relay else {},
+        compiler_params=pltpu.CompilerParams(
+            collective_id=collective, has_side_effects=True, vmem_limit_bytes=16 * 2**20
+        ),
+        name="exchange",
+    )(*gathers, *scatters, *swaps, *relay)
+    return outs[: count + len(relay)]
+
+
+PARTS = 4
+
+
+def open_body(image_in, packed_in, tokens_in, embed_in, weight_in, attend_in, *refs):
+    image, packed, tokens, embed, weight, attend = refs[:6]
+    passing = refs[6:9]
+    hold, send, recv, keep, cross_out, cross_in, pass_out, pass_in, own_out, own_in, block_out, block_in = refs[9:]
+    core = lax.axis_index("cond")
+    level = lax.axis_index("pair")
+    me = lax.axis_index("dp")
+    mate = (1 - core, level, me)
+    side = lax.rem(level, 2)
+    across = (core, level + 1 - 2 * side, me)
+    rows = image_in.shape[0]
+    wide = weight.shape[3]
+    unit = weight.shape[2]
+    turn = rev(level)
+    goal = near_of(me, turn)
+    quarter = rev(near_of(level, me))
+    shifts = level != 0
+    rises = goal != level
+    turned = jnp.logical_and(level == 1, me == 1)
+    raises = jnp.logical_and(level > 0, jnp.logical_not(turned))
+    falls = level < 3
+    taken = jnp.logical_and(quarter < 3, jnp.logical_not(turned))
+    greet(mate)
+    greet(across)
+    for step in (1, 2, 3):
+        greet((core, level, near_of(me, step)))
+    pl.when(rises)(lambda: greet((core, quarter, me)))
+    pl.when(quarter > 0)(lambda: greet((core, quarter - 1, level)))
+    pl.when(taken)(lambda: greet((core, quarter + 1, level)))
+    expected = (
+        5 + jnp.where(rises, 1, 0) + jnp.where(raises, 1, 0) + jnp.where(falls, 1, 0)
+    )
+    pl.semaphore_wait(pltpu.get_barrier_semaphore(), expected)
+
+    body = image.at[pl.ds(1, rows)]
+    ins = (image_in, tokens_in, embed_in)
+    ends = (body, tokens, embed)
+
+    def shift(goals):
+        return [
+            remote(src, dst, send.at[i], recv.at[i], (core, level, goal))
+            for i, (src, dst) in enumerate(zip(ins, goals))
+        ]
+
+    def rise(sources):
+        return [
+            remote(src, dst, send.at[3 + i], recv.at[3 + i], (core, goal, me))
+            for i, (src, dst) in enumerate(zip(sources, ends))
+        ]
+
+    def stay():
+        image_load = pltpu.make_async_copy(image_in, hold, keep.at[0])
+        image_load.start()
+        rest = [
+            pltpu.make_async_copy(src, dst, keep.at[i])
+            for i, (src, dst) in ((1, (tokens_in, tokens)), (2, (embed_in, embed)))
+        ]
+        run("start", *rest)
+        image_load.wait()
+        image_store = pltpu.make_async_copy(hold, body, keep.at[0])
+        image_store.start()
+        run("wait", image_store, *rest)
+
+    lower = remote(
+        image_in.at[pl.ds(rows - 1, 1)], image.at[pl.ds(0, 1)], send.at[6], recv.at[6],
+        (core, me, near_of(me, rev(jnp.minimum(level + 1, 3)))),
+    )
+    upper = remote(
+        image_in.at[pl.ds(0, 1)], image.at[pl.ds(rows + 1, 1)], send.at[7], recv.at[7],
+        (core, me, near_of(me, rev(jnp.maximum(level - 1, 0)))),
+    )
+    around = pltpu.make_async_copy(
+        image_in.at[pl.ds(0, 1)], image.at[pl.ds(rows + 1, 1)], keep.at[4]
+    )
+
+    def vectors(step):
+        return remote(
+            packed_in, packed.at[me], send.at[7 + step], recv.at[7 + step],
+            (core, level, near_of(me, step)),
+        )
+
+    mine = core * 2 + side
+    other = core * 2 + 1 - side
+
+    size = unit // PARTS
+
+    def block(step, h):
+        to = near_of(me, step)
+        src = weight_in.at[
+            pl.ds(pl.multiple_of(mine * unit + h * size, 8), size),
+            pl.ds(pl.multiple_of(to * wide, wide), wide),
+        ]
+        dst = weight.at[me, mine, pl.ds(h * size, size)]
+        return remote(
+            src, dst, block_out.at[h, step - 1], block_in.at[h, step - 1], (core, level, to)
+        )
+
+    piece = attend.shape[2] // 3
+
+    def thirds(step):
+        to = near_of(me, step)
+        found = []
+        for p in range(3):
+            src = attend_in.at[
+                pl.ds(pl.multiple_of(mine * unit, 8), unit),
+                pl.ds(pl.multiple_of((p * 4 + to) * piece, piece), piece),
+            ]
+            dst = attend.at[
+                me, pl.ds(pl.multiple_of(mine * unit, 8), unit), pl.ds(p * piece, piece)
+            ]
+            spot = 11 + step * 3 + p
+            found.append(remote(src, dst, send.at[spot], recv.at[spot], (core, level, to)))
+        return found
+
+    def crossed(step, u, h):
+        spot = weight.at[near_of(me, step), u, pl.ds(h * size, size)]
+        return remote(spot, spot, cross_out.at[h, step - 1], cross_in.at[h, step - 1], across)
+
+    def passed(step, u, turn, h):
+        spot = weight.at[near_of(me, step), u, pl.ds(h * size, size)]
+        k = turn * PARTS + h
+        return remote(spot, spot, pass_out.at[k, step - 1], pass_in.at[k, step - 1], mate)
+
+    def run(method, *copies):
+        for copy in copies:
+            getattr(copy, method)()
+
+    final = me == level
+    pl.when(jnp.logical_and(shifts, final))(lambda: run("start", *shift(ends)))
+    pl.when(jnp.logical_and(shifts, jnp.logical_not(final)))(lambda: run("start", *shift(passing)))
+    pl.when(jnp.logical_and(jnp.logical_not(shifts), rises))(lambda: run("start", *rise(ins)))
+    pl.when(falls)(lower.start)
+    pl.when(raises)(upper.start)
+    pl.when(turned)(around.start)
+    own = [pltpu.make_async_copy(packed_in, packed.at[me], keep.at[3])]
+    own_blocks = [
+        remote(
+            weight_in.at[pl.ds(u * unit, unit), pl.ds(pl.multiple_of(me * wide, wide), wide)],
+            weight.at[me, u],
+            own_out.at[u],
+            own_in.at[u],
+            mate,
+        )
+        for u in range(4)
+    ] + [
+        remote(
+            attend_in.at[:, pl.ds(pl.multiple_of((p * 4 + me) * piece, piece), piece)],
+            attend.at[me, :, pl.ds(p * piece, piece)],
+            own_out.at[4 + p],
+            own_in.at[4 + p],
+            mate,
+        )
+        for p in range(3)
+    ]
+    for step in (3, 1, 2):
+        vectors(step).start()
+    for h in range(PARTS):
+        for step in (3, 1, 2):
+            block(step, h).start()
+    run("start", *own, *own_blocks)
+    pl.when(jnp.logical_and(jnp.logical_not(shifts), jnp.logical_not(rises)))(stay)
+
+    for step in (3, 1, 2):
+        run("start", *thirds(step))
+
+    @pl.when(shifts)
+    def _():
+        run("wait_recv", *shift(passing))
+        pl.when(rises)(lambda: run("start", *rise(passing)))
+
+    for h in range(PARTS):
+        for step in (2, 1, 3):
+            block(step, h).wait_recv()
+            crossed(step, mine, h).start()
+            passed(step, mine, 0, h).start()
+    for h in range(PARTS):
+        for step in (2, 1, 3):
+            crossed(step, other, h).wait_recv()
+            passed(step, other, 1, h).start()
+    pl.when(shifts)(lambda: run("wait_send", *shift(passing)))
+    pl.when(rises)(lambda: run("wait_send", *rise(ins)))
+    pl.when(quarter != level)(lambda: run("wait_recv", *rise(ins)))
+    pl.when(falls)(lower.wait_send)
+    pl.when(raises)(upper.wait_send)
+    pl.when(quarter > 0)(lower.wait_recv)
+    pl.when(taken)(upper.wait_recv)
+    pl.when(turned)(around.wait)
+    for step in (1, 2, 3):
+        vectors(step).wait()
+        run("wait", *thirds(step))
+        for h in range(PARTS):
+            block(step, h).wait_send()
+            crossed(step, mine, h).wait_send()
+            for u, turn_of in ((mine, 0), (other, 1)):
+                passed(step, u, turn_of, h).wait()
+    run("wait", *own, *own_blocks)
+
+
+def open_exchange(collective, image, packed, tokens, embed, weight, attend):
+    rows, cols, chan = image.shape
+    unit = weight.shape[0] // 4
+    shapes = [
+        (rows + 2, cols, chan),
+        (4,) + packed.shape,
+        tokens.shape,
+        embed.shape,
+        (4, 4, unit, weight.shape[1] // 4),
+        (4, attend.shape[0], attend.shape[1] // 4),
+        image.shape,
+        tokens.shape,
+        embed.shape,
+    ]
+    return pl.pallas_call(
+        open_body,
+        out_shape=[jax.ShapeDtypeStruct(shape, jnp.float32) for shape in shapes],
+        in_specs=[ANY] * 6,
+        out_specs=[ANY] * 9,
+        scratch_shapes=[
+            pltpu.VMEM(image.shape, jnp.float32),
+            DMA((23,)),
+            DMA((23,)),
+            DMA((5,)),
+            DMA((PARTS, 3)),
+            DMA((PARTS, 3)),
+            DMA((2 * PARTS, 3)),
+            DMA((2 * PARTS, 3)),
+            DMA((7,)),
+            DMA((7,)),
+            DMA((PARTS, 3)),
+            DMA((PARTS, 3)),
+        ],
+        compiler_params=pltpu.CompilerParams(collective_id=collective, has_side_effects=True),
+        name="open_exchange",
+    )(image, packed, tokens, embed, weight, attend)
+
+
+def rev(z):
+    return 2 * lax.rem(z, 2) + lax.div(z, 2)
+
+
+def plane_spot(level, me):
+    return me, near_of(me, rev(level))
+
+
+def home_spot(level, me):
+    return rev(near_of(level, me)), level
+
+
+def stream_setup(homeward=False):
+    core = lax.axis_index("cond")
+    level = lax.axis_index("pair")
+    me = lax.axis_index("dp")
+    greet((1 - core, level, me))
+    for step in (1, 2, 3):
+        greet((core, level, near_of(me, step)))
+    pl.when(level > 0)(lambda: greet((core, level - 1, me)))
+    pl.when(level < 3)(lambda: greet((core, level + 1, me)))
+    ends = jnp.where(level == 0, 1, 0) + jnp.where(level == 3, 1, 0)
+    expected = 6 - ends
+    if homeward:
+        moves = jnp.logical_or(level != 0, me != 0)
+        back_up, back_over = plane_spot(level, me)
+        pl.when(moves)(lambda: greet((core, back_up, back_over)))
+        expected = expected + jnp.where(moves, 1, 0)
+    pl.semaphore_wait(pltpu.get_barrier_semaphore(), expected)
+
+
+def sum_stream(sections, scratch, hooks):
+    (
+        data,
+        stage,
+        first,
+        second,
+        own,
+        load_sem,
+        core_out,
+        core_in,
+        plane_out,
+        plane_in,
+        first_in,
+        second_in,
+        hop_out,
+        cast_out,
+        cast_low,
+        final_in,
+        keep_sem,
+        pair_out,
+        pair_in,
+    ) = scratch
+    ranges = []
+    total = 0
+    for kind, src, dst in sections:
+        if kind == "plain":
+            count, width = src.shape[1] // CHUNK, src.shape[2]
+        else:
+            count, width = 4 * (src.shape[2] // CHUNK), src.shape[3]
+        ranges.append((total, total + count, kind, src, dst, width))
+        total += count
+    core = lax.axis_index("cond")
+    level = lax.axis_index("pair")
+    me = lax.axis_index("dp")
+    mate = (1 - core, level, me)
+    ring = data.shape[0]
+    full = data.shape[2]
+
+    def rank_of(j):
+        return jnp.where(lax.rem(j, 2) == 0, level, 3 - level)
+
+    def at_rank(j, rank):
+        return (core, jnp.where(lax.rem(j, 2) == 0, rank, 3 - rank), me)
+
+    def inside(j, low, high):
+        return jnp.logical_and(j >= low, j < high)
+
+    def swap_place(j):
+        inner = False
+        k = 0
+        for low, high, kind, src, dst, width in ranges:
+            if kind == "swap":
+                here = inside(j, low, high)
+                inner = jnp.logical_or(inner, here)
+                k = jnp.where(here, j - low, k)
+        return inner, k
+
+    def moved(j):
+        inner, k = swap_place(j)
+        return jnp.logical_and(inner, lax.rem(k, 4) != 0)
+
+    def kinds(j, action):
+        narrow = False
+        for low, high, kind, src, dst, width in ranges:
+            if width != full:
+                here = inside(j, low, high)
+                narrow = jnp.logical_or(narrow, here)
+                pl.when(here)(lambda width=width: action(width))
+        pl.when(jnp.logical_not(narrow))(lambda: action(full))
+
+    def cut(ref, width):
+        return ref if ref.shape[-1] == width else ref.at[:, pl.ds(0, width)]
+
+    def each_source(j, action):
+        target = data.at[lax.rem(j, ring)]
+        mine = own.at[lax.rem(j, 4)]
+        for low, high, kind, src, dst, width in ranges:
+
+            @pl.when(inside(j, low, high))
+            def _(low=low, kind=kind, src=src, width=width):
+                k = j - low
+                if kind == "plain":
+                    rows = pl.ds(pl.multiple_of(k * CHUNK, CHUNK), CHUNK)
+                    action(lambda half: src.at[half, rows], target, mine)
+                else:
+                    rows = pl.ds(pl.multiple_of(lax.div(k, 4) * CHUNK, CHUNK), CHUNK)
+                    spot = near_of(me, lax.rem(k, 4))
+                    action(
+                        lambda half: src.at[spot, half, rows], cut(target, width), cut(mine, width)
+                    )
+
+    def each_final(j, action):
+        for low, high, kind, src, dst, width in ranges:
+
+            @pl.when(inside(j, low, high))
+            def _(low=low, kind=kind, dst=dst, width=width):
+                k = j - low
+                if kind == "plain":
+                    rows = pl.ds(pl.multiple_of(k * CHUNK, CHUNK), CHUNK)
+                    action(
+                        lambda half: [(dst.at[half, rows], lambda x: x, 0)],
+                        first.at[lax.rem(j, ring)],
+                    )
+                else:
+                    rows = pl.ds(pl.multiple_of(lax.div(k, 4) * CHUNK, CHUNK), CHUNK)
+                    spot = near_of(me, lax.rem(k, 4))
+                    pieces = 1 if width == full else 3
+                    piece = width // pieces
+
+                    def targets(half):
+                        found = []
+                        for p in range(pieces):
+                            columns = pl.ds(
+                                pl.multiple_of(p * 4 * piece + spot * piece, piece), piece
+                            )
+                            found.append(
+                                (
+                                    dst.at[half, rows, columns],
+                                    lambda x, p=p: x
+                                    if x.shape[-1] == piece
+                                    else x.at[:, pl.ds(p * piece, piece)],
+                                    p,
+                                )
+                            )
+                        return found
+
+                    action(targets, stage.at[k])
+
+    def core_copy(j, src, dst):
+        return remote(src, dst, core_out.at[j], core_in.at[j], mate)
+
+    def plane_copy(j, width):
+        inner, k = swap_place(j)
+        return remote(
+            cut(first.at[lax.rem(j, ring)], width),
+            cut(stage.at[k], width),
+            plane_out.at[j],
+            plane_in.at[j],
+            (core, level, near_of(me, lax.rem(k, 4))),
+        )
+
+    def hop_first(j, src, rank, width):
+        return remote(
+            cut(src, width), cut(first.at[lax.rem(j, ring)], width), hop_out.at[j], first_in.at[j], at_rank(j, rank)
+        )
+
+    def hop_second(j, width):
+        k = lax.div(j, 2)
+        return remote(
+            cut(data.at[lax.rem(j, ring)], width), cut(second.at[lax.rem(k, ring // 2)], width), hop_out.at[j], second_in.at[k],
+            at_rank(j, 2),
+        )
+
+    def start(j):
+        def go(source, target, mine):
+            core_copy(j, source(1 - core), target).start()
+            pltpu.make_async_copy(source(core), mine, load_sem.at[lax.rem(j, 4)]).start()
+
+        each_source(j, go)
+
+    def combine(j):
+        def go(source, target, mine):
+            pltpu.make_async_copy(source(core), mine, load_sem.at[lax.rem(j, 4)]).wait()
+            core_copy(j, source(1 - core), target).wait_recv()
+            target[...] += mine[...]
+
+        each_source(j, go)
+
+    def depart(j):
+        rank = rank_of(j)
+
+        def go(width):
+            pl.when(rank == 0)(lambda: hop_first(j, data.at[lax.rem(j, ring)], 1, width).start())
+            pl.when(rank == 3)(lambda: hop_second(j, width).start())
+
+        kinds(j, go)
+
+    def relay(j):
+        def go(width):
+            hop_first(j, data.at[lax.rem(j, ring)], 1, width).wait_recv()
+            spot = lax.rem(j, ring)
+            first[spot, :, :width] += data[spot, :, :width]
+            hop_first(j, first.at[lax.rem(j, ring)], 2, width).start()
+
+        pl.when(rank_of(j) == 1)(lambda: kinds(j, go))
+
+    def casts(j, rank, half_targets, source, sems):
+        return [
+            remote(
+                cut_of(source) if source is not None else ref, ref, sems.at[j, p], final_in.at[j, p],
+                at_rank(j, rank),
+            )
+            for ref, cut_of, p in half_targets
+        ]
+
+    def pairs(j, half_targets, source):
+        return [
+            remote(
+                cut_of(source) if source is not None else ref, ref, pair_out.at[j, p],
+                pair_in.at[j, p], mate,
+            )
+            for ref, cut_of, p in half_targets
+        ]
+
+    def keeps(j, half_targets, source):
+        return [
+            pltpu.make_async_copy(cut_of(source), ref, keep_sem.at[j, p])
+            for ref, cut_of, p in half_targets
+        ]
+
+    def root(j):
+        def add(width):
+            hop_first(j, first.at[lax.rem(j, ring)], 2, width).wait_recv()
+            hop_second(j, width).wait_recv()
+            spot = lax.rem(j, ring)
+            first[spot, :, :width] += (
+                data[spot, :, :width] + second[lax.rem(lax.div(j, 2), ring // 2), :, :width]
+            )
+
+        @pl.when(rank_of(j) == 2)
+        def _():
+            kinds(j, add)
+
+            @pl.when(moved(j))
+            def _():
+                kinds(j, lambda width: plane_copy(j, width).start())
+
+            inner, k = swap_place(j)
+
+            @pl.when(jnp.logical_and(inner, jnp.logical_not(moved(j))))
+            def _():
+                stage[k] = first[lax.rem(j, ring)]
+
+    def spread(j):
+        def send(targets, source):
+            goals = targets(core)
+            for copy in (
+                casts(j, 1, goals, source, cast_out)
+                + casts(j, 3, goals, source, cast_low)
+                + keeps(j, goals, source)
+                + pairs(j, goals, source)
+            ):
+                copy.start()
+
+        @pl.when(rank_of(j) == 2)
+        def _():
+            @pl.when(moved(j))
+            def _():
+                kinds(j, lambda width: plane_copy(j, width).wait_recv())
+
+            each_final(j, send)
+
+    def landed(j):
+        rank = rank_of(j)
+
+        def go(targets, source):
+            goals = targets(core)
+            for copy in casts(j, 1, goals, None, cast_out):
+                copy.wait_recv()
+            pl.when(rank == 1)(
+                lambda: [copy.start() for copy in casts(j, 0, goals, None, cast_out)] and None
+            )
+            for copy in pairs(j, goals, None):
+                copy.start()
+
+        @pl.when(jnp.logical_or(rank == 1, rank == 3))
+        def _():
+            each_final(j, go)
+
+    def arrived(j):
+        def go(targets, source):
+            goals = targets(core)
+            for copy in casts(j, 0, goals, None, cast_out):
+                copy.wait_recv()
+            for copy in pairs(j, goals, None):
+                copy.start()
+
+        @pl.when(rank_of(j) == 0)
+        def _():
+            each_final(j, go)
+
+    def finish(j):
+        rank = rank_of(j)
+
+        def sent(source, target, mine):
+            core_copy(j, source(1 - core), target).wait_send()
+
+        each_source(j, sent)
+
+        @pl.when(jnp.logical_and(moved(j), rank == 2))
+        def _():
+            kinds(j, lambda width: plane_copy(j, width).wait_send())
+
+        @pl.when(rank != 2)
+        def _():
+            kinds(j, lambda width: hop_first(j, data.at[lax.rem(j, ring)], 1, width).wait_send())
+
+        def go(targets, source):
+            goals = targets(core)
+
+            @pl.when(jnp.logical_or(rank == 1, rank == 2))
+            def _():
+                for copy in casts(j, 1, goals, None, cast_out):
+                    copy.wait_send()
+
+            @pl.when(rank == 2)
+            def _():
+                for copy in casts(j, 3, goals, None, cast_low):
+                    copy.wait_send()
+                for copy in keeps(j, goals, source):
+                    copy.wait()
+
+            for copy in pairs(j, goals, None):
+                copy.wait()
+
+        each_final(j, go)
+
+    stages = (
+        (0, start),
+        (3, combine),
+        (5, depart),
+        (8, relay),
+        (11, root),
+        (14, spread),
+        (17, landed),
+        (20, arrived),
+        (23, finish),
+    )
+
+    def step(t, carry):
+        for lag, stage_of in stages:
+            j = t - lag
+
+            @pl.when(jnp.logical_and(j >= 0, j < total))
+            def _(j=j, stage_of=stage_of):
+                stage_of(j)
+
+        for low, high, hook in hooks:
+            pl.when(jnp.logical_and(t >= low, t < high))(lambda hook=hook, low=low: hook(t - low))
+        return carry
+
+    lax.fori_loop(0, total + 23, step, 0)
+
+
+def stream_scratch(total, most, width):
+    ring = 32
+    return [
+        pltpu.VMEM((ring, CHUNK, width), jnp.float32),
+        pltpu.VMEM((most, CHUNK, width), jnp.float32),
+        pltpu.VMEM((ring, CHUNK, width), jnp.float32),
+        pltpu.VMEM((ring // 2, CHUNK, width), jnp.float32),
+        pltpu.VMEM((4, CHUNK, width), jnp.float32),
+        DMA((4,)),
+        DMA((total,)),
+        DMA((total,)),
+        DMA((total,)),
+        DMA((total,)),
+        DMA((total,)),
+        DMA(((total + 1) // 2,)),
+        DMA((total,)),
+        DMA((total, 3)),
+        DMA((total, 3)),
+        DMA((total, 3)),
+        DMA((total, 3)),
+        DMA((total, 3)),
+        DMA((total, 3)),
+    ]
+
+
+SCRATCH = 19
+
+
+def near_slots(shares, arrived, send, recv, base):
+    core = lax.axis_index("cond")
+    level = lax.axis_index("pair")
+    me = lax.axis_index("dp")
+    return [
+        remote(
+            shares.at[step], arrived.at[step - 1], send.at[base + step - 1],
+            recv.at[base + step - 1], (core, level, near_of(me, step)),
+        )
+        for step in (3, 1, 2)
+    ]
+
+
+def near_blocks(block, everyone, send, recv, base):
+    core = lax.axis_index("cond")
+    level = lax.axis_index("pair")
+    me = lax.axis_index("dp")
+    return [
+        remote(
+            block, everyone.at[step], send.at[base + step - 1], recv.at[base + step - 1],
+            (core, level, near_of(me, step)),
+        )
+        for step in (3, 1, 2)
+    ]
+
+
+def row_stats(rows):
+    centered = rows - jnp.mean(rows, axis=-1, keepdims=True)
+    inverse = lax.rsqrt(jnp.mean(centered * centered, axis=-1, keepdims=True) + EPSILON)
+    return centered * inverse, inverse
+
+
+def halves(value):
+    high = value.astype(jnp.bfloat16)
+    return high, (value - high.astype(jnp.float32)).astype(jnp.bfloat16)
+
+
+def three_pass(left, right, dims):
+    def one(x, y):
+        return lax.dot_general(x, y, (dims, ((), ())), preferred_element_type=jnp.float32)
+
+    return one(left[0], right[1]) + one(left[1], right[0]) + one(left[0], right[0])
+
+
+TILE = 256
+
+
+def backward_body(
+    output_ref, attend_ref, two_ref, text_ref, cot_ref, one_ref, response_ref, reduce_w_ref,
+    act_ref, slope_ref, normed_ref, expand_w_ref, conv_ref, out_ref, base_ref, small_ref,
+    rows_ref, embed_ref, silu_ref,
+    output_out, attend_out, mapper_out, reduce_out, small_out, expand_out,
+    mapper_part, reduce_part, expand_part, one_out, text_out, grad_out, layer_out,
+    *scratch
+):
+    (
+        front_got, front_own, conv, grad, one, out_got, out_own, base, small, wide, high, low,
+        weights, acts, slopes, columns, product, front, sums, spread_own, spread_got,
+        text_got, text_own, text_all, ratio, mapped,
+    ) = scratch[SCRATCH : SCRATCH + 26]
+    (
+        send, recv, keep, tile_out, tile_in, load, front_out, front_in, spread_out, spread_in,
+        piece_out, piece_in, text_out_sem, text_in_sem,
+    ) = scratch[SCRATCH + 26 :]
+    stream_setup(True)
+    core = lax.axis_index("cond")
+    level = lax.axis_index("pair")
+    me = lax.axis_index("dp")
+    moves = jnp.logical_or(level != 0, me != 0)
+    up, over = home_spot(level, me)
+    pixels, chan = conv.shape
+    spots = wide.shape[0]
+    texts = text_own.shape[0]
+    count = chan // TILE
+    scatters = near_slots(two_ref, front_got, send, recv, 0)
+    scatters += near_slots(text_ref, text_got, send, recv, 6)
+    start_loads = [
+        pltpu.make_async_copy(src, dst, keep.at[6 + i])
+        for i, (src, dst) in enumerate(
+            ((two_ref.at[0], front_own), (text_ref.at[0], text_own), (cot_ref, conv), (one_ref, one))
+        )
+    ]
+
+    def near_tile(i):
+        rows = pl.ds(pl.multiple_of(i * 16, 16), 16)
+        return [
+            remote(
+                grad.at[rows],
+                wide.at[pl.ds(pl.multiple_of(step * pixels + i * 16, 16), 16)],
+                piece_out.at[i, step - 1],
+                piece_in.at[i, step - 1],
+                (core, level, near_of(me, step)),
+            )
+            for step in (3, 1, 2)
+        ]
+
+    def late():
+        found = []
+        for step in (3, 1, 2):
+            device = (core, level, near_of(me, step))
+            found.append(
+                remote(
+                    text_all.at[0], text_all.at[step], text_out_sem.at[step - 1],
+                    text_in_sem.at[step - 1], device,
+                )
+            )
+            found.append(
+                remote(
+                    ratio.at[0], ratio.at[step], text_out_sem.at[2 + step],
+                    text_in_sem.at[2 + step], device,
+                )
+            )
+        return found
+
+    one_kept = pltpu.make_async_copy(grad, one_out, keep.at[10])
+    text_kept = pltpu.make_async_copy(text_all, text_out, keep.at[11])
+
+    def arrive(t):
+        for copy in start_loads + scatters:
+            copy.wait()
+        ratio[0] = jnp.zeros_like(ratio[0])
+        text_all[0] = jnp.zeros_like(text_all[0])
+        text_all[0, 0:texts] = text_own[...] + text_got[0] + text_got[1] + text_got[2]
+
+    def normalize(t):
+        scale = rows_ref[6:7]
+        shift = rows_ref[7:8]
+        for half in range(2):
+            rows = pl.ds(pl.multiple_of(t * 16 + half * 8, 8), 8)
+            back = front_own[rows] + front_got[0, rows] + front_got[1, rows] + front_got[2, rows]
+            hidden = one[rows]
+            normed, inverse = row_stats(hidden * scale + shift)
+            two = conv[rows] + inverse * (
+                back
+                - jnp.mean(back, axis=-1, keepdims=True)
+                - normed * jnp.mean(back * normed, axis=-1, keepdims=True)
+            )
+            grad[rows] = two * scale
+            ratio[0, 0:8] += two * hidden
+            ratio[0, 8:16] += two
+        for copy in near_tile(t):
+            copy.start()
+
+    def give_late(t):
+        for copy in late():
+            copy.start()
+        one_kept.start()
+        wide[0:pixels] = grad[...]
+
+    def gathered(t):
+        def wait(i, carry):
+            for copy in near_tile(i):
+                copy.wait()
+            return carry
+
+        lax.fori_loop(0, pixels // 16, wait, 0)
+        for copy in late():
+            copy.wait()
+        one_kept.wait()
+        text_kept.start()
+
+        def piece(i, carry):
+            rows = pl.ds(pl.multiple_of(i * 16, 16), 16)
+            high[rows], low[rows] = halves(wide[rows])
+            return carry
+
+        lax.fori_loop(0, spots // 16, piece, 0)
+
+    def mapper_stores():
+        half = mapper_part.shape[1]
+        return [
+            pltpu.make_async_copy(
+                mapped.at[pl.ds(c * half, half)], mapper_part.at[c], load.at[10 + c]
+            )
+            for c in (0, 1)
+        ]
+
+    def text_products(t):
+        left = halves(silu_ref[...])
+
+        def strip(k, carry):
+            cols = pl.ds(pl.multiple_of(k * TILE, TILE), TILE)
+            right = halves(text_all[:, :, cols].reshape(-1, TILE))
+            mapped[:, cols] = three_pass(left, right, ((0,), (0,)))
+            return carry
+
+        lax.fori_loop(0, count, strip, 0)
+        for copy in mapper_stores():
+            copy.start()
+        column_pair(0)[0].start()
+        column_pair(0)[1].start()
+        first_loads[0].wait()
+        total = ratio[0] + ratio[1] + ratio[2] + ratio[3]
+        scale_sum = jnp.sum(total[0:8], axis=0, keepdims=True)
+        shift_sum = jnp.sum(total[8:16], axis=0, keepdims=True)
+        odd = lax.rem(lax.broadcasted_iota(jnp.int32, (CHUNK, chan), 0), 2) == 1
+        both = jnp.where(odd, shift_sum, scale_sum)
+        small[0] = both * embed_ref[:, 0:1]
+        sums[4:5] = scale_sum
+        sums[5:6] = shift_sum
+        sums[6:7] = jnp.sum(wide[...], axis=0, keepdims=True)
+        sums[7:8] = jnp.sum(text_all[...].reshape(-1, chan), axis=0, keepdims=True)
+        width = chan // 4
+        place = pl.ds(pl.multiple_of(me * width, width), width)
+        small[1, 3:4, 0:width] = sums[6:7, place]
+        small[1, 3:4, width : 2 * width] = sums[7:8, place]
+        pair_place = pl.ds(pl.multiple_of(lax.rem(me, 2) * 2 * width, width), 2 * width)
+        small[1, 4:5, width : 3 * width] = jnp.where(
+            me < 2, sums[4:5, pair_place], sums[5:6, pair_place]
+        )
+
+    def column_pair(i):
+        return [
+            pltpu.make_async_copy(
+                response_ref.at[
+                    :, pl.ds(pl.multiple_of(c * (chan // 2) + i * 128, 128), 128)
+                ],
+                columns.at[lax.rem(i, 2), :, pl.ds(c * 128, 128)],
+                load.at[6 + lax.rem(i, 2) if c == 0 else 12 + lax.rem(i, 2)],
+            )
+            for c in (0, 1)
+        ]
+
+    def reduce_stores(i):
+        return [
+            pltpu.make_async_copy(
+                product.at[pl.ds(c * 128, 128)],
+                reduce_part.at[c, pl.ds(pl.multiple_of(i * 128, 128), 128)],
+                load.at[8 + c],
+            )
+            for c in (0, 1)
+        ]
+
+    def reduce_outer(i):
+        for copy in column_pair(i):
+            copy.wait()
+
+        @pl.when(i + 1 < count)
+        def _():
+            for copy in column_pair(jnp.minimum(i + 1, count - 1)):
+                copy.start()
+
+        @pl.when(i + 1 == count)
+        def _():
+            weight_load(reduce_w_ref, 0).start()
+            act_load(0).start()
+
+        @pl.when(i > 0)
+        def _():
+            for copy in reduce_stores(jnp.maximum(i - 1, 0)):
+                copy.wait()
+
+        @pl.when(i == 0)
+        def _():
+            for copy in mapper_stores():
+                copy.wait()
+
+        left = halves(columns[lax.rem(i, 2), :, 0:TILE])
+
+        def strip(k, carry):
+            cols = pl.ds(pl.multiple_of(k * TILE, TILE), TILE)
+            product[0:TILE, cols] = three_pass(left, (high[:, cols], low[:, cols]), ((0,), (0,)))
+            return carry
+
+        lax.fori_loop(0, count, strip, 0)
+        for copy in reduce_stores(i):
+            copy.start()
+
+    def settle_reduce(t):
+        for copy in reduce_stores(count - 1):
+            copy.wait()
+        text_kept.wait()
+        for copy in loads:
+            copy.start()
+        sums[0:4] = jnp.zeros((4, chan), jnp.float32)
+
+    outward = near_slots(out_ref, out_got, send, recv, 3)
+
+    def away(i):
+        rows = pl.ds(pl.multiple_of(i * 8, 8), 8)
+        return remote(
+            base.at[rows], layer_out.at[rows], tile_out.at[i], tile_in.at[i], (core, up, over)
+        )
+
+    def here(i):
+        rows = pl.ds(pl.multiple_of(i * 8, 8), 8)
+        return pltpu.make_async_copy(base.at[rows], layer_out.at[rows], tile_out.at[i])
+
+    first_loads = [pltpu.make_async_copy(small_ref, small, keep.at[1])]
+    loads = [
+        pltpu.make_async_copy(conv_ref, conv, keep.at[2]),
+        pltpu.make_async_copy(out_ref.at[0], out_own, keep.at[3]),
+        pltpu.make_async_copy(base_ref, base, keep.at[4]),
+    ]
+    kept = pltpu.make_async_copy(one, grad_out, keep.at[5])
+
+    def tile_rows(i):
+        return pl.ds(pl.multiple_of(i * TILE, TILE), TILE)
+
+    def weight_load(ref, i):
+        return pltpu.make_async_copy(
+            ref.at[tile_rows(i)], weights.at[lax.rem(i, 2)], load.at[lax.rem(i, 2)]
+        )
+
+    def act_load(i):
+        return pltpu.make_async_copy(
+            act_ref.at[:, tile_rows(i)], acts.at[lax.rem(i, 2)], load.at[2 + lax.rem(i, 2)]
+        )
+
+    def slope_load(i):
+        return pltpu.make_async_copy(
+            slope_ref.at[:, tile_rows(i)], slopes.at[lax.rem(i, 2)], load.at[4 + lax.rem(i, 2)]
+        )
+
+    part = columns.shape[2]
+
+    def column_load(i):
+        return pltpu.make_async_copy(
+            normed_ref.at[:, pl.ds(pl.multiple_of(i * part, part), part)],
+            columns.at[lax.rem(i, 2)],
+            load.at[6 + lax.rem(i, 2)],
+        )
+
+    def product_stores(i):
+        half = part // 2
+        return [
+            pltpu.make_async_copy(
+                product.at[pl.ds(c * half, half)], expand_part.at[i, c], load.at[8 + c]
+            )
+            for c in (0, 1)
+        ]
+
+    def front_sends(i):
+        found = []
+        for step in (3, 1, 2):
+            found.append(
+                remote(
+                    front.at[lax.rem(i, 2), pl.ds(step * pixels, pixels)],
+                    front_got.at[step - 1, :, tile_rows(i)],
+                    front_out.at[i, step - 1],
+                    front_in.at[i, step - 1],
+                    (core, level, near_of(me, step)),
+                )
+            )
+        return found
+
+    for copy in scatters + start_loads + first_loads:
+        copy.start()
+
+    def respond(i):
+        weight_load(reduce_w_ref, i).wait()
+        act_load(i).wait()
+
+        @pl.when(i + 1 < count)
+        def _():
+            weight_load(reduce_w_ref, i + 1).start()
+            act_load(i + 1).start()
+
+        @pl.when(i + 1 == count)
+        def _():
+            act_load(0).start()
+            slope_load(0).start()
+
+        right = halves(weights[lax.rem(i, 2)])
+        cols = tile_rows(i)
+
+        def strip(k, carry):
+            rows = pl.ds(pl.multiple_of(k * pixels, pixels), pixels)
+            value = three_pass((high[rows], low[rows]), right, ((1,), (1,)))
+            wide[rows, cols] = value
+            sums[0:1, cols] += jnp.sum(value * acts[lax.rem(i, 2), rows], axis=0, keepdims=True)
+            sums[1:2, cols] += jnp.sum(value, axis=0, keepdims=True)
+            return carry
+
+        lax.fori_loop(0, 4, strip, 0)
+
+    def spreads():
+        return [
+            remote(
+                spread_own, spread_got.at[step - 1], spread_out.at[step - 1],
+                spread_in.at[step - 1], (core, level, near_of(me, step)),
+            )
+            for step in (3, 1, 2)
+        ]
+
+    def send_out(t):
+        for copy in outward:
+            copy.start()
+
+    def share(t):
+        total = jnp.sum(sums[0:1] * rows_ref[0:1] * rows_ref[1:2], axis=1, keepdims=True)
+        spread_own[...] = jnp.broadcast_to(total, spread_own.shape)
+        for copy in spreads():
+            copy.start()
+
+    def agree(t):
+        for copy in spreads():
+            copy.wait()
+        total = spread_own[...] + spread_got[0] + spread_got[1] + spread_got[2]
+        total = jnp.max(total[0:1], axis=1, keepdims=True)
+        inverse = rows_ref[3:4]
+        norms = rows_ref[1:2]
+        grad_norms = (
+            sums[0:1] * rows_ref[0:1] * inverse - total * rows_ref[4:5] * inverse * inverse
+        )
+        sums[2:3] = grad_norms / norms
+        small[1, 1:2] = sums[0:1] * rows_ref[5:6]
+        small[1, 2:3] = sums[1:2]
+
+    def bend(i):
+        act_load(i).wait()
+        slope_load(i).wait()
+
+        @pl.when(i + 1 < count)
+        def _():
+            act_load(i + 1).start()
+            slope_load(i + 1).start()
+
+        @pl.when(i + 1 == count)
+        def _():
+            column_load(0).start()
+            weight_load(expand_w_ref, 0).start()
+
+        cols = tile_rows(i)
+        factor = rows_ref[2:3, cols]
+        twice = sums[2:3, cols]
+
+        def strip(k, carry):
+            rows = pl.ds(pl.multiple_of(k * 48, 48), 48)
+            value = (
+                wide[rows, cols] * factor + acts[lax.rem(i, 2), rows] * twice
+            ) * slopes[lax.rem(i, 2), rows]
+            high[rows, cols], low[rows, cols] = halves(value)
+            sums[3:4, cols] += jnp.sum(value, axis=0, keepdims=True)
+            return carry
+
+        lax.fori_loop(0, spots // 48, strip, 0)
+
+    def outer(i):
+        column_load(i).wait()
+        pl.when(i + 1 < 4)(lambda: column_load(jnp.minimum(i + 1, 3)).start())
+        pl.when(i > 0)(lambda: [copy.wait() for copy in product_stores(jnp.maximum(i - 1, 0))] and None)
+        left = halves(columns[lax.rem(i, 2)])
+
+        def strip(k, carry):
+            cols = pl.ds(pl.multiple_of(k * TILE, TILE), TILE)
+            product[:, cols] = three_pass(left, (high[:, cols], low[:, cols]), ((0,), (0,)))
+            return carry
+
+        lax.fori_loop(0, count, strip, 0)
+        for copy in product_stores(i):
+            copy.start()
+
+    def settle_outer(t):
+        for copy in product_stores(3):
+            copy.wait()
+        small[1, 0:1] = sums[3:4]
+
+    def backward(i):
+        weight_load(expand_w_ref, i).wait()
+        pl.when(i + 1 < count)(lambda: weight_load(expand_w_ref, jnp.minimum(i + 1, count - 1)).start())
+
+        @pl.when(i > 1)
+        def _():
+            for copy in front_sends(jnp.maximum(i - 2, 0)):
+                copy.wait_send()
+
+        right = halves(weights[lax.rem(i, 2)])
+
+        def strip(k, carry):
+            rows = pl.ds(pl.multiple_of(k * pixels, pixels), pixels)
+            front[lax.rem(i, 2), rows] = three_pass((high[rows], low[rows]), right, ((1,), (1,)))
+            return carry
+
+        lax.fori_loop(0, 4, strip, 0)
+        front_own[:, tile_rows(i)] = front[lax.rem(i, 2), 0:pixels]
+        for copy in front_sends(i):
+            copy.start()
+
+    def middle(t):
+        loads[0].wait()
+        for i in range(count):
+            for copy in front_sends(i):
+                copy.wait_recv()
+                if i >= count - 2:
+                    copy.wait_send()
+
+    def tiles(t):
+        def tile(i, carry):
+            rows = pl.ds(pl.multiple_of(i * 8, 8), 8)
+            back = front_own[rows] + front_got[0, rows] + front_got[1, rows] + front_got[2, rows]
+            normed, inverse = row_stats(conv[rows])
+            one[rows] = inverse * (
+                back
+                - jnp.mean(back, axis=-1, keepdims=True)
+                - normed * jnp.mean(back * normed, axis=-1, keepdims=True)
+            )
+            return carry
+
+        size = pixels // 48
+        lax.fori_loop(t * size, (t + 1) * size, tile, 0)
+
+    def give(t):
+        kept.start()
+
+    def outlet(t):
+        pl.when(t == 0)(lambda: [copy.wait() for copy in loads[1:] + outward] and None)
+        rows = pl.ds(pl.multiple_of(t * 8, 8), 8)
+        base[rows] += out_own[rows] + out_got[0, rows] + out_got[1, rows] + out_got[2, rows]
+        pl.when(moves)(away(t).start)
+        pl.when(jnp.logical_not(moves))(here(t).start)
+
+    sum_stream(
+        [
+            ("plain", output_ref, output_out),
+            ("swap", attend_ref, attend_out),
+            ("plain", mapper_part, mapper_out),
+            ("plain", reduce_part, reduce_out),
+            ("plain", small, small_out),
+            ("swap", expand_part, expand_out),
+        ],
+        scratch[:SCRATCH],
+        [
+            (12, 13, arrive),
+            (12, 21, normalize),
+            (21, 22, give_late),
+            (24, 25, gathered),
+            (25, 26, text_products),
+            (26, 32, reduce_outer),
+            (32, 33, settle_reduce),
+            (33, 39, respond),
+            (39, 40, share),
+            (40, 41, agree),
+            (41, 47, bend),
+            (47, 51, outer),
+            (51, 52, settle_outer),
+            (52, 58, backward),
+            (68, 69, middle),
+            (68, 74, tiles),
+            (74, 75, give),
+            (60, 78, outlet),
+            (43, 44, send_out),
+        ],
+    )
+    kept.wait()
+
+    def settle(i, carry):
+        pl.when(moves)(away(i).wait)
+        pl.when(jnp.logical_not(moves))(here(i).wait)
+        return carry
+
+    lax.fori_loop(0, base.shape[0] // 8, settle, 0)
+
+
+def backward_sums(
+    collective, output_part, attend_part, two_share, text_share, cot, one, response, reduce_w, act,
+    slope, normed_all, expand_w, conv, out_share, base, small, rows, embed, silu, mapper_half
+):
+    pixels, chan = conv.shape
+    spots = normed_all.shape[0]
+    texts = text_share.shape[1]
+    slots = silu.shape[0] // 4
+    f32, bf16 = jnp.float32, jnp.bfloat16
+    half = chan // 8
+    count = chan // TILE
+
+    def shape(*dims):
+        return jax.ShapeDtypeStruct(dims, f32)
+
+    total = (half + 8 * half // 2 + mapper_half + chan // 2 + CHUNK + 8 * half // 2) // CHUNK
+    block = (pixels, chan)
+    return pl.pallas_call(
+        backward_body,
+        out_shape=[
+            shape(2, half, chan),
+            shape(2, half, 3 * chan),
+            shape(2, mapper_half, chan),
+            shape(2, chan // 2, chan),
+            shape(2, CHUNK, chan),
+            shape(2, half, 4 * chan),
+            shape(2, mapper_half, chan),
+            shape(2, chan // 2, chan),
+            shape(4, 2, half, chan),
+            shape(*block),
+            shape(4, slots, chan),
+            shape(*block),
+            shape(*block),
+        ],
+        in_specs=[ANY] * 16 + [pl.BlockSpec(memory_space=pltpu.VMEM)] * 3,
+        out_specs=[ANY] * 13,
+        scratch_shapes=stream_scratch(total, 4 * half // CHUNK, chan)
+        + [
+            pltpu.VMEM((3,) + block, f32),
+            pltpu.VMEM(block, f32),
+            pltpu.VMEM(block, f32),
+            pltpu.VMEM(block, f32),
+            pltpu.VMEM(block, f32),
+            pltpu.VMEM((3,) + block, f32),
+            pltpu.VMEM(block, f32),
+            pltpu.VMEM(block, f32),
+            pltpu.VMEM(small.shape, f32),
+            pltpu.VMEM((spots, chan), f32),
+            pltpu.VMEM((spots, chan), bf16),
+            pltpu.VMEM((spots, chan), bf16),
+            pltpu.VMEM((2, TILE, chan), f32),
+            pltpu.VMEM((2, spots, TILE), f32),
+            pltpu.VMEM((2, spots, TILE), f32),
+            pltpu.VMEM((2, spots, chan // 4), f32),
+            pltpu.VMEM((chan // 4, chan), f32),
+            pltpu.VMEM((2, spots, TILE), f32),
+            pltpu.VMEM((8, chan), f32),
+            pltpu.VMEM((8, 128), f32),
+            pltpu.VMEM((3, 8, 128), f32),
+            pltpu.VMEM((3, texts, chan), f32),
+            pltpu.VMEM((texts, chan), f32),
+            pltpu.VMEM((4, slots, chan), f32),
+            pltpu.VMEM((4, 16, chan), f32),
+            pltpu.VMEM((silu.shape[1], chan), f32),
+            DMA((9,)),
+            DMA((9,)),
+            DMA((12,)),
+            DMA((pixels // 8,)),
+            DMA((pixels // 8,)),
+            DMA((14,)),
+            DMA((count, 3)),
+            DMA((count, 3)),
+            DMA((3,)),
+            DMA((3,)),
+            DMA((pixels // 16, 3)),
+            DMA((pixels // 16, 3)),
+            DMA((6,)),
+            DMA((6,)),
+        ],
+        compiler_params=pltpu.CompilerParams(
+            collective_id=collective, has_side_effects=True, vmem_limit_bytes=62 * 2**20
+        ),
+        name="backward_sums",
+    )(
+        output_part, attend_part, two_share, text_share, cot, one, response, reduce_w, act, slope,
+        normed_all, expand_w, conv, out_share, base, small, rows, embed, silu,
+    )
+
+
+def close_body(grad_in, token_in, conv_in, grad_home, token_home, conv_all, hold, send, recv, keep):
+    core = lax.axis_index("cond")
+    level = lax.axis_index("pair")
+    me = lax.axis_index("dp")
+    up, over = home_spot(level, me)
+    back_up, back_over = plane_spot(level, me)
+    moves = jnp.logical_or(level != 0, me != 0)
+    others = [(c, s) for c in (0, 1) for s in (0, 1, 2, 3) if (c, s) != (0, 0)]
+
+    def other(c, s):
+        return (lax.rem(core + c, 2), lax.rem(level + s, 4), me)
+
+    for c, s in others:
+        greet(other(c, s))
+    pl.when(moves)(lambda: greet((core, back_up, back_over)))
+    pl.semaphore_wait(pltpu.get_barrier_semaphore(), 7 + jnp.where(moves, 1, 0))
+    swaps = ((grad_in, grad_home), (token_in, token_home))
+    aways = [remote(src, dst, send.at[i], recv.at[i], (core, up, over)) for i, (src, dst) in enumerate(swaps)]
+    spreads = [
+        remote(conv_in, conv_all.at[1 + i], send.at[2 + i], recv.at[2 + i], other(c, s))
+        for i, (c, s) in enumerate(others)
+    ]
+    mine = pltpu.make_async_copy(conv_in, conv_all.at[0], keep.at[2])
+    for copy in spreads + [mine]:
+        copy.start()
+    for away in aways:
+        pl.when(moves)(away.start)
+
+    @pl.when(jnp.logical_not(moves))
+    def _():
+        load = pltpu.make_async_copy(grad_in, hold, keep.at[0])
+        store = pltpu.make_async_copy(hold, grad_home, keep.at[0])
+        small = pltpu.make_async_copy(token_in, token_home, keep.at[1])
+        small.start()
+        load.start()
+        load.wait()
+        store.start()
+        store.wait()
+        small.wait()
+
+    for copy in spreads + [mine]:
+        copy.wait()
+    for away in aways:
+        pl.when(moves)(away.wait)
+
+
+def close_exchange(collective, grad, tokens, conv):
+    shapes = [grad.shape, tokens.shape, (8,) + conv.shape]
+    return pl.pallas_call(
+        close_body,
+        out_shape=[jax.ShapeDtypeStruct(shape, jnp.float32) for shape in shapes],
+        in_specs=[ANY] * 3,
+        out_specs=[ANY] * 3,
+        scratch_shapes=[pltpu.VMEM(grad.shape, jnp.float32), DMA((9,)), DMA((9,)), DMA((3,))],
+        compiler_params=pltpu.CompilerParams(collective_id=collective, has_side_effects=True),
+        name="close_exchange",
+    )(grad, tokens, conv)
 
 
 def plane_body(
@@ -373,26 +1882,14 @@
     size = lax.axis_size("dp")
     core = lax.axis_index("cond")
     me = lax.axis_index("dp")
+    level = lax.axis_index("pair")
+    quarter = home_spot(level, me)[0]
+    order = jnp.bitwise_xor(jnp.arange(4), me)
     _, rows, cols, chan = latents.shape
     pixels = rows * cols
     part = chan // size
     hid = size * expand_bias.shape[0]
     texts = clip_tokens.shape[1]
-    grid = [(z, d) for z in range(size) for d in range(size)]
-    swap_perm = [(z * size + d, d * size + z) for z, d in grid]
-    down_perm = [(z * size + d, d * size + z + 1) for z, d in grid if z + 1 < size]
-    up_perm = [(z * size + d, d * size + z - 1) for z, d in grid if z >= 1]
-
-    def swap(value, perm=swap_perm):
-        return lax.ppermute(value, ("pair", "dp"), perm)
-
-    image = swap(latents[0])
-    above = swap(latents[0, -1:], down_perm)
-    below = swap(latents[0, :1], up_perm)
-    embed = swap(ratio_embed)
-    tokens = swap(clip_tokens[0])
-    cot = swap(cotangent[0].reshape(pixels, chan))
-
     packed = jnp.concatenate(
         [
             conv_kernel.reshape(9, part),
@@ -404,7 +1901,13 @@
         ],
         axis=0,
     )
-    every = lax.all_gather(packed, "dp", axis=0)
+    row_padded, every, tokens, embed, expand_w, attend_units = open_exchange(
+        3, latents[0], packed, clip_tokens[0], ratio_embed, expand_weight, attend_weight
+    )[:6]
+    row_padded = row_padded.at[:1].set(jnp.where(quarter > 0, row_padded[:1], 0.0))
+    row_padded = row_padded.at[-1:].set(jnp.where(quarter < size - 1, row_padded[-1:], 0.0))
+    image = row_padded[1:-1]
+    expand_w = expand_w.reshape(chan, -1)
     channel_rows = every[:, :13].transpose(1, 0, 2).reshape(13, chan)
     kernel = channel_rows[:9].reshape(3, 3, chan)
     conv_shift, reduce_b, text_b, out_b = (channel_rows[9 + i] for i in range(4))
@@ -412,63 +1915,73 @@
 
     half = part // 2
     wide = hid // size
-    expand_w = to_both_cores(
-        lambda to, c: lax.dynamic_slice(expand_weight, (c * half, to * wide), (half, wide)), core, me
-    ).reshape(chan, wide)
-    attend_thirds = attend_weight.reshape(part, 3, chan)
-    attend_w = to_both_cores(
-        lambda to, c: lax.dynamic_slice(
-            attend_thirds, (c * half, 0, to * part), (half, 3, part)
-        ).reshape(half, 3 * part),
-        core,
-        me,
-    ).reshape(chan, 3 * part)
-
     text_part = text_weight.shape[0]
-    silu_tokens = jax.nn.silu(tokens)
     token_cols = [
-        lax.dynamic_slice(tokens, (0, (me ^ step) * text_part), (texts, text_part))
+        lax.dynamic_slice(tokens, (0, near_of(me, step) * text_part), (texts, text_part))
         for step in range(4)
     ]
-    near_tokens = jnp.concatenate(
-        [token_cols[0]] + [partners(token_cols[step], step) for step in (1, 2, 3)], axis=0
-    )
-    silu_near = jax.nn.silu(near_tokens)
-    mapped_share = dot(silu_near, text_weight)
-    mapped = scatter_near(jnp.split(mapped_share, 4, axis=0)) + text_b
-    mapped_all = jnp.concatenate(gather_near(mapped), axis=0)
     ratio_part = ratio_weight.shape[0]
     embed_part = lax.dynamic_slice(embed, (0, me * ratio_part), (1, ratio_part))
-    modulation = (
-        lax.psum(jnp.dot(embed_part, ratio_weight, precision=HIGHEST_ACCURACY), "dp")[0] + ratio_b
-    )
-    mod_scale = 1.0 + modulation[:chan]
-    mod_shift = modulation[chan:]
-
-    row_padded = jnp.concatenate([above, image, below], axis=0)
+    mod_part = jnp.dot(embed_part, ratio_weight, precision=HIGHEST_ACCURACY)
+
     padded = jnp.pad(row_padded, ((0, 0), (1, 1), (0, 0)))
     total_conv = conv_shift
     for i in range(3):
         for j in range(3):
             total_conv = total_conv + padded[i : i + rows, j : j + cols] * kernel[i, j]
     normed, inverse = norm_stats(total_conv.reshape(pixels, chan))
-    normed_all = jnp.concatenate(gather_near(normed), axis=0)
+    normed_all, mod_near, near_tokens, attend_w = exchange(
+        4,
+        gathers=(normed, mod_part),
+        scatters=(jnp.stack(token_cols),),
+        relay=(attend_units,),
+    )
+    attend_w = attend_w.reshape(chan, 3 * part)
+    modulation = jnp.sum(mod_near[:, 0], axis=0) + ratio_b
+    mod_scale = 1.0 + modulation[:chan]
+    mod_shift = modulation[chan:]
+    normed_all = normed_all.reshape(size * pixels, chan)
+    cot, normed_all = lax.optimization_barrier((cotangent[0].reshape(pixels, chan), normed_all))
+    turns = (0, 2, 1, 3)
+    grid = [(z, d) for z in range(size) for d in range(size)]
+    cot = lax.ppermute(
+        cot, ("pair", "dp"), [(z * size + d, z * size + (d ^ turns[z])) for z, d in grid]
+    )
+    near_tokens = jnp.concatenate([token_cols[0], near_tokens.reshape(-1, text_part)], axis=0)
+    silu_near = jax.nn.silu(near_tokens)
+    mapped_share = dot(silu_near, text_weight).reshape(4, texts, chan)
     hidden = dot(normed_all, expand_w) + expand_bias
     bell = 0.5 * (1.0 + lax.erf(hidden * 0.5**0.5))
     activated = hidden * bell
+    density = jnp.exp(-0.5 * hidden * hidden) * (2.0 * jnp.pi) ** -0.5
+    slope = bell + hidden * density
     totals = jnp.sum(activated * activated, axis=0)
     norms = jnp.sqrt(totals + EPSILON)
-    middle = lax.psum(jnp.sum(norms), "dp") / hid + EPSILON
+    norm_sums = exchange(5, gathers=(jnp.full((8, 128), jnp.sum(norms)),))[0]
+    middle = jnp.sum(norm_sums[:, 0, 0]) / hid + EPSILON
     scaled = norms / middle
     factor = 1.0 + response_gain * scaled
     response = activated * factor + response_bias
-    one_share = dot(response, reduce_weight)
-    hidden_one = (
-        scatter_near(jnp.split(one_share, 4, axis=0)) + image.reshape(pixels, chan) + reduce_b
-    )
+    one_share = dot(response, reduce_weight).reshape(4, pixels, chan)
+    cot, one_share = lax.optimization_barrier((cot, one_share))
+    cot = lax.ppermute(
+        cot, ("pair", "dp"), [(z * size + d, (d ^ turns[z]) * size + d) for z, d in grid]
+    )
+    one_arrived, mapped_arrived = exchange(6, scatters=(one_share, mapped_share))
+    mapped = mapped_share[0] + jnp.sum(mapped_arrived, axis=0) + text_b
+    hidden_one = one_share[0] + jnp.sum(one_arrived, axis=0) + image.reshape(pixels, chan) + reduce_b
     hidden_two = hidden_one * mod_scale + mod_shift
     normed_two, inverse_two = norm_stats(hidden_two)
-    normed_two_all = jnp.concatenate(gather_near(normed_two), axis=0)
+    cot, normed_two = lax.optimization_barrier((cot, normed_two))
+    normed_two_all, mapped_all = exchange(7, gathers=(normed_two, mapped))
+    cot, normed_two_all = lax.optimization_barrier((cot, normed_two_all))
+    cot_all = jnp.concatenate(
+        [cot]
+        + [lax.ppermute(cot, "dp", [(i, i ^ step) for i in range(size)]) for step in (1, 2, 3)],
+        axis=0,
+    )
+    normed_two_all = normed_two_all.reshape(size * pixels, chan)
+    mapped_all = mapped_all.reshape(size * texts, chan)
 
     source = jnp.concatenate([normed_two_all, mapped_all], axis=0)
     query = dot(normed_two_all, attend_w[:, :part]) + query_bias
@@ -481,11 +1994,9 @@
     probs = expo / jnp.sum(expo, axis=-1, keepdims=True)
     mixture_h = jnp.einsum("uio,ouy->iuy", probs, value_h, precision=FAST)
     mixture = mixture_h.reshape(query.shape)
-    out_share = dot(mixture, output_weight)
-    plane_out = scatter_near(jnp.split(out_share, 4, axis=0)) + hidden_two + out_b
-    layer_output = swap(plane_out).reshape(latents.shape)
-
-    cot_all = jnp.concatenate(gather_near(cot), axis=0)
+    out_share = dot(mixture, output_weight).reshape(4, pixels, chan)
+    out_base = hidden_two + out_b
+
     output_grad = t_dot(mixture, cot_all)
     grad_mix_h = heads_of(dot_t(cot_all, output_weight))
     grad_probs = jnp.einsum("iuy,ouy->uio", grad_mix_h, value_h, precision=FAST)
@@ -497,42 +2008,87 @@
     spots = size * pixels
     grad_kv = jnp.concatenate([grad_key, grad_value], axis=1)
     grad_qkv = jnp.concatenate([grad_query, grad_kv[:spots]], axis=1)
-    two_share = dot_t(grad_qkv, attend_w)
-    text_share = dot_t(grad_kv[spots:], attend_w[:, part:])
-    grad_normed_two = scatter_near(jnp.split(two_share, 4, axis=0))
-    grad_mapped = scatter_near(jnp.split(text_share, 4, axis=0))
+    two_share = dot_t(grad_qkv, attend_w).reshape(4, pixels, chan)
+    text_share = dot_t(grad_kv[spots:], attend_w[:, part:]).reshape(4, texts, chan)
     attend_grad = t_dot(normed_two_all, grad_qkv)
     attend_grad = attend_grad.at[:, part:].add(t_dot(mapped_all, grad_kv[spots:]))
-    grad_two = cot + norm_back(grad_normed_two, normed_two, inverse_two)
-    grad_one = grad_two * mod_scale
-    grad_one_all = jnp.concatenate(gather_near(grad_one), axis=0)
-    grad_mapped_all = jnp.concatenate(gather_near(grad_mapped), axis=0)
-    mapper_grad = t_dot(silu_near, grad_mapped_all)
+    def row(value):
+        return jnp.sum(value, axis=0, keepdims=True)
+
+    def mine(value):
+        width = value.shape[1] // size
+        return lax.dynamic_slice(value, (0, me * width), (value.shape[0], width))
+
+    gap = jnp.zeros((1, part), jnp.float32)
+    small_rows = jnp.concatenate(
+        [
+            jnp.zeros((3, chan), jnp.float32),
+            jnp.concatenate([gap, gap, row(grad_query), row(grad_value)], axis=1),
+            jnp.concatenate([row(mine(cot_all)), gap, gap, gap], axis=1),
+            jnp.zeros((CHUNK - 5, chan), jnp.float32),
+        ],
+        axis=0,
+    )
+    one_row = jnp.full((1, chan), 1.0, jnp.float32)
+    back_rows = jnp.concatenate(
+        [
+            response_gain[None],
+            norms[None],
+            factor[None],
+            one_row / middle,
+            one_row / hid,
+            scaled[None],
+            mod_scale[None],
+            mod_shift[None],
+        ],
+        axis=0,
+    )
+    slots = (texts + 7) // 8 * 8
+    silu_padded = jnp.pad(
+        silu_near.reshape(4, texts, text_part), ((0, 0), (0, slots - texts), (0, -text_part % 128))
+    ).reshape(4 * slots, -1)
+    embed_rows = jnp.broadcast_to(
+        embed_part.reshape(ratio_part, 1, 1), (ratio_part, 2, 128)
+    ).reshape(2 * ratio_part, 128)
+    (
+        output_sum, attend_sum, mapper_sum, reduce_sum, small, expand_sum, _, _, _,
+        grad_one, grad_mapped_all, grad_conv, layer_output,
+    ) = backward_sums(
+        1,
+        output_grad.reshape(2, half, chan),
+        attend_grad.reshape(size, 2, half, 3 * part),
+        two_share,
+        text_share,
+        cot,
+        hidden_one,
+        response,
+        reduce_weight,
+        activated,
+        slope,
+        normed_all,
+        expand_w,
+        total_conv.reshape(pixels, chan),
+        out_share,
+        out_base,
+        jnp.stack([jnp.zeros((CHUNK, chan), jnp.float32), small_rows]),
+        back_rows,
+        embed_rows,
+        silu_padded,
+        text_part // 2,
+    )
+    output_sum = output_sum.reshape(part, chan)
+    attend_sum = attend_sum.reshape(part, 3 * chan)
+    mapper_sum = mapper_sum.reshape(text_part, chan)
+    reduce_sum = reduce_sum.reshape(wide, chan)
+    expand_sum = expand_sum.reshape(part, hid)
+    layer_output = layer_output.reshape(latents.shape)
+    grad_mapped_all = grad_mapped_all[:, :texts].reshape(size * texts, chan)
     gate = 1.0 / (1.0 + jnp.exp(-near_tokens))
     tokens_near = dot_t(grad_mapped_all, text_weight) * (
         gate * (1.0 + near_tokens * (1.0 - gate))
     )
-    token_blocks = exchange_near(jnp.split(tokens_near, 4, axis=0), me)
-    tokens_grad = swap(token_blocks.transpose(1, 0, 2).reshape(texts, size * text_part))[None]
-    ratio_sums = lax.psum(
-        jnp.concatenate([jnp.sum(grad_two * hidden_one, axis=0), jnp.sum(grad_two, axis=0)]), "dp"
-    )
-    ratio_grad = embed_part.reshape(ratio_part, 1) * ratio_sums
-
-    reduce_grad = t_dot(response, grad_one_all)
-    grad_response = dot_t(grad_one_all, reduce_weight)
-    gain_sum = jnp.sum(grad_response * activated, axis=0)
-    grad_scaled = gain_sum * response_gain
-    spread = lax.psum(jnp.sum(grad_scaled * norms), "dp") / hid
-    grad_norms = grad_scaled / middle - spread / (middle * middle)
-    grad_totals = grad_norms / (2.0 * norms)
-    grad_activated = grad_response * factor + 2.0 * activated * grad_totals
-    density = jnp.exp(-0.5 * hidden * hidden) * (2.0 * jnp.pi) ** -0.5
-    grad_hidden = grad_activated * (bell + hidden * density)
-    expand_grad = t_dot(normed_all, grad_hidden)
-    front_share = dot_t(grad_hidden, expand_w)
-    grad_normed = scatter_near(jnp.split(front_share, 4, axis=0))
-    grad_conv = norm_back(grad_normed, normed, inverse).reshape(rows, cols, chan)
+    tokens_near = tokens_near.reshape(4, texts, text_part)
+    grad_conv = grad_conv.reshape(rows, cols, chan)
     kernel_grad = jnp.stack(
         [
             jnp.sum(padded[i : i + rows, j : j + cols] * grad_conv, axis=(0, 1))
@@ -548,71 +2104,41 @@
                 latent_rows
                 + spread_conv[2 - i : 2 - i + rows + 2, 2 - j : 2 - j + cols] * kernel[i, j]
             )
-    inner = swap(latent_rows[1:-1] + grad_one.reshape(rows, cols, chan))
-    back_up = [(d * size + z, (z - 1) * size + d) for z, d in grid if z >= 1]
-    back_down = [(d * size + z, (z + 1) * size + d) for z, d in grid if z + 1 < size]
-    from_below = swap(latent_rows[:1], back_up)
-    from_above = swap(latent_rows[-1:], back_down)
-    latent_grad = inner.at[-1:].add(from_below).at[:1].add(from_above)[None]
-
-    def over_planes(value, axis):
-        count = value.shape[axis] // 2
-        low = lax.slice_in_dim(value, 0, count, axis=axis)
-        high = lax.slice_in_dim(value, count, None, axis=axis)
-        kept = jnp.where(core == 0, low, high) + other_core(jnp.where(core == 0, high, low))
-        return kept
-
-    def from_both(value, axis):
-        other = other_core(value)
-        return jnp.concatenate(
-            [jnp.where(core == 0, value, other), jnp.where(core == 0, other, value)], axis=axis
-        )
-
-    def columns_home(value):
-        kept = over_planes(value.reshape(size, part, value.shape[1]), 1)
-        blocks = [
-            lax.dynamic_slice(kept, (me ^ step, 0, 0), (1,) + kept.shape[1:])[0]
+    conv_part = jnp.concatenate([kernel_grad, jnp.sum(grad_conv, axis=(0, 1))[None]], axis=0)
+    conv_blocks = jnp.stack(
+        [
+            lax.dynamic_slice(conv_part, (0, near_of(me, step) * part), (10, part))
             for step in range(4)
         ]
-        return exchange_near(blocks, me)
-
-    output_sum = from_both(lax.psum(over_planes(output_grad, 0), "pair"), 0)
-    attend_home = columns_home(attend_grad)
-    attend_home = attend_home.reshape(size, half, 3, part).transpose(1, 2, 0, 3)
-    attend_sum = from_both(lax.psum(attend_home.reshape(half, 3 * chan), "pair"), 0)
-    mapper_sum = from_both(lax.psum(over_planes(mapper_grad, 0), "pair"), 0)
-    reduce_sum = from_both(lax.psum(over_planes(reduce_grad, 0), "pair"), 0)
-    expand_home = columns_home(expand_grad).transpose(1, 0, 2).reshape(half, hid)
-    expand_sum = from_both(lax.psum(expand_home, "pair"), 0)
-
-    def mine(value):
-        return lax.dynamic_slice(value, (me * (value.shape[0] // size),), (value.shape[0] // size,))
-
-    small = (
-        jnp.sum(grad_hidden, axis=0),
-        scaled * gain_sum,
-        jnp.sum(grad_response, axis=0),
-        mine(jnp.sum(grad_one_all, axis=0)),
-        mine(jnp.sum(grad_mapped_all, axis=0)),
-        jnp.sum(grad_query, axis=0),
-        jnp.sum(grad_value, axis=0),
-        mine(jnp.sum(cot_all, axis=0)),
-        mine(ratio_sums),
-        ratio_grad.reshape(-1),
-    )
-    lengths = [item.shape[0] for item in small]
-    small_sum = lax.psum(jnp.concatenate(small), ("cond", "pair"))
-    ends = []
-    position = 0
-    for length in lengths:
-        ends.append(small_sum[position : position + length])
-        position += length
-    expb, gain, respb, redb, mapb, queryb, valueb, outb, ratiob, ratio = ends
-    conv_sum = lax.psum(
-        jnp.concatenate([kernel_grad, jnp.sum(grad_conv, axis=(0, 1))[None]], axis=0),
-        ("cond", "pair", "dp"),
-    )
-    conv_mine = lax.dynamic_slice(conv_sum, (0, me * part), (10, part))
+    )
+    rims, conv_arrived, token_arrived = exchange(
+        13,
+        gathers=(jnp.stack([latent_rows[0], latent_rows[-1]]),),
+        scatters=(conv_blocks, tokens_near),
+    )
+    token_blocks = jnp.take(
+        jnp.concatenate([tokens_near[:1], token_arrived], axis=0), order, axis=0
+    )
+    prior = near_of(rev(quarter), rev(jnp.maximum(quarter - 1, 0)))
+    after = near_of(rev(quarter), rev(jnp.minimum(quarter + 1, size - 1)))
+    from_above = jnp.where(quarter > 0, rims[prior, 1], 0.0)
+    from_below = jnp.where(quarter < size - 1, rims[after, 0], 0.0)
+    inner = latent_rows[1:-1] + grad_one.reshape(rows, cols, chan)
+    inner = inner.at[-1].add(from_below).at[0].add(from_above)
+    latent_grad, tokens_grad, conv_all = close_exchange(
+        14,
+        inner.reshape(pixels, chan),
+        token_blocks.transpose(1, 0, 2).reshape(texts, size * text_part),
+        conv_blocks[0] + jnp.sum(conv_arrived, axis=0),
+    )
+    latent_grad = latent_grad.reshape(latents.shape)
+    tokens_grad = tokens_grad[None]
+    conv_mine = jnp.sum(conv_all, axis=0)
+    ratio = small[0]
+    expb, gain, respb = (small[1, i] for i in range(3))
+    redb, mapb, queryb, valueb = (small[1, 3, i * part : (i + 1) * part] for i in range(4))
+    outb = small[1, 4, :part]
+    ratiob = small[1, 4, part : 3 * part]
     return (
         layer_output,
         latent_grad,

time: 1710 us -> 1070 us (0.63)
  waiting for transfers between devices: 858 us -> 20.8 us
  Pallas kernels: 0 us -> 757 us
  starting transfers between devices: 176 us -> 18.6 us
  blocking collectives: 129 us -> 0 us
  other arithmetic: 176 us -> 48.1 us
  local copies, waits for them, and re-layouts: 150 us -> 88.2 us
  matrix products: 191 us -> 132 us
    pallas_call x0 -> x8, Pallas kernels: none -> 757 us  [the longest x1 447 us: backward_sums(): pl.pallas_call(backward_body, out_shape=[shape(2, half, chan), shape(2, h...]
    psum x2 -> x0, waiting for transfers between devices: 485 us -> none  [the longest x1 485 us: plane_body(): expand_sum = from_both(lax.psum(expand_home, 'pair'), 0)]
    ppermute x77 -> x5, waiting for transfers between devices: 373 us -> 20.8 us  [the longest x1 16 us: plane_body(): lax.ppermute(cot, ('pair', 'dp'), [(z * size + d, (d ^ turns[z]) * size +...]
    ppermute x77 -> x5, starting transfers between devices: 176 us -> 18.6 us  [the longest x1 12.7 us: plane_body(): lax.ppermute(cot, ('pair', 'dp'), [(z * size + d, (d ^ turns[z]) * size +...]
    psum x3 -> x0, blocking collectives: 77.8 us -> none  [the longest x1 43 us: plane_body(): lax.psum(jnp.concatenate([kernel_grad, jnp.sum(grad_conv, axis=(0, 1))[No...]
    all_gather x1 -> x0, blocking collectives: 51.6 us -> none  [plane_body(): every = lax.all_gather(packed, 'dp', axis=0)]
    select_n x18 -> x2, other arithmetic: 51.3 us -> 0.09 us  [plane_body(): jnp.take(jnp.concatenate([tokens_near[:1], token_arrived], axis=0), order...]
    concatenate x9 -> x2, other arithmetic: 33 us -> 0.03 us  [the longest x1 0.02 us: plane_body(): jnp.concatenate([token_cols[0], near_tokens.reshape(-1, text_part)], axis=0)]
  transfers between devices with their start and end apart: 79 -> 5, of which waited for: 24 -> 2; matrix products, arithmetic and copies ran while one was open for 21% -> 7% of each run, Pallas kernels for 0% -> 0%
where the time goes in v2:
time: 1070 us
  Pallas kernels  757 us (71%)
  matrix products  132 us (12%)
  local copies, waits for them, and re-layouts  88.2 us (8%)
  other arithmetic  48.1 us (4%)
  waiting for transfers between devices  20.8 us (2%)
  starting transfers between devices  18.6 us (2%)
    pallas_call x1, Pallas kernels, backward_sums(): pl.pallas_call(backward_body, out_shape=[shape(2, half, chan), shape(2, h...  447 us
    pallas_call x5, Pallas kernels, exchange(): pl.pallas_call(functools.partial(exchange_body, len(gathers), len(scatter...  195 us
    pallas_call x1, Pallas kernels, open_exchange(): pl.pallas_call(open_body, out_shape=[jax.ShapeDtypeStruct(shape, jnp.floa...  75.2 us
    unnamed x136, local copies, waits for them, and re-layouts  48.7 us
    dot_general x6, matrix products, dot(): return jnp.dot(left, right, precision=FAST)  47.9 us
    pallas_call x1, Pallas kernels, close_exchange(): pl.pallas_call(close_body, out_shape=[jax.ShapeDtypeStruct(shape, jnp.flo...  39.3 us
    dot_general x3, matrix products, t_dot(): lax.dot_general(left, right, (((0,), (0,)), ((), ())), precision=FAST)  31 us
  transfers between devices with their start and end apart: 5, of which 2 were waited for; matrix products, arithmetic and copies ran while one was open for 7% of the time, Pallas kernels for 0%

profile of v2, /device:TPU:16, one launch (start us, length us, event | category | flops | bytes accessed | tf_op | source)
XLA Modules:
  0.0 1067.5 jit_solution(512824659589319954)
XLA Ops:
  8.5 75.2 %open_exchange.1 = (f32[8,24,1536]{2,1,0:T(8,128)}, f32[4,15,384]{2,1,0:T(8,128)}, f32[19,1280]{1,0:T(8,128)}, f32[1,64]{1,0:T(1,128)}, f32[4,4,96,1536]{3,2,1,0...) custom-call(f32[6,24,1536]{2,1,0:T(8,128)} %bitcast.189, ...), custom_call_target="tpu_custom_call" | custom-call | tf_op jit(solution)/shard_map/open_exchange/pallas_call | solution.py:730
  88.2 5.5 fusion.79
  99.4 65.1 %exchange.5 = (f32[4,144,1536]{2,1,0:T(8,128)S(1)}, f32[4,1,3072]{2,1,0:T(1,128)S(1)}, f32[3,19,320]{2,1,0:T(8,128)S(1)}, f32[4,384,1152]{2,1,0:T(8,128)S(1)}) custom-call(f32[144,1536]{1,0:T(8,128)S(1)} %subtract_multiply_fusion.1.refs_0_, f32[1,3072]{1,0:T(1,128)S(1)} %fusion.63.refs_1_, ...), custom_call_target="tpu_custom_call", output_to_operand_aliasing={{3}: (3, {})} | custom-call | tf_op jit(solution)/shard_map/exchange/pallas_call | solution.py:500
  170.7 14.3 %multiply_reduce_fusion.1 = (f32[1536]{0:T(1024)S(1)}, f32[576,1536]{1,0:T(8,128)}, f32[576,1536]{1,0:T(8,128)}) fusion(f32[1536]{0:T(1024)S(1)} %copy-done.56, f32[576,1536]{1,0:T(8,128)S(1)} %bitcast.149, f32[1536,1536]{1,0:T(8,128)} %bitcast.160), kind=kOutput, calls=%fused_computation.32 | convolution fusion | flops 8164342272 | bytes 20066304 | tf_op jit(solution)/shard_map/dot_general | solution.py:291
  186.2 5.2 exchange.6
  197.3 4.2 multiply_add_fusion.response_ref
  202.2 12.6 %fusion.82 = f32[576,1536]{1,0:T(8,128)S(1)} fusion(f32[576,1536]{1,0:T(8,128)} %multiply_add_fusion.response_ref, f32[1536,1536]{1,0:T(8,128)} %reduce_w_ref.1), kind=kOutput, calls=%fused_computation.198 | convolution fusion | flops 8153726976 | bytes 16515072 | tf_op jit(solution)/shard_map/dot_general | solution.py:291
  215.8 45.9 %exchange.7 = (f32[3,144,1536]{2,1,0:T(8,128)S(1)}, f32[3,19,1536]{2,1,0:T(8,128)S(1)}) custom-call(f32[4,144,1536]{2,1,0:T(8,128)S(1)} %bitcast.147, f32[4,19,1536]{2,1,0:T(8,128)S(1)} %reshape.509.refs_1_), custom_call_target="tpu_custom_call" | custom-call | tf_op jit(solution)/shard_map/exchange/pallas_call | solution.py:500
  272.6 12.7 %collective-permute-start.1 = (f32[144,1536]{1,0:T(8,128)}, f32[144,1536]{1,0:T(8,128)}, u32[]{:S(2)}, u32[]{:S(2)}) collective-permute-start(f32[144,1536]{1,0:T(8,128)} %collective-permute-done), channel_id=1, source_target_pairs={{0,0},{1,5},{2,10},{3,15},{4,8},{5,13},{6,2},{7,7},{8,4},{9,1},{10... | collective-permute-start | bytes 2654216 | tf_op jit(solution)/shard_map/ppermute | solution.py:1967
  289.4 16.0 %collective-permute-done.1.cot_ref = f32[144,1536]{1,0:T(8,128)} collective-permute-done((f32[144,1536]{1,0:T(8,128)}, f32[144,1536]{1,0:T(8,128)}, u32[]{:S(2)}, u32[]{:S(2)}) %collective-permute-start.1) | collective-permute-done | bytes 884768 | tf_op jit(solution)/shard_map/ppermute | solution.py:1967
  305.4 53.9 %exchange.8 = (f32[4,144,1536]{2,1,0:T(8,128)S(1)}, f32[4,19,1536]{2,1,0:T(8,128)S(1)}) custom-call(f32[144,1536]{1,0:T(8,128)S(1)} %subtract_multiply_fusion.refs_0_, f32[19,1536]{1,0:T(8,128)S(1)} %fusion.57.refs_1_), custom_call_target="tpu_custom_call" | custom-call | tf_op jit(solution)/shard_map/exchange/pallas_call | solution.py:500
  362.9 4.6 fusion.30
  368.9 8.7 fusion.5
  380.7 5.8 multiply_reduce_fusion
  395.5 4.8 collective-permute-done.3
  408.1 5.9 bitcast_reduce_fusion
  414.0 5.6 multiply_reduce_fusion.2
  419.6 6.6 multiply_multiply_fusion
  426.3 4.7 bitcast_reduce_fusion.1
  431.0 5.1 fusion.84
  440.0 4.7 fusion.3
  452.5 19.8 %fusion.16 = f32[1536,1152]{1,0:T(8,128)} fusion(f32[576,1536]{1,0:T(8,128)} %bitcast.145, f32[576,768]{0,1:T(8,128)} %fusion.28, f32[576,384]{0,1:T(8,128)S(1)} %bitcast.176), kind=kOutput, calls=%fused_computation.35 | convolution fusion | flops 6115958784 | bytes 13271040 | tf_op jit(solution)/shard_map/dot_general | solution.py:299
  472.3 6.6 fusion.2
  481.8 6.8 fusion.26.out_ref
  488.6 4.6 fusion.14.output_ref
  493.3 10.8 %fusion.20.two_ref = f32[4,144,1536]{2,1,0:T(8,128)} fusion(f32[1536,1152,1]{1,0,2:T(8,128)} %bitcast.142, f32[4,144,768]{2,1,0:T(8,128)S(1)} %bitcast.180, f32[4,144,384]{2,1,0:T(8,128)S(1)} %copy-done.31), kind=kOutput, calls=%fused_computation.39 | convolution fusion | flops 6115958784 | bytes 13271040 | tf_op jit(solution)/shard_map/dot_general | solution.py:295
  504.7 447.2 %backward_sums.1 = (f32[2,192,1536]{2,1,0:T(8,128)}, f32[2,192,4608]{2,1,0:T(8,128)}, f32[2,160,1536]{2,1,0:T(8,128)}, f32[2,768,1536]{2,1,0:T(8,128)}, f32[2,32...) custom-call(f32[2,192,1536]{2,1,0:T(8,128)} %fusion.14.output_ref, ...), custom_call_target="tpu_custom_call" | custom-call | tf_op jit(solution)/shard_map/backward_sums/pallas_call | solution.py:1728
  953.2 5.6 multiply_reduce_fusion.3
  966.0 24.8 %exchange.9 = (f32[4,2,24,1536]{3,2,1,0:T(8,128)S(1)}, f32[3,10,384]{2,1,0:T(8,128)S(1)}, f32[3,19,320]{2,1,0:T(8,128)S(1)}) custom-call(f32[2,24,1536]{2,1,0:T(8,128)S(1)} %pad_maximum_fusion.1.refs_0_, f32[4,10,384]{2,1,0:T(8,128)S(1)} %pad_maximum_fusion.5.refs_1_, f32[4,19,320]{2,1,0:T(8,128)S(1)} %reshape.530.refs_2_), custom_call_target="tpu_custom_call" | custom-call | tf_op jit(solution)/shard_map/exchange/pallas_call | solution.py:500
  998.5 39.3 %close_exchange.1 = (f32[144,1536]{1,0:T(8,128)}, f32[19,1280]{1,0:T(8,128)}, f32[8,10,384]{2,1,0:T(8,128)}) custom-call(f32[144,1536]{1,0:T(8,128)} %bitcast.170, f32[19,1280]{1,0:T(8,128)} %reshape.532.token_in, f32[10,384]{1,0:T(8,128)} %dynamic-slice_add_fusion.conv_in), custom_call_target="tpu_custom_call" | custom-call | tf_op jit(solution)/shard_map/close_exchange/pallas_call | solution.py:1848
  1046.7 8.6 copy.88
  1055.4 4.2 copy.89
  (279 shorter events, 119.3 us)
Async XLA Ops:
  0.7 193.6 %copy-start = (f32[320,1536]{1,0:T(8,128)S(1)}, f32[320,1536]{1,0:T(8,128)}, u32[]{:S(2)}) copy-start(f32[320,1536]{1,0:T(8,128)} %param.45) | copy-start | bytes 5898244
  84.9 10.9 %copy-start.35 = (f32[1536]{0:T(1024)}, f32[1536]{0:T(1024)S(1)}, u32[]{:S(2)}) copy-start(f32[1536]{0:T(1024)S(1)} %get-tuple-element.219) | copy-start | bytes 18436
  84.9 10.9 %copy-start.37 = (f32[1536]{0:T(1024)}, f32[1536]{0:T(1024)S(1)}, u32[]{:S(2)}) copy-start(f32[1536]{0:T(1024)S(1)} %get-tuple-element.220) | copy-start | bytes 18436
  84.9 10.9 %copy-start.39 = (f32[1536]{0:T(1024)}, f32[1536]{0:T(1024)S(1)}, u32[]{:S(2)}) copy-start(f32[1536]{0:T(1024)S(1)} %get-tuple-element.221) | copy-start | bytes 18436
  84.9 10.9 %copy-start.41 = (f32[1536]{0:T(1024)}, f32[1536]{0:T(1024)S(1)}, u32[]{:S(2)}) copy-start(f32[1536]{0:T(1024)S(1)} %get-tuple-element.222) | copy-start | bytes 18436
  85.0 10.9 %copy-start.43 = (f32[1536]{0:T(1024)}, f32[1536]{0:T(1024)S(1)}, u32[]{:S(2)}) copy-start(f32[1536]{0:T(1024)S(1)} %get-tuple-element.223) | copy-start | bytes 18436
  85.0 10.9 %copy-start.45 = (f32[1536]{0:T(1024)}, f32[1536]{0:T(1024)S(1)}, u32[]{:S(2)}) copy-start(f32[1536]{0:T(1024)S(1)} %get-tuple-element.224) | copy-start | bytes 18436
  85.0 10.9 %copy-start.47 = (f32[1536]{0:T(1024)}, f32[1536]{0:T(1024)S(1)}, u32[]{:S(2)}) copy-start(f32[1536]{0:T(1024)S(1)} %get-tuple-element.225) | copy-start | bytes 18436
  99.4 71.2 %copy-start.56 = (f32[1536]{0:T(1024)S(1)}, f32[1536]{0:T(1024)}, u32[]{:S(2)}) copy-start(f32[1536]{0:T(1024)} %param.38) | copy-start | bytes 18436
  167.4 17.5 %copy-start.5 = (f32[4,144,1536]{2,1,0:T(8,128)}, f32[4,144,1536]{2,1,0:T(8,128)S(1)}, u32[]{:S(2)}) copy-start(f32[4,144,1536]{2,1,0:T(8,128)S(1)} %get-tuple-element.123) | copy-start | bytes 10616836
  167.5 47.4 %collective-permute-start = (f32[144,1536]{1,0:T(8,128)}, f32[144,1536]{1,0:T(8,128)}, u32[]{:S(2)}, u32[]{:S(2)}) collective-permute-start(f32[144,1536]{1,0:T(8,128)} %bitcast), channel_id=1, source_target_pairs={{0,0},{1,1},{2,2},{3,3},{4,6},{5,7},{6,4},{7,5},{8,9},{9,8},{10,11... | collective-permute-start | bytes 2654216 | tf_op jit(solution)/shard_map/ppermute | solution.py:1947
  170.6 22.1 %copy-start.49 = (f32[1536]{0:T(1024)S(1)}, f32[1536]{0:T(1024)}, u32[]{:S(2)}) copy-start(f32[1536]{0:T(1024)} %param.39) | copy-start | bytes 18436
  185.0 12.3 %copy-start.50 = (f32[1536]{0:T(1024)S(1)}, f32[1536]{0:T(1024)}, u32[]{:S(2)}) copy-start(f32[1536]{0:T(1024)} %param.40) | copy-start | bytes 18436
  272.6 32.8 %collective-permute-start.1 = (f32[144,1536]{1,0:T(8,128)}, f32[144,1536]{1,0:T(8,128)}, u32[]{:S(2)}, u32[]{:S(2)}) collective-permute-start(f32[144,1536]{1,0:T(8,128)} %collective-permute-done), channel_id=1, source_target_pairs={{0,0},{1,5},{2,10},{3,15},{4,8},{5,13},{6,2},{7,7},{8,4},{9,1},{10... | collective-permute-start | bytes 2654216 | tf_op jit(solution)/shard_map/ppermute | solution.py:1967
  285.3 77.6 %copy-start.52 = (f32[384]{0:T(512)S(1)}, f32[384]{0:T(512)}, u32[]{:S(2)}) copy-start(f32[384]{0:T(512)} %param.48) | copy-start | bytes 4612
  288.2 71.2 %copy-start.16 = (f32[144,1536]{1,0:T(8,128)}, f32[144,1536]{1,0:T(8,128)S(1)}, u32[]{:S(2)}) copy-start(f32[144,1536]{1,0:T(8,128)S(1)} %get-tuple-element.227.one_ref) | copy-start | bytes 2654212
  359.4 34.9 %collective-permute-start.2 = (f32[144,1536]{1,0:T(8,128)}, f32[144,1536]{1,0:T(8,128)}, u32[]{:S(2)}, u32[]{:S(2)}) collective-permute-start(f32[144,1536]{1,0:T(8,128)} %collective-permute-done.1.cot_ref), channel_id=1, source_target_pairs={{0,1},{1,0},{2,3},{3,2},{4,5},{5,4},{6,7},{7,6},{8,9},{9,8},{10,11... | collective-permute-start | bytes 2654216 | tf_op jit(solution)/shard_map/ppermute | solution.py:1980
  360.0 40.3 %collective-permute-start.3 = (f32[144,1536]{1,0:T(8,128)}, f32[144,1536]{1,0:T(8,128)}, u32[]{:S(2)}, u32[]{:S(2)}) collective-permute-start(f32[144,1536]{1,0:T(8,128)} %collective-permute-done.1.cot_ref), channel_id=1, source_target_pairs={{0,2},{1,3},{2,0},{3,1},{4,6},{5,7},{6,4},{7,5},{8,10},{9,11},{10,... | collective-permute-start | bytes 2654216 | tf_op jit(solution)/shard_map/ppermute | solution.py:1980
  361.4 40.2 %collective-permute-start.4 = (f32[144,1536]{1,0:T(8,128)}, f32[144,1536]{1,0:T(8,128)}, u32[]{:S(2)}, u32[]{:S(2)}) collective-permute-start(f32[144,1536]{1,0:T(8,128)} %collective-permute-done.1.cot_ref), channel_id=1, source_target_pairs={{0,3},{1,2},{2,1},{3,0},{4,7},{5,6},{6,5},{7,4},{8,11},{9,10},{10,... | collective-permute-start | bytes 2654216 | tf_op jit(solution)/shard_map/ppermute | solution.py:1980
  368.9 8.7 copy-start.19
  368.9 8.7 copy-start.51
  392.9 12.2 %copy-start.14 = (f32[384,1536]{1,0:T(8,128)S(1)}, f32[384,1536]{1,0:T(8,128)}, u32[]{:S(2)}) copy-start(f32[384,1536]{1,0:T(8,128)} %param.50) | copy-start | bytes 7077892
  436.3 8.4 copy-start.23
  452.4 19.8 %copy-start.20 = (f32[76,1536]{1,0:T(8,128)S(1)}, f32[76,1536]{1,0:T(8,128)}, u32[]{:S(2)}) copy-start(f32[76,1536]{1,0:T(8,128)} %copy-done.19) | copy-start | bytes 1400836
  452.4 19.8 %copy-start.24 = (f32[76,768]{0,1:T(8,128)S(1)}, f32[76,768]{0,1:T(8,128)}, u32[]{:S(2)}) copy-start(f32[76,768]{0,1:T(8,128)} %copy-done.23) | copy-start | bytes 700420
  493.3 10.8 %copy-start.53 = (f32[32]{0:T(128)S(1)}, f32[32]{0:T(128)}, u32[]{:S(2)}) copy-start(f32[32]{0:T(128)} %broadcast_in_dim.113) | copy-start | bytes 388
  953.2 8.5 copy-start.28
  961.8 31.4 %copy-start.54 = (pred[4]{0:T(512)(128)(4,1)S(1)}, pred[4]{0:T(512)(128)(4,1)}, u32[]{:S(2)}) copy-start(pred[4]{0:T(512)(128)(4,1)} %compare_and_fusion) | copy-start | bytes 16
  1044.4 10.9 %slice-start = ((s8[9437184]{0:T(1024)(128)(4,1)}), s8[4194304]{0:T(1024)(128)(4,1)S(1)}, s32[]{:S(2)}) async-start(s8[9437184]{0:T(1024)(128)(4,1)} %bitcast.156), calls=%async_computation | async-start | bytes 8388608
  1046.7 8.6 slice-start.1
  1046.7 8.6 slice-start.2
  1046.7 15.8 %slice-start.3 = ((s8[7077888]{0:T(1024)(128)(4,1)}), s8[4194304]{0:T(1024)(128)(4,1)S(1)}, s32[]{:S(2)}) async-start(s8[7077888]{0:T(1024)(128)(4,1)} %bitcast.167), calls=%async_computation.3 | async-start | bytes 8388608
  (35 other events, 169.8 us)

commit v3 on v2

--- a/solution.py
+++ b/solution.py
@@ -671,15 +671,12 @@
     ]
     for step in (3, 1, 2):
         vectors(step).start()
-    for h in range(PARTS):
+    for h in range(2):
         for step in (3, 1, 2):
             block(step, h).start()
     run("start", *own, *own_blocks)
     pl.when(jnp.logical_and(jnp.logical_not(shifts), jnp.logical_not(rises)))(stay)
 
-    for step in (3, 1, 2):
-        run("start", *thirds(step))
-
     @pl.when(shifts)
     def _():
         run("wait_recv", *shift(passing))
@@ -688,8 +685,12 @@
     for h in range(PARTS):
         for step in (2, 1, 3):
             block(step, h).wait_recv()
+            if h + 2 < PARTS:
+                block(step, h + 2).start()
             crossed(step, mine, h).start()
             passed(step, mine, 0, h).start()
+    for step in (3, 1, 2):
+        run("start", *thirds(step))
     for h in range(PARTS):
         for step in (2, 1, 3):
             crossed(step, other, h).wait_recv()
@@ -1202,11 +1203,11 @@
 
 
 def backward_body(
-    output_ref, attend_ref, two_ref, text_ref, cot_ref, one_ref, response_ref, reduce_w_ref,
+    output_ref, qkv_ref, two_ref, text_ref, cot_ref, one_ref, response_ref, reduce_w_ref,
     act_ref, slope_ref, normed_ref, expand_w_ref, conv_ref, out_ref, base_ref, small_ref,
-    rows_ref, embed_ref, silu_ref,
+    normed_two_ref, rows_ref, embed_ref, silu_ref, mapped_ref, text_kv_ref,
     output_out, attend_out, mapper_out, reduce_out, small_out, expand_out,
-    mapper_part, reduce_part, expand_part, one_out, text_out, grad_out, layer_out,
+    attend_part, mapper_part, reduce_part, expand_part, one_out, text_out, grad_out, layer_out,
     *scratch
 ):
     (
@@ -1271,6 +1272,76 @@
     one_kept = pltpu.make_async_copy(grad, one_out, keep.at[10])
     text_kept = pltpu.make_async_copy(text_all, text_out, keep.at[11])
 
+    def early_loads():
+        homes = [(acts, 0), (acts, 1), (slopes, 0), (slopes, 1), (front, 0)]
+        found = []
+        for i, (buffer, slot) in enumerate(homes):
+            width = min(TILE, qkv_ref.shape[1] - i * TILE)
+            dst = buffer.at[slot] if width == TILE else buffer.at[slot, :, pl.ds(0, width)]
+            found.append(
+                pltpu.make_async_copy(
+                    qkv_ref.at[:, pl.ds(i * TILE, width)], dst, load.at[2 + i if i < 4 else 0]
+                )
+            )
+        return found, homes
+
+    def early_column(i):
+        return pltpu.make_async_copy(
+            normed_two_ref.at[:, pl.ds(pl.multiple_of(i * part, part), part)],
+            columns.at[lax.rem(i, 2)],
+            load.at[6 + lax.rem(i, 2)],
+        )
+
+    def attend_stores(i):
+        half = part // 2
+        return [
+            pltpu.make_async_copy(
+                product.at[pl.ds(c * half, half), pl.ds(0, 3 * part)],
+                attend_part.at[i, c],
+                load.at[8 + c],
+            )
+            for c in (0, 1)
+        ]
+
+    def prepare(t):
+        copies, homes = early_loads()
+        for i, (copy, (buffer, slot)) in enumerate(zip(copies, homes)):
+            copy.wait()
+            width = min(TILE, qkv_ref.shape[1] - i * TILE)
+
+            def strip(k, carry, i=i, buffer=buffer, slot=slot, width=width):
+                rows = pl.ds(pl.multiple_of(k * 48, 48), 48)
+                cols = pl.ds(i * TILE, width)
+                high[rows, cols], low[rows, cols] = halves(buffer[slot, rows, 0:width])
+                return carry
+
+            lax.fori_loop(0, spots // 48, strip, 0)
+
+    def attend_outer(i):
+        early_column(i).wait()
+
+        @pl.when(i > 0)
+        def _():
+            for copy in attend_stores(jnp.maximum(i - 1, 0)):
+                copy.wait()
+
+        left = halves(columns[lax.rem(i, 2)])
+        text_left = halves(mapped_ref[:, pl.ds(pl.multiple_of(i * part, part), part)])
+        for k in range(3):
+            cols = pl.ds(k * part, part)
+            value = three_pass(left, (high[:, cols], low[:, cols]), ((0,), (0,)))
+            if k > 0:
+                right = halves(text_kv_ref[:, (k - 1) * part : k * part])
+                value = value + three_pass(text_left, right, ((0,), (0,)))
+            product[:, cols] = value
+        for copy in attend_stores(i):
+            copy.start()
+        pl.when(i + 2 < 4)(lambda: early_column(jnp.minimum(i + 2, 3)).start())
+
+    def settle_attend(t):
+        for copy in attend_stores(3):
+            copy.wait()
+
     def arrive(t):
         for copy in start_loads + scatters:
             copy.wait()
@@ -1500,6 +1571,8 @@
             )
         return found
 
+    for copy in early_loads()[0] + [early_column(0), early_column(1)]:
+        copy.start()
     for copy in scatters + start_loads + first_loads:
         copy.start()
 
@@ -1669,7 +1742,7 @@
     sum_stream(
         [
             ("plain", output_ref, output_out),
-            ("swap", attend_ref, attend_out),
+            ("swap", attend_part, attend_out),
             ("plain", mapper_part, mapper_out),
             ("plain", reduce_part, reduce_out),
             ("plain", small, small_out),
@@ -1677,6 +1750,9 @@
         ],
         scratch[:SCRATCH],
         [
+            (0, 1, prepare),
+            (1, 5, attend_outer),
+            (5, 6, settle_attend),
             (12, 13, arrive),
             (12, 21, normalize),
             (21, 22, give_late),
@@ -1709,8 +1785,9 @@
 
 
 def backward_sums(
-    collective, output_part, attend_part, two_share, text_share, cot, one, response, reduce_w, act,
-    slope, normed_all, expand_w, conv, out_share, base, small, rows, embed, silu, mapper_half
+    collective, output_part, qkv, two_share, text_share, cot, one, response, reduce_w, act, slope,
+    normed_all, expand_w, conv, out_share, base, small, normed_two, rows, embed, silu, mapped,
+    text_kv, mapper_half
 ):
     pixels, chan = conv.shape
     spots = normed_all.shape[0]
@@ -1734,6 +1811,7 @@
             shape(2, chan // 2, chan),
             shape(2, CHUNK, chan),
             shape(2, half, 4 * chan),
+            shape(4, 2, half, 3 * chan // 4),
             shape(2, mapper_half, chan),
             shape(2, chan // 2, chan),
             shape(4, 2, half, chan),
@@ -1742,8 +1820,8 @@
             shape(*block),
             shape(*block),
         ],
-        in_specs=[ANY] * 16 + [pl.BlockSpec(memory_space=pltpu.VMEM)] * 3,
-        out_specs=[ANY] * 13,
+        in_specs=[ANY] * 17 + [pl.BlockSpec(memory_space=pltpu.VMEM)] * 5,
+        out_specs=[ANY] * 14,
         scratch_shapes=stream_scratch(total, 4 * half // CHUNK, chan)
         + [
             pltpu.VMEM((3,) + block, f32),
@@ -1792,12 +1870,17 @@
         ),
         name="backward_sums",
     )(
-        output_part, attend_part, two_share, text_share, cot, one, response, reduce_w, act, slope,
-        normed_all, expand_w, conv, out_share, base, small, rows, embed, silu,
-    )
-
-
-def close_body(grad_in, token_in, conv_in, grad_home, token_home, conv_all, hold, send, recv, keep):
+        output_part, qkv, two_share, text_share, cot, one, response, reduce_w, act, slope,
+        normed_all, expand_w, conv, out_share, base, small, normed_two, rows, embed, silu, mapped,
+        text_kv,
+    )
+
+
+def close_body(
+    grad_in, token_in, conv_in, up_in, down_in,
+    grad_home, token_home, conv_all, below, above,
+    hold, send, recv, keep
+):
     core = lax.axis_index("cond")
     level = lax.axis_index("pair")
     me = lax.axis_index("dp")
@@ -1812,7 +1895,24 @@
     for c, s in others:
         greet(other(c, s))
     pl.when(moves)(lambda: greet((core, back_up, back_over)))
-    pl.semaphore_wait(pltpu.get_barrier_semaphore(), 7 + jnp.where(moves, 1, 0))
+    turned = jnp.logical_and(level == 1, me == 1)
+    quarter = up
+    lifts = quarter > 0
+    drops = jnp.logical_and(quarter < 3, jnp.logical_not(turned))
+    lifted = level < 3
+    dropped = jnp.logical_and(level > 0, jnp.logical_not(turned))
+    pl.when(lifted)(lambda: greet((core, me, near_of(me, rev(jnp.minimum(level + 1, 3))))))
+    pl.when(dropped)(lambda: greet((core, me, near_of(me, rev(jnp.maximum(level - 1, 0))))))
+    pl.semaphore_wait(
+        pltpu.get_barrier_semaphore(),
+        7 + jnp.where(moves, 1, 0) + jnp.where(lifts, 1, 0) + jnp.where(drops, 1, 0),
+    )
+    lift = remote(up_in, below, send.at[9], recv.at[9], (core, jnp.maximum(quarter - 1, 0), level))
+    drop = remote(down_in, above, send.at[10], recv.at[10], (core, jnp.minimum(quarter + 1, 3), level))
+    around = pltpu.make_async_copy(down_in, above, keep.at[3])
+    pl.when(lifts)(lift.start)
+    pl.when(drops)(drop.start)
+    pl.when(turned)(around.start)
     swaps = ((grad_in, grad_home), (token_in, token_home))
     aways = [remote(src, dst, send.at[i], recv.at[i], (core, up, over)) for i, (src, dst) in enumerate(swaps)]
     spreads = [
@@ -1841,19 +1941,24 @@
         copy.wait()
     for away in aways:
         pl.when(moves)(away.wait)
-
-
-def close_exchange(collective, grad, tokens, conv):
-    shapes = [grad.shape, tokens.shape, (8,) + conv.shape]
+    pl.when(lifts)(lift.wait_send)
+    pl.when(drops)(drop.wait_send)
+    pl.when(lifted)(lift.wait_recv)
+    pl.when(dropped)(drop.wait_recv)
+    pl.when(turned)(around.wait)
+
+
+def close_exchange(collective, grad, tokens, conv, up, down):
+    shapes = [grad.shape, tokens.shape, (8,) + conv.shape, up.shape, down.shape]
     return pl.pallas_call(
         close_body,
         out_shape=[jax.ShapeDtypeStruct(shape, jnp.float32) for shape in shapes],
-        in_specs=[ANY] * 3,
-        out_specs=[ANY] * 3,
-        scratch_shapes=[pltpu.VMEM(grad.shape, jnp.float32), DMA((9,)), DMA((9,)), DMA((3,))],
+        in_specs=[ANY] * 5,
+        out_specs=[ANY] * 5,
+        scratch_shapes=[pltpu.VMEM(grad.shape, jnp.float32), DMA((11,)), DMA((11,)), DMA((4,))],
         compiler_params=pltpu.CompilerParams(collective_id=collective, has_side_effects=True),
         name="close_exchange",
-    )(grad, tokens, conv)
+    )(grad, tokens, conv, up, down)
 
 
 def plane_body(
@@ -2010,8 +2115,6 @@
     grad_qkv = jnp.concatenate([grad_query, grad_kv[:spots]], axis=1)
     two_share = dot_t(grad_qkv, attend_w).reshape(4, pixels, chan)
     text_share = dot_t(grad_kv[spots:], attend_w[:, part:]).reshape(4, texts, chan)
-    attend_grad = t_dot(normed_two_all, grad_qkv)
-    attend_grad = attend_grad.at[:, part:].add(t_dot(mapped_all, grad_kv[spots:]))
     def row(value):
         return jnp.sum(value, axis=0, keepdims=True)
 
@@ -2044,6 +2147,11 @@
         axis=0,
     )
     slots = (texts + 7) // 8 * 8
+
+    def padded_rows(value):
+        value = value.reshape(4, texts, -1)
+        return jnp.pad(value, ((0, 0), (0, slots - texts), (0, 0))).reshape(4 * slots, -1)
+
     silu_padded = jnp.pad(
         silu_near.reshape(4, texts, text_part), ((0, 0), (0, slots - texts), (0, -text_part % 128))
     ).reshape(4 * slots, -1)
@@ -2051,12 +2159,12 @@
         embed_part.reshape(ratio_part, 1, 1), (ratio_part, 2, 128)
     ).reshape(2 * ratio_part, 128)
     (
-        output_sum, attend_sum, mapper_sum, reduce_sum, small, expand_sum, _, _, _,
+        output_sum, attend_sum, mapper_sum, reduce_sum, small, expand_sum, _, _, _, _,
         grad_one, grad_mapped_all, grad_conv, layer_output,
     ) = backward_sums(
         1,
         output_grad.reshape(2, half, chan),
-        attend_grad.reshape(size, 2, half, 3 * part),
+        grad_qkv,
         two_share,
         text_share,
         cot,
@@ -2071,9 +2179,12 @@
         out_share,
         out_base,
         jnp.stack([jnp.zeros((CHUNK, chan), jnp.float32), small_rows]),
+        normed_two_all,
         back_rows,
         embed_rows,
         silu_padded,
+        padded_rows(mapped_all),
+        padded_rows(grad_kv[spots:]),
         text_part // 2,
     )
     output_sum = output_sum.reshape(part, chan)
@@ -2111,27 +2222,26 @@
             for step in range(4)
         ]
     )
-    rims, conv_arrived, token_arrived = exchange(
-        13,
-        gathers=(jnp.stack([latent_rows[0], latent_rows[-1]]),),
-        scatters=(conv_blocks, tokens_near),
-    )
+    conv_arrived, token_arrived = exchange(13, scatters=(conv_blocks, tokens_near))
     token_blocks = jnp.take(
         jnp.concatenate([tokens_near[:1], token_arrived], axis=0), order, axis=0
     )
-    prior = near_of(rev(quarter), rev(jnp.maximum(quarter - 1, 0)))
-    after = near_of(rev(quarter), rev(jnp.minimum(quarter + 1, size - 1)))
-    from_above = jnp.where(quarter > 0, rims[prior, 1], 0.0)
-    from_below = jnp.where(quarter < size - 1, rims[after, 0], 0.0)
     inner = latent_rows[1:-1] + grad_one.reshape(rows, cols, chan)
-    inner = inner.at[-1].add(from_below).at[0].add(from_above)
-    latent_grad, tokens_grad, conv_all = close_exchange(
+    latent_grad, tokens_grad, conv_all, from_below, from_above = close_exchange(
         14,
         inner.reshape(pixels, chan),
         token_blocks.transpose(1, 0, 2).reshape(texts, size * text_part),
         conv_blocks[0] + jnp.sum(conv_arrived, axis=0),
-    )
-    latent_grad = latent_grad.reshape(latents.shape)
+        latent_rows[0],
+        latent_rows[-1],
+    )
+    from_above = jnp.where(level > 0, from_above, 0.0)[None]
+    from_below = jnp.where(level < size - 1, from_below, 0.0)[None]
+    still = jnp.zeros((rows - 2, cols, chan), jnp.float32)
+    latent_grad = latent_grad.reshape(rows, cols, chan) + jnp.concatenate(
+        [from_above, still, from_below], axis=0
+    )
+    latent_grad = latent_grad[None]
     tokens_grad = tokens_grad[None]
     conv_mine = jnp.sum(conv_all, axis=0)
     ratio = small[0]

time: 1070 us -> 1050 us (0.981)
  matrix products: 132 us -> 113 us
    dot_general x3 -> x1, matrix products: 31 us -> 6.6 us  [t_dot(): lax.dot_general(left, right, (((0,), (0,)), ((), ())), precision=FAST)]
    pallas_call x5, Pallas kernels: 195 us -> 177 us  [exchange(): pl.pallas_call(functools.partial(exchange_body, len(gathers), len(scatter...]
    unnamed x136 -> x141, local copies, waits for them, and re-layouts: 48.7 us -> 43.3 us
  transfers between devices with their start and end apart: 5 -> 5, of which waited for: 2 -> 2; matrix products, arithmetic and copies ran while one was open for 7% -> 8% of each run, Pallas kernels for 0% -> 1%
where the time goes in v3:
time: 1050 us; the launch traced here: 1040 us
  Pallas kernels  748 us (71%)
  matrix products  113 us (11%)
  local copies, waits for them, and re-layouts  94.8 us (9%)
  other arithmetic  53 us (5%)
  waiting for transfers between devices  16.2 us (2%)
  starting transfers between devices  14.2 us (1%)
    pallas_call x1, Pallas kernels, backward_sums(): pl.pallas_call(backward_body, out_shape=[shape(2, half, chan), shape(2, h...  447 us
    pallas_call x5, Pallas kernels, exchange(): pl.pallas_call(functools.partial(exchange_body, len(gathers), len(scatter...  177 us
    pallas_call x1, Pallas kernels, open_exchange(): pl.pallas_call(open_body, out_shape=[jax.ShapeDtypeStruct(shape, jnp.floa...  83.7 us
    dot_general x6, matrix products, dot(): return jnp.dot(left, right, precision=FAST)  49.3 us
    unnamed x141, local copies, waits for them, and re-layouts  43.3 us
    pallas_call x1, Pallas kernels, close_exchange(): pl.pallas_call(close_body, out_shape=[jax.ShapeDtypeStruct(shape, jnp.flo...  40.1 us
  transfers between devices with their start and end apart: 5, of which 2 were waited for; matrix products, arithmetic and copies ran while one was open for 8% of the time, Pallas kernels for 1%

profile of v3, /device:TPU:16, one launch (start us, length us, event | category | flops | bytes accessed | tf_op | source)
XLA Modules:
  0.0 1042.1 jit_solution(7081543911861603316)
XLA Ops:
  8.5 83.7 %open_exchange.1 = (f32[8,24,1536]{2,1,0:T(8,128)}, f32[4,15,384]{2,1,0:T(8,128)}, f32[19,1280]{1,0:T(8,128)}, f32[1,64]{1,0:T(1,128)}, f32[4,4,96,1536]{3,2,1,0...) custom-call(f32[6,24,1536]{2,1,0:T(8,128)} %bitcast.193, ...), custom_call_target="tpu_custom_call" | custom-call | tf_op jit(solution)/shard_map/open_exchange/pallas_call | solution.py:731
  96.6 5.5 fusion.71
  104.9 3.0 copy-done.1
  107.9 53.2 %exchange.5 = (f32[4,144,1536]{2,1,0:T(8,128)S(1)}, f32[4,1,3072]{2,1,0:T(1,128)S(1)}, f32[3,19,320]{2,1,0:T(8,128)S(1)}, f32[4,384,1152]{2,1,0:T(8,128)S(1)}) custom-call(f32[144,1536]{1,0:T(8,128)S(1)} %subtract_multiply_fusion.1.refs_0_, f32[1,3072]{1,0:T(1,128)S(1)} %fusion.56.refs_1_, ...), custom_call_target="tpu_custom_call", output_to_operand_aliasing={{3}: (3, {})} | custom-call | tf_op jit(solution)/shard_map/exchange/pallas_call | solution.py:500
  167.0 14.2 %multiply_reduce_fusion.1 = (f32[1536]{0:T(1024)S(1)}, f32[576,1536]{1,0:T(8,128)}, f32[576,1536]{1,0:T(8,128)}) fusion(f32[1536]{0:T(1024)S(1)} %copy-done.57, f32[576,1536]{1,0:T(8,128)S(1)} %bitcast.153, f32[1536,1536]{1,0:T(8,128)} %bitcast.162), kind=kOutput, calls=%fused_computation.30 | convolution fusion | flops 8164342272 | bytes 20066304 | tf_op jit(solution)/shard_map/dot_general | solution.py:291
  182.5 5.2 exchange.6
  195.2 4.2 multiply_add_fusion.response_ref
  200.1 12.6 %fusion.73 = f32[576,1536]{1,0:T(8,128)S(1)} fusion(f32[576,1536]{1,0:T(8,128)} %multiply_add_fusion.response_ref, f32[1536,1536]{1,0:T(8,128)} %reduce_w_ref.1), kind=kOutput, calls=%fused_computation.191 | convolution fusion | flops 8153726976 | bytes 16515072 | tf_op jit(solution)/shard_map/dot_general | solution.py:291
  213.7 46.0 %exchange.7 = (f32[3,144,1536]{2,1,0:T(8,128)S(1)}, f32[3,19,1536]{2,1,0:T(8,128)S(1)}) custom-call(f32[4,144,1536]{2,1,0:T(8,128)S(1)} %bitcast.151, f32[4,19,1536]{2,1,0:T(8,128)S(1)} %reshape.462.refs_1_), custom_call_target="tpu_custom_call" | custom-call | tf_op jit(solution)/shard_map/exchange/pallas_call | solution.py:500
  263.1 3.0 reduce_sum.250
  270.5 8.5 collective-permute-start.1
  283.1 15.8 %collective-permute-done.1.cot_ref = f32[144,1536]{1,0:T(8,128)} collective-permute-done((f32[144,1536]{1,0:T(8,128)}, f32[144,1536]{1,0:T(8,128)}, u32[]{:S(2)}, u32[]{:S(2)}) %collective-permute-start.1) | collective-permute-done | bytes 884768 | tf_op jit(solution)/shard_map/ppermute | solution.py:2072
  298.9 53.8 %exchange.8 = (f32[4,144,1536]{2,1,0:T(8,128)S(1)}, f32[4,19,1536]{2,1,0:T(8,128)S(1)}) custom-call(f32[144,1536]{1,0:T(8,128)S(1)} %subtract_multiply_fusion.refs_0_, f32[19,1536]{1,0:T(8,128)S(1)} %fusion.50.refs_1_), custom_call_target="tpu_custom_call" | custom-call | tf_op jit(solution)/shard_map/exchange/pallas_call | solution.py:500
  356.3 5.5 fusion.25
  364.1 9.3 fusion.4
  377.5 5.7 multiply_reduce_fusion
  398.3 3.0 fusion.74
  401.4 7.6 bitcast_reduce_fusion
  409.0 5.2 multiply_reduce_fusion.2
  414.2 7.0 multiply_multiply_fusion
  421.2 5.1 bitcast_reduce_fusion.1
  426.4 6.1 fusion.75
  437.6 5.4 fusion.2
  459.9 6.8 fusion.21.out_ref
  466.7 6.6 fusion.13.output_ref
  475.0 9.4 fusion.15.two_ref
  485.1 447.4 %backward_sums.1 = (f32[2,192,1536]{2,1,0:T(8,128)}, f32[2,192,4608]{2,1,0:T(8,128)}, f32[2,160,1536]{2,1,0:T(8,128)}, f32[2,768,1536]{2,1,0:T(8,128)}, f32[2,32...) custom-call(f32[2,192,1536]{2,1,0:T(8,128)} %fusion.13.output_ref, ...), custom_call_target="tpu_custom_call" | custom-call | tf_op jit(solution)/shard_map/backward_sums/pallas_call | solution.py:1805
  945.4 18.7 %exchange.9 = (f32[3,10,384]{2,1,0:T(8,128)S(1)}, f32[3,19,320]{2,1,0:T(8,128)S(1)}) custom-call(f32[4,10,384]{2,1,0:T(8,128)S(1)} %pad_maximum_fusion.5.refs_0_, f32[4,19,320]{2,1,0:T(8,128)S(1)} %reshape.486.refs_1_), custom_call_target="tpu_custom_call" | custom-call | tf_op jit(solution)/shard_map/exchange/pallas_call | solution.py:500
  970.7 40.1 %close_exchange.1 = (f32[144,1536]{1,0:T(8,128)}, f32[19,1280]{1,0:T(8,128)}, f32[8,10,384]{2,1,0:T(8,128)}, f32[24,1536]{1,0:T(8,128)}, f32[24,1536]{1,0:T(8,128)}) custom-call(f32[144,1536]{1,0:T(8,128)} %bitcast.179, f32[19,1280]{1,0:T(8,128)} %reshape.487.token_in, f32[10,384]{1,0:T(8,128)} %dynamic-slice_add_fusion.conv_in, ...), custom_call_target="tpu_custom_call" | custom-call | tf_op jit(solution)/shard_map/close_exchange/pallas_call | solution.py:1953
  1020.5 9.3 copy.87
  1029.8 4.2 copy.88
  1036.9 3.2 copy.90
  (290 shorter events, 124.8 us)
Async XLA Ops:
  0.7 189.9 %copy-start = (f32[320,1536]{1,0:T(8,128)S(1)}, f32[320,1536]{1,0:T(8,128)}, u32[]{:S(2)}) copy-start(f32[320,1536]{1,0:T(8,128)} %param.39) | copy-start | bytes 5898244
  93.4 10.9 %copy-start.34 = (f32[1536]{0:T(1024)}, f32[1536]{0:T(1024)S(1)}, u32[]{:S(2)}) copy-start(f32[1536]{0:T(1024)S(1)} %get-tuple-element.185) | copy-start | bytes 18436
  93.4 10.9 %copy-start.36 = (f32[1536]{0:T(1024)}, f32[1536]{0:T(1024)S(1)}, u32[]{:S(2)}) copy-start(f32[1536]{0:T(1024)S(1)} %get-tuple-element.186) | copy-start | bytes 18436
  93.4 10.9 %copy-start.38 = (f32[1536]{0:T(1024)}, f32[1536]{0:T(1024)S(1)}, u32[]{:S(2)}) copy-start(f32[1536]{0:T(1024)S(1)} %get-tuple-element.187) | copy-start | bytes 18436
  93.4 10.9 %copy-start.40 = (f32[1536]{0:T(1024)}, f32[1536]{0:T(1024)S(1)}, u32[]{:S(2)}) copy-start(f32[1536]{0:T(1024)S(1)} %get-tuple-element.188) | copy-start | bytes 18436
  93.4 10.9 %copy-start.41 = (f32[1536]{0:T(1024)}, f32[1536]{0:T(1024)S(1)}, u32[]{:S(2)}) copy-start(f32[1536]{0:T(1024)S(1)} %get-tuple-element.189) | copy-start | bytes 18436
  93.5 10.9 %copy-start.42 = (f32[1536]{0:T(1024)}, f32[1536]{0:T(1024)S(1)}, u32[]{:S(2)}) copy-start(f32[1536]{0:T(1024)S(1)} %get-tuple-element.190) | copy-start | bytes 18436
  93.5 10.9 %copy-start.43 = (f32[1536]{0:T(1024)}, f32[1536]{0:T(1024)S(1)}, u32[]{:S(2)}) copy-start(f32[1536]{0:T(1024)S(1)} %get-tuple-element.191) | copy-start | bytes 18436
  96.6 8.1 copy-start.30
  107.9 59.1 %copy-start.57 = (f32[1536]{0:T(1024)S(1)}, f32[1536]{0:T(1024)}, u32[]{:S(2)}) copy-start(f32[1536]{0:T(1024)} %param.32) | copy-start | bytes 18436
  164.1 17.2 %copy-start.5 = (f32[4,144,1536]{2,1,0:T(8,128)}, f32[4,144,1536]{2,1,0:T(8,128)S(1)}, u32[]{:S(2)}) copy-start(f32[4,144,1536]{2,1,0:T(8,128)S(1)} %get-tuple-element.88) | copy-start | bytes 10616836
  164.1 48.7 %collective-permute-start = (f32[144,1536]{1,0:T(8,128)}, f32[144,1536]{1,0:T(8,128)}, u32[]{:S(2)}, u32[]{:S(2)}) collective-permute-start(f32[144,1536]{1,0:T(8,128)} %bitcast), channel_id=1, source_target_pairs={{0,0},{1,1},{2,2},{3,3},{4,6},{5,7},{6,4},{7,5},{8,9},{9,8},{10,11... | collective-permute-start | bytes 2654216 | tf_op jit(solution)/shard_map/ppermute | solution.py:2052
  167.0 22.0 %copy-start.45 = (f32[1536]{0:T(1024)S(1)}, f32[1536]{0:T(1024)}, u32[]{:S(2)}) copy-start(f32[1536]{0:T(1024)} %param.33) | copy-start | bytes 18436
  181.2 13.9 %copy-start.48 = (f32[1536]{0:T(1024)S(1)}, f32[1536]{0:T(1024)}, u32[]{:S(2)}) copy-start(f32[1536]{0:T(1024)} %param.34) | copy-start | bytes 18436
  270.5 28.4 %collective-permute-start.1 = (f32[144,1536]{1,0:T(8,128)}, f32[144,1536]{1,0:T(8,128)}, u32[]{:S(2)}, u32[]{:S(2)}) collective-permute-start(f32[144,1536]{1,0:T(8,128)} %collective-permute-done), channel_id=1, source_target_pairs={{0,0},{1,5},{2,10},{3,15},{4,8},{5,13},{6,2},{7,7},{8,4},{9,1},{10... | collective-permute-start | bytes 2654216 | tf_op jit(solution)/shard_map/ppermute | solution.py:2072
  279.0 77.2 %copy-start.51 = (f32[384]{0:T(512)S(1)}, f32[384]{0:T(512)}, u32[]{:S(2)}) copy-start(f32[384]{0:T(512)} %param.42) | copy-start | bytes 4612
  281.9 70.8 %copy-start.16 = (f32[144,1536]{1,0:T(8,128)}, f32[144,1536]{1,0:T(8,128)S(1)}, u32[]{:S(2)}) copy-start(f32[144,1536]{1,0:T(8,128)S(1)} %get-tuple-element.193.one_ref) | copy-start | bytes 2654212
  352.7 39.2 %collective-permute-start.2 = (f32[144,1536]{1,0:T(8,128)}, f32[144,1536]{1,0:T(8,128)}, u32[]{:S(2)}, u32[]{:S(2)}) collective-permute-start(f32[144,1536]{1,0:T(8,128)} %collective-permute-done.1.cot_ref), channel_id=1, source_target_pairs={{0,1},{1,0},{2,3},{3,2},{4,5},{5,4},{6,7},{7,6},{8,9},{9,8},{10,11... | collective-permute-start | bytes 2654216 | tf_op jit(solution)/shard_map/ppermute | solution.py:2085
  353.3 40.3 %collective-permute-start.3 = (f32[144,1536]{1,0:T(8,128)}, f32[144,1536]{1,0:T(8,128)}, u32[]{:S(2)}, u32[]{:S(2)}) collective-permute-start(f32[144,1536]{1,0:T(8,128)} %collective-permute-done.1.cot_ref), channel_id=1, source_target_pairs={{0,2},{1,3},{2,0},{3,1},{4,6},{5,7},{6,4},{7,5},{8,10},{9,11},{10,... | collective-permute-start | bytes 2654216 | tf_op jit(solution)/shard_map/ppermute | solution.py:2085
  354.7 40.2 %collective-permute-start.4 = (f32[144,1536]{1,0:T(8,128)}, f32[144,1536]{1,0:T(8,128)}, u32[]{:S(2)}, u32[]{:S(2)}) collective-permute-start(f32[144,1536]{1,0:T(8,128)} %collective-permute-done.1.cot_ref), channel_id=1, source_target_pairs={{0,3},{1,2},{2,1},{3,0},{4,7},{5,6},{6,5},{7,4},{8,11},{9,10},{10,... | collective-permute-start | bytes 2654216 | tf_op jit(solution)/shard_map/ppermute | solution.py:2085
  364.1 9.3 copy-start.50
  437.6 8.8 copy-start.47
  437.6 8.8 copy-start.49
  459.9 15.2 %slice-start = ((s8[7077888]{0:T(1024)(128)(4,1)}), s8[4194304]{0:T(1024)(128)(4,1)S(1)}, s32[]{:S(2)}) async-start(s8[7077888]{0:T(1024)(128)(4,1)} %bitcast.144), calls=%async_computation | async-start | bytes 8388608
  466.7 8.3 slice-start.1
  475.0 9.4 copy-start.52
  965.5 51.8 %copy-start.53 = (f32[6]{0:T(128)S(1)}, f32[6]{0:T(128)}, u32[]{:S(2)}) copy-start(f32[6]{0:T(128)} %pad.32.clone) | copy-start | bytes 76
  970.7 48.8 %copy-start.26 = (f32[144,1536]{1,0:T(8,128)S(1)}, f32[144,1536]{1,0:T(8,128)}, u32[]{:S(2)}) copy-start(f32[144,1536]{1,0:T(8,128)} %get-tuple-element.105) | copy-start | bytes 2654212
  1019.6 10.2 slice-start.2
  1020.5 9.3 slice-start.3
  1020.5 9.3 slice-start.4
  1020.5 16.4 %slice-start.5 = ((s8[7077888]{0:T(1024)(128)(4,1)}), s8[4194304]{0:T(1024)(128)(4,1)S(1)}, s32[]{:S(2)}) async-start(s8[7077888]{0:T(1024)(128)(4,1)} %bitcast.171), calls=%async_computation.5 | async-start | bytes 8388608
  (38 other events, 169.1 us)

commit v4 on v3

--- a/solution.py
+++ b/solution.py
@@ -399,8 +399,8 @@
     refs = refs[count + relays :]
     passing, refs = refs[:swap_count], refs[swap_count:]
     holds = refs[: gather_count + swap_count]
-    send, recv, keep = refs[gather_count + swap_count :][:3]
-    sems = refs[gather_count + swap_count + 3 :]
+    send, recv, keep, diag_out, diag_in = refs[gather_count + swap_count :][:5]
+    sems = refs[gather_count + swap_count + 5 :]
     core = lax.axis_index("cond")
     level = lax.axis_index("pair")
     me = lax.axis_index("dp")
@@ -443,8 +443,11 @@
         pl.when(jnp.logical_and(shifts, final))(shift(i, swap_outs).start)
         pl.when(jnp.logical_and(shifts, jnp.logical_not(final)))(shift(i, passing).start)
         pl.when(jnp.logical_and(jnp.logical_not(shifts), rises))(rise(i, swap_ins).start)
+    tall = [i for i in range(gather_count) if ins[i].shape[0] % 16 == 0]
     for step in (3, 1, 2):
         for i in range(near_count):
+            if step == 3 and i in tall:
+                continue
             if i < gather_count:
                 src, dst = ins[i], outs[i].at[step]
             else:
@@ -454,7 +457,22 @@
                 (core, level, near_of(me, step)),
             )
             copy.start()
-            near_copies.append(copy)
+            if i not in tall:
+                near_copies.append(copy)
+
+    def direct(i, step):
+        return remote(
+            ins[i], outs[i].at[step], send.at[i, step - 1], recv.at[i, step - 1],
+            (core, level, near_of(me, step)),
+        )
+
+    def onward(i, step):
+        half = ins[i].shape[0] // 2
+        rows = pl.ds(half * (step - 1), half)
+        return remote(
+            outs[i].at[step, rows], outs[i].at[3, rows], diag_out.at[i, step - 1],
+            diag_in.at[i, step - 1], (core, level, near_of(me, 3 - step)),
+        )
 
     def through(src, hold, dst, sem):
         load = pltpu.make_async_copy(src, hold, sem)
@@ -474,8 +492,16 @@
         )
         pl.when(shifts)(shift(i, passing).wait_recv)
         pl.when(jnp.logical_and(shifts, rises))(rise(i, passing).start)
+    for i in tall:
+        for step in (1, 2):
+            direct(i, step).wait_recv()
+            onward(i, step).start()
     if relays:
         relay_end()
+    for i in tall:
+        for step in (1, 2):
+            direct(i, step).wait_send()
+            onward(i, step).wait()
     for copy in near_copies:
         copy.wait()
     for i in range(swap_count):
@@ -495,6 +521,7 @@
     staged = len(gathers) + len(swaps)
     scratch = [pltpu.VMEM(item.shape, f32) for item in tuple(gathers) + tuple(swaps)]
     scratch += [DMA((count, 3)), DMA((count, 3)), DMA((max(staged, 1),))]
+    scratch += [DMA((count, 2)), DMA((count, 2))]
     if relay:
         scratch += [DMA((3,)), DMA((3,)), DMA((2, 3)), DMA((2, 3))]
     outs = pl.pallas_call(
@@ -1204,7 +1231,8 @@
 
 def backward_body(
     output_ref, qkv_ref, two_ref, text_ref, cot_ref, one_ref, response_ref, reduce_w_ref,
-    act_ref, slope_ref, normed_ref, expand_w_ref, conv_ref, out_ref, base_ref, small_ref,
+    act_ref, slope_ref, normed_ref, expand_w_ref, conv_ref, mixture_ref, out_w_ref, base_ref,
+    small_ref,
     normed_two_ref, rows_ref, embed_ref, silu_ref, mapped_ref, text_kv_ref,
     output_out, attend_out, mapper_out, reduce_out, small_out, expand_out,
     attend_part, mapper_part, reduce_part, expand_part, one_out, text_out, grad_out, layer_out,
@@ -1497,11 +1525,11 @@
         for copy in reduce_stores(count - 1):
             copy.wait()
         text_kept.wait()
-        for copy in loads:
+        for copy in loads + out_loads():
             copy.start()
         sums[0:4] = jnp.zeros((4, chan), jnp.float32)
 
-    outward = near_slots(out_ref, out_got, send, recv, 3)
+    outward = near_slots(out_own, out_got, send, recv, 3)
 
     def away(i):
         rows = pl.ds(pl.multiple_of(i * 8, 8), 8)
@@ -1516,7 +1544,6 @@
     first_loads = [pltpu.make_async_copy(small_ref, small, keep.at[1])]
     loads = [
         pltpu.make_async_copy(conv_ref, conv, keep.at[2]),
-        pltpu.make_async_copy(out_ref.at[0], out_own, keep.at[3]),
         pltpu.make_async_copy(base_ref, base, keep.at[4]),
     ]
     kept = pltpu.make_async_copy(one, grad_out, keep.at[5])
@@ -1612,6 +1639,24 @@
             for step in (3, 1, 2)
         ]
 
+    def out_loads():
+        return [
+            pltpu.make_async_copy(mixture_ref, columns.at[0], load.at[6]),
+            pltpu.make_async_copy(out_w_ref, product, load.at[7]),
+        ]
+
+    def out_product(i):
+        pl.when(i == 0)(lambda: [copy.wait() for copy in out_loads()] and None)
+        rows = pl.ds(pl.multiple_of(i * pixels, pixels), pixels)
+        left = halves(columns[0, rows])
+
+        def strip(k, carry):
+            cols = pl.ds(pl.multiple_of(k * TILE, TILE), TILE)
+            out_own[i, :, cols] = three_pass(left, halves(product[:, cols]), ((1,), (0,)))
+            return carry
+
+        lax.fori_loop(0, count, strip, 0)
+
     def send_out(t):
         for copy in outward:
             copy.start()
@@ -1735,7 +1780,7 @@
     def outlet(t):
         pl.when(t == 0)(lambda: [copy.wait() for copy in loads[1:] + outward] and None)
         rows = pl.ds(pl.multiple_of(t * 8, 8), 8)
-        base[rows] += out_own[rows] + out_got[0, rows] + out_got[1, rows] + out_got[2, rows]
+        base[rows] += out_own[0, rows] + out_got[0, rows] + out_got[1, rows] + out_got[2, rows]
         pl.when(moves)(away(t).start)
         pl.when(jnp.logical_not(moves))(here(t).start)
 
@@ -1771,6 +1816,7 @@
             (68, 74, tiles),
             (74, 75, give),
             (60, 78, outlet),
+            (39, 43, out_product),
             (43, 44, send_out),
         ],
     )
@@ -1786,8 +1832,8 @@
 
 def backward_sums(
     collective, output_part, qkv, two_share, text_share, cot, one, response, reduce_w, act, slope,
-    normed_all, expand_w, conv, out_share, base, small, normed_two, rows, embed, silu, mapped,
-    text_kv, mapper_half
+    normed_all, expand_w, conv, mixture, out_w, base, small, normed_two, rows, embed, silu,
+    mapped, text_kv, mapper_half
 ):
     pixels, chan = conv.shape
     spots = normed_all.shape[0]
@@ -1820,7 +1866,7 @@
             shape(*block),
             shape(*block),
         ],
-        in_specs=[ANY] * 17 + [pl.BlockSpec(memory_space=pltpu.VMEM)] * 5,
+        in_specs=[ANY] * 18 + [pl.BlockSpec(memory_space=pltpu.VMEM)] * 5,
         out_specs=[ANY] * 14,
         scratch_shapes=stream_scratch(total, 4 * half // CHUNK, chan)
         + [
@@ -1830,7 +1876,7 @@
             pltpu.VMEM(block, f32),
             pltpu.VMEM(block, f32),
             pltpu.VMEM((3,) + block, f32),
-            pltpu.VMEM(block, f32),
+            pltpu.VMEM((4,) + block, f32),
             pltpu.VMEM(block, f32),
             pltpu.VMEM(small.shape, f32),
             pltpu.VMEM((spots, chan), f32),
@@ -1871,8 +1917,8 @@
         name="backward_sums",
     )(
         output_part, qkv, two_share, text_share, cot, one, response, reduce_w, act, slope,
-        normed_all, expand_w, conv, out_share, base, small, normed_two, rows, embed, silu, mapped,
-        text_kv,
+        normed_all, expand_w, conv, mixture, out_w, base, small, normed_two, rows, embed, silu,
+        mapped, text_kv,
     )
 
 
@@ -2099,7 +2145,6 @@
     probs = expo / jnp.sum(expo, axis=-1, keepdims=True)
     mixture_h = jnp.einsum("uio,ouy->iuy", probs, value_h, precision=FAST)
     mixture = mixture_h.reshape(query.shape)
-    out_share = dot(mixture, output_weight).reshape(4, pixels, chan)
     out_base = hidden_two + out_b
 
     output_grad = t_dot(mixture, cot_all)
@@ -2176,7 +2221,8 @@
         normed_all,
         expand_w,
         total_conv.reshape(pixels, chan),
-        out_share,
+        mixture,
+        output_weight,
         out_base,
         jnp.stack([jnp.zeros((CHUNK, chan), jnp.float32), small_rows]),
         normed_two_all,

time: 1050 us -> 1030 us (0.981)
  Pallas kernels: 748 us -> 731 us
    pallas_call x5, Pallas kernels: 177 us -> 153 us  [exchange(): pl.pallas_call(functools.partial(exchange_body, len(gathers), len(scatter...]
    dot_general x6 -> x5, matrix products: 49.3 us -> 42.2 us  [dot(): return jnp.dot(left, right, precision=FAST)]
    unnamed x141 -> x135, local copies, waits for them, and re-layouts: 43.3 us -> 43.3 us
  transfers between devices with their start and end apart: 5 -> 5, of which waited for: 2 -> 1; matrix products, arithmetic and copies ran while one was open for 8% -> 8% of each run, Pallas kernels for 1% -> 0%
where the time goes in v4:
time: 1030 us; the launch traced here: 1020 us
  Pallas kernels  731 us (71%)
  matrix products  107 us (10%)
  local copies, waits for them, and re-layouts  93.6 us (9%)
  other arithmetic  54.9 us (5%)
  starting transfers between devices  15.6 us (2%)
  waiting for transfers between devices  14.8 us (1%)
    pallas_call x1, Pallas kernels, backward_sums(): pl.pallas_call(backward_body, out_shape=[shape(2, half, chan), shape(2, h...  454 us
    pallas_call x5, Pallas kernels, exchange(): pl.pallas_call(functools.partial(exchange_body, len(gathers), len(scatter...  153 us
    pallas_call x1, Pallas kernels, open_exchange(): pl.pallas_call(open_body, out_shape=[jax.ShapeDtypeStruct(shape, jnp.floa...  83.7 us
    unnamed x135, local copies, waits for them, and re-layouts  43.3 us
    dot_general x5, matrix products, dot(): return jnp.dot(left, right, precision=FAST)  42.2 us
    pallas_call x1, Pallas kernels, close_exchange(): pl.pallas_call(close_body, out_shape=[jax.ShapeDtypeStruct(shape, jnp.flo...  40.1 us
    dot_general x4, matrix products, dot_t(): lax.dot_general(left, right, (((1,), (1,)), ((), ())), precision=FAST)  21.3 us
  transfers between devices with their start and end apart: 5, of which 1 were waited for; matrix products, arithmetic and copies ran while one was open for 8% of the time, Pallas kernels for 0%

profile of v4, /device:TPU:16, one launch (start us, length us, event | category | flops | bytes accessed | tf_op | source)
XLA Modules:
  0.0 1020.3 jit_solution(8560111530698546342)
XLA Ops:
  8.5 83.7 %open_exchange.1 = (f32[8,24,1536]{2,1,0:T(8,128)}, f32[4,15,384]{2,1,0:T(8,128)}, f32[19,1280]{1,0:T(8,128)}, f32[1,64]{1,0:T(1,128)}, f32[4,4,96,1536]{3,2,1,0...) custom-call(f32[6,24,1536]{2,1,0:T(8,128)} %bitcast.188, ...), custom_call_target="tpu_custom_call" | custom-call | tf_op jit(solution)/shard_map/open_exchange/pallas_call | solution.py:758
  96.6 5.5 fusion.69
  107.9 43.8 %exchange.5 = (f32[4,144,1536]{2,1,0:T(8,128)S(1)}, f32[4,1,3072]{2,1,0:T(1,128)S(1)}, f32[3,19,320]{2,1,0:T(8,128)S(1)}, f32[4,384,1152]{2,1,0:T(8,128)S(1)}) custom-call(f32[144,1536]{1,0:T(8,128)S(1)} %subtract_multiply_fusion.1.refs_0_, f32[1,3072]{1,0:T(1,128)S(1)} %fusion.54.refs_1_, ...), custom_call_target="tpu_custom_call", output_to_operand_aliasing={{3}: (3, {})} | custom-call | tf_op jit(solution)/shard_map/exchange/pallas_call | solution.py:527
  154.7 3.6 collective-permute-start
  159.0 14.2 %multiply_reduce_fusion.1 = (f32[1536]{0:T(1024)S(1)}, f32[576,1536]{1,0:T(8,128)}, f32[576,1536]{1,0:T(8,128)}) fusion(f32[1536]{0:T(1024)S(1)} %copy-done.56, f32[576,1536]{1,0:T(8,128)S(1)} %bitcast.148, f32[1536,1536]{1,0:T(8,128)} %bitcast.157), kind=kOutput, calls=%fused_computation.30 | convolution fusion | flops 8164342272 | bytes 20066304 | tf_op jit(solution)/shard_map/dot_general | solution.py:291
  174.5 4.7 exchange.6
  186.7 4.2 multiply_add_fusion.response_ref
  191.6 12.6 %fusion.71 = f32[576,1536]{1,0:T(8,128)S(1)} fusion(f32[576,1536]{1,0:T(8,128)} %multiply_add_fusion.response_ref, f32[1536,1536]{1,0:T(8,128)} %reduce_w_ref.1), kind=kOutput, calls=%fused_computation.189 | convolution fusion | flops 8153726976 | bytes 16515072 | tf_op jit(solution)/shard_map/dot_general | solution.py:291
  205.2 46.2 %exchange.7 = (f32[3,144,1536]{2,1,0:T(8,128)S(1)}, f32[3,19,1536]{2,1,0:T(8,128)S(1)}) custom-call(f32[4,144,1536]{2,1,0:T(8,128)S(1)} %bitcast.146, f32[4,19,1536]{2,1,0:T(8,128)S(1)} %reshape.459.refs_1_), custom_call_target="tpu_custom_call" | custom-call | tf_op jit(solution)/shard_map/exchange/pallas_call | solution.py:527
  254.8 3.0 reduce_sum.250
  262.2 8.5 collective-permute-start.1
  274.8 14.8 %collective-permute-done.1.cot_ref = f32[144,1536]{1,0:T(8,128)} collective-permute-done((f32[144,1536]{1,0:T(8,128)}, f32[144,1536]{1,0:T(8,128)}, u32[]{:S(2)}, u32[]{:S(2)}) %collective-permute-start.1) | collective-permute-done | bytes 884768 | tf_op jit(solution)/shard_map/ppermute | solution.py:2118
  289.6 43.1 %exchange.8 = (f32[4,144,1536]{2,1,0:T(8,128)S(1)}, f32[4,19,1536]{2,1,0:T(8,128)S(1)}) custom-call(f32[144,1536]{1,0:T(8,128)S(1)} %subtract_multiply_fusion.refs_0_, f32[19,1536]{1,0:T(8,128)S(1)} %fusion.48.refs_1_), custom_call_target="tpu_custom_call" | custom-call | tf_op jit(solution)/shard_map/exchange/pallas_call | solution.py:527
  336.3 5.5 fusion.22
  344.2 9.0 fusion.4
  357.3 5.7 multiply_reduce_fusion
  377.7 3.0 fusion.72
  380.7 7.6 bitcast_reduce_fusion
  388.4 5.2 fusion.42
  393.6 7.0 multiply_multiply_fusion
  400.6 5.1 bitcast_reduce_fusion.1
  405.8 6.1 fusion.73
  417.0 5.4 fusion.2
  436.8 6.8 fusion.13.output_ref
  444.9 3.5 pad_maximum_fusion.qkv_ref
  448.5 10.8 %fusion.15.two_ref = f32[4,144,1536]{2,1,0:T(8,128)} fusion(f32[1536,1152,1]{1,0,2:T(8,128)} %bitcast.141, f32[4,144,768]{2,1,0:T(8,128)S(1)} %bitcast.169, f32[4,144,384]{2,1,0:T(8,128)S(1)} %copy-done.26), kind=kOutput, calls=%fused_computation.34 | convolution fusion | flops 6115958784 | bytes 13271040 | tf_op jit(solution)/shard_map/dot_general | solution.py:295
  459.9 454.2 %backward_sums.1 = (f32[2,192,1536]{2,1,0:T(8,128)}, f32[2,192,4608]{2,1,0:T(8,128)}, f32[2,160,1536]{2,1,0:T(8,128)}, f32[2,768,1536]{2,1,0:T(8,128)}, f32[2,32...) custom-call(f32[2,192,1536]{2,1,0:T(8,128)} %fusion.13.output_ref, ...), custom_call_target="tpu_custom_call" | custom-call | tf_op jit(solution)/shard_map/backward_sums/pallas_call | solution.py:1851
  927.0 15.5 %exchange.9 = (f32[3,10,384]{2,1,0:T(8,128)S(1)}, f32[3,19,320]{2,1,0:T(8,128)S(1)}) custom-call(f32[4,10,384]{2,1,0:T(8,128)S(1)} %pad_maximum_fusion.5.refs_0_, f32[4,19,320]{2,1,0:T(8,128)S(1)} %reshape.483.refs_1_), custom_call_target="tpu_custom_call" | custom-call | tf_op jit(solution)/shard_map/exchange/pallas_call | solution.py:527
  949.1 40.1 %close_exchange.1 = (f32[144,1536]{1,0:T(8,128)}, f32[19,1280]{1,0:T(8,128)}, f32[8,10,384]{2,1,0:T(8,128)}, f32[24,1536]{1,0:T(8,128)}, f32[24,1536]{1,0:T(8,128)}) custom-call(f32[144,1536]{1,0:T(8,128)} %bitcast.174, f32[19,1280]{1,0:T(8,128)} %reshape.484.token_in, f32[10,384]{1,0:T(8,128)} %dynamic-slice_add_fusion.conv_in, ...), custom_call_target="tpu_custom_call" | custom-call | tf_op jit(solution)/shard_map/close_exchange/pallas_call | solution.py:1999
  998.9 9.3 copy.86
  1008.2 4.2 copy.87
  1015.3 3.2 copy.89
  (282 shorter events, 122.4 us)
Async XLA Ops:
  0.7 181.3 %copy-start = (f32[320,1536]{1,0:T(8,128)S(1)}, f32[320,1536]{1,0:T(8,128)}, u32[]{:S(2)}) copy-start(f32[320,1536]{1,0:T(8,128)} %param.39) | copy-start | bytes 5898244
  93.4 10.9 %copy-start.33 = (f32[1536]{0:T(1024)}, f32[1536]{0:T(1024)S(1)}, u32[]{:S(2)}) copy-start(f32[1536]{0:T(1024)S(1)} %get-tuple-element.185) | copy-start | bytes 18436
  93.4 10.9 %copy-start.35 = (f32[1536]{0:T(1024)}, f32[1536]{0:T(1024)S(1)}, u32[]{:S(2)}) copy-start(f32[1536]{0:T(1024)S(1)} %get-tuple-element.186) | copy-start | bytes 18436
  93.4 10.9 %copy-start.37 = (f32[1536]{0:T(1024)}, f32[1536]{0:T(1024)S(1)}, u32[]{:S(2)}) copy-start(f32[1536]{0:T(1024)S(1)} %get-tuple-element.187) | copy-start | bytes 18436
  93.4 10.9 %copy-start.39 = (f32[1536]{0:T(1024)}, f32[1536]{0:T(1024)S(1)}, u32[]{:S(2)}) copy-start(f32[1536]{0:T(1024)S(1)} %get-tuple-element.188) | copy-start | bytes 18436
  93.4 10.9 %copy-start.40 = (f32[1536]{0:T(1024)}, f32[1536]{0:T(1024)S(1)}, u32[]{:S(2)}) copy-start(f32[1536]{0:T(1024)S(1)} %get-tuple-element.189) | copy-start | bytes 18436
  93.5 10.9 %copy-start.41 = (f32[1536]{0:T(1024)}, f32[1536]{0:T(1024)S(1)}, u32[]{:S(2)}) copy-start(f32[1536]{0:T(1024)S(1)} %get-tuple-element.190) | copy-start | bytes 18436
  93.5 10.9 %copy-start.42 = (f32[1536]{0:T(1024)}, f32[1536]{0:T(1024)S(1)}, u32[]{:S(2)}) copy-start(f32[1536]{0:T(1024)S(1)} %get-tuple-element.191) | copy-start | bytes 18436
  96.6 7.8 copy-start.55
  96.6 8.1 copy-start.29
  107.9 51.1 %copy-start.56 = (f32[1536]{0:T(1024)S(1)}, f32[1536]{0:T(1024)}, u32[]{:S(2)}) copy-start(f32[1536]{0:T(1024)} %param.32) | copy-start | bytes 18436
  154.7 18.6 %copy-start.5 = (f32[4,144,1536]{2,1,0:T(8,128)}, f32[4,144,1536]{2,1,0:T(8,128)S(1)}, u32[]{:S(2)}) copy-start(f32[4,144,1536]{2,1,0:T(8,128)S(1)} %get-tuple-element.88) | copy-start | bytes 10616836
  154.7 49.6 %collective-permute-start = (f32[144,1536]{1,0:T(8,128)}, f32[144,1536]{1,0:T(8,128)}, u32[]{:S(2)}, u32[]{:S(2)}) collective-permute-start(f32[144,1536]{1,0:T(8,128)} %bitcast), channel_id=1, source_target_pairs={{0,0},{1,1},{2,2},{3,3},{4,6},{5,7},{6,4},{7,5},{8,9},{9,8},{10,11... | collective-permute-start | bytes 2654216 | tf_op jit(solution)/shard_map/ppermute | solution.py:2098
  159.0 21.4 %copy-start.44 = (f32[1536]{0:T(1024)S(1)}, f32[1536]{0:T(1024)}, u32[]{:S(2)}) copy-start(f32[1536]{0:T(1024)} %param.33) | copy-start | bytes 18436
  173.2 13.4 %copy-start.47 = (f32[1536]{0:T(1024)S(1)}, f32[1536]{0:T(1024)}, u32[]{:S(2)}) copy-start(f32[1536]{0:T(1024)} %param.34) | copy-start | bytes 18436
  182.8 8.1 copy-start.20
  262.2 27.4 %collective-permute-start.1 = (f32[144,1536]{1,0:T(8,128)}, f32[144,1536]{1,0:T(8,128)}, u32[]{:S(2)}, u32[]{:S(2)}) collective-permute-start(f32[144,1536]{1,0:T(8,128)} %collective-permute-done), channel_id=1, source_target_pairs={{0,0},{1,5},{2,10},{3,15},{4,8},{5,13},{6,2},{7,7},{8,4},{9,1},{10... | collective-permute-start | bytes 2654216 | tf_op jit(solution)/shard_map/ppermute | solution.py:2118
  270.7 65.6 %copy-start.50 = (f32[384]{0:T(512)S(1)}, f32[384]{0:T(512)}, u32[]{:S(2)}) copy-start(f32[384]{0:T(512)} %param.42) | copy-start | bytes 4612
  273.6 59.2 %copy-start.17 = (f32[144,1536]{1,0:T(8,128)}, f32[144,1536]{1,0:T(8,128)S(1)}, u32[]{:S(2)}) copy-start(f32[144,1536]{1,0:T(8,128)S(1)} %get-tuple-element.193.one_ref) | copy-start | bytes 2654212
  332.8 38.9 %collective-permute-start.2 = (f32[144,1536]{1,0:T(8,128)}, f32[144,1536]{1,0:T(8,128)}, u32[]{:S(2)}, u32[]{:S(2)}) collective-permute-start(f32[144,1536]{1,0:T(8,128)} %collective-permute-done.1.cot_ref), channel_id=1, source_target_pairs={{0,1},{1,0},{2,3},{3,2},{4,5},{5,4},{6,7},{7,6},{8,9},{9,8},{10,11... | collective-permute-start | bytes 2654216 | tf_op jit(solution)/shard_map/ppermute | solution.py:2131
  333.5 39.5 %collective-permute-start.3 = (f32[144,1536]{1,0:T(8,128)}, f32[144,1536]{1,0:T(8,128)}, u32[]{:S(2)}, u32[]{:S(2)}) collective-permute-start(f32[144,1536]{1,0:T(8,128)} %collective-permute-done.1.cot_ref), channel_id=1, source_target_pairs={{0,2},{1,3},{2,0},{3,1},{4,6},{5,7},{6,4},{7,5},{8,10},{9,11},{10,... | collective-permute-start | bytes 2654216 | tf_op jit(solution)/shard_map/ppermute | solution.py:2131
  334.9 39.4 %collective-permute-start.4 = (f32[144,1536]{1,0:T(8,128)}, f32[144,1536]{1,0:T(8,128)}, u32[]{:S(2)}, u32[]{:S(2)}) collective-permute-start(f32[144,1536]{1,0:T(8,128)} %collective-permute-done.1.cot_ref), channel_id=1, source_target_pairs={{0,3},{1,2},{2,1},{3,0},{4,7},{5,6},{6,5},{7,4},{8,11},{9,10},{10,... | collective-permute-start | bytes 2654216 | tf_op jit(solution)/shard_map/ppermute | solution.py:2131
  344.2 9.1 copy-start.49
  417.0 8.8 copy-start.46
  417.0 8.9 copy-start.48
  448.5 10.8 %copy-start.51 = (f32[32]{0:T(128)S(1)}, f32[32]{0:T(128)}, u32[]{:S(2)}) copy-start(f32[32]{0:T(128)} %broadcast_in_dim.119) | copy-start | bytes 388
  943.9 51.8 %copy-start.52 = (f32[6]{0:T(128)S(1)}, f32[6]{0:T(128)}, u32[]{:S(2)}) copy-start(f32[6]{0:T(128)} %pad.32.clone) | copy-start | bytes 76
  949.1 48.8 %copy-start.25 = (f32[144,1536]{1,0:T(8,128)S(1)}, f32[144,1536]{1,0:T(8,128)}, u32[]{:S(2)}) copy-start(f32[144,1536]{1,0:T(8,128)} %get-tuple-element.105) | copy-start | bytes 2654212
  998.0 10.2 slice-start
  998.9 9.3 slice-start.1
  998.9 9.3 slice-start.2
  998.9 16.4 %slice-start.3 = ((s8[7077888]{0:T(1024)(128)(4,1)}), s8[4194304]{0:T(1024)(128)(4,1)S(1)}, s32[]{:S(2)}) async-start(s8[7077888]{0:T(1024)(128)(4,1)} %bitcast.166), calls=%async_computation.3 | async-start | bytes 8388608
  (35 other events, 145.0 us)

commit v5 on v4

--- a/solution.py
+++ b/solution.py
@@ -399,8 +399,12 @@
     refs = refs[count + relays :]
     passing, refs = refs[:swap_count], refs[swap_count:]
     holds = refs[: gather_count + swap_count]
-    send, recv, keep, diag_out, diag_in = refs[gather_count + swap_count :][:5]
-    sems = refs[gather_count + swap_count + 5 :]
+    refs = refs[gather_count + swap_count :]
+    joined = [i for i in range(gather_count, near_count) if ins[i].shape[1] % 16 == 0]
+    sums = dict(zip(joined, zip(refs[: 2 * len(joined) : 2], refs[1 : 2 * len(joined) : 2])))
+    refs = refs[2 * len(joined) :]
+    send, recv, keep, diag_out, diag_in, join_out, join_in, join_load = refs[:8]
+    sems = refs[8:]
     core = lax.axis_index("cond")
     level = lax.axis_index("pair")
     me = lax.axis_index("dp")
@@ -433,6 +437,40 @@
             recv.at[near_count + i, 1], (core, goal, me),
         )
 
+    def part_rows(i, k):
+        half = ins[i].shape[1] // 2
+        return pl.ds(half * k, half)
+
+    def early(i, step):
+        return remote(
+            ins[i].at[3, part_rows(i, step - 1)], sums[i][1].at[step - 1],
+            diag_out.at[i, step - 1], diag_in.at[i, step - 1], (core, level, near_of(me, step)),
+        )
+
+    def alone(i, step):
+        rows = part_rows(i, step - 1)
+        return remote(
+            ins[i].at[step, rows], outs[i].at[step - 1, rows], send.at[i, step - 1],
+            recv.at[i, step - 1], (core, level, near_of(me, step)),
+        )
+
+    def join(i, step):
+        rows = part_rows(i, 2 - step)
+        return remote(
+            sums[i][0].at[step - 1], outs[i].at[step - 1, rows], join_out.at[i, step - 1],
+            join_in.at[i, step - 1], (core, level, near_of(me, step)),
+        )
+
+    def join_own(i, step):
+        return pltpu.make_async_copy(
+            ins[i].at[step, part_rows(i, 2 - step)], sums[i][0].at[step - 1], join_load.at[i, step - 1]
+        )
+
+    for i in joined:
+        for step in (1, 2):
+            early(i, step).start()
+            alone(i, step).start()
+            join_own(i, step).start()
     swap_ins = ins[near_count:]
     swap_outs = outs[near_count:]
     near_copies = []
@@ -446,7 +484,7 @@
     tall = [i for i in range(gather_count) if ins[i].shape[0] % 16 == 0]
     for step in (3, 1, 2):
         for i in range(near_count):
-            if step == 3 and i in tall:
+            if (step == 3 and i in tall) or i in joined:
                 continue
             if i < gather_count:
                 src, dst = ins[i], outs[i].at[step]
@@ -492,6 +530,16 @@
         )
         pl.when(shifts)(shift(i, passing).wait_recv)
         pl.when(jnp.logical_and(shifts, rises))(rise(i, passing).start)
+    for i in joined:
+        for step in (1, 2):
+            early(i, 3 - step).wait_recv()
+            join_own(i, step).wait()
+            sums[i][0][step - 1] += sums[i][1][2 - step]
+            join(i, step).start()
+        for step in (1, 2):
+            early(i, step).wait_send()
+            alone(i, step).wait()
+            join(i, step).wait()
     for i in tall:
         for step in (1, 2):
             direct(i, step).wait_recv()
@@ -513,15 +561,19 @@
 def exchange(collective, gathers=(), scatters=(), swaps=(), relay=()):
     f32 = jnp.float32
     shapes = [(4,) + item.shape for item in gathers]
-    shapes += [(3,) + item.shape[1:] for item in scatters]
+    joined = [item for item in scatters if item.shape[1] % 16 == 0]
+    shapes += [(2 if item.shape[1] % 16 == 0 else 3,) + item.shape[1:] for item in scatters]
     shapes += [item.shape for item in swaps]
     count = len(shapes)
     shapes += [item.shape for item in relay]
     shapes += [item.shape for item in swaps]
     staged = len(gathers) + len(swaps)
     scratch = [pltpu.VMEM(item.shape, f32) for item in tuple(gathers) + tuple(swaps)]
+    for item in joined:
+        half = (2, item.shape[1] // 2) + item.shape[2:]
+        scratch += [pltpu.VMEM(half, f32), pltpu.VMEM(half, f32)]
     scratch += [DMA((count, 3)), DMA((count, 3)), DMA((max(staged, 1),))]
-    scratch += [DMA((count, 2)), DMA((count, 2))]
+    scratch += [DMA((count, 2))] * 5
     if relay:
         scratch += [DMA((3,)), DMA((3,)), DMA((2, 3)), DMA((2, 3))]
     outs = pl.pallas_call(

time: 1030 us -> 1010 us (0.981)
  Pallas kernels: 731 us -> 717 us
    pallas_call x5, Pallas kernels: 153 us -> 142 us  [exchange(): pl.pallas_call(functools.partial(exchange_body, len(gathers), len(scatter...]
    unnamed x135 -> x149, local copies, waits for them, and re-layouts: 43.3 us -> 43 us
where the time goes in v5:
time: 1010 us
  Pallas kernels  717 us (71%)
  matrix products  107 us (11%)
  local copies, waits for them, and re-layouts  96.6 us (10%)
  other arithmetic  54 us (5%)
  starting transfers between devices  15.7 us (2%)
  waiting for transfers between devices  14.7 us (1%)
    pallas_call x1, Pallas kernels, backward_sums(): pl.pallas_call(backward_body, out_shape=[shape(2, half, chan), shape(2, h...  451 us
    pallas_call x5, Pallas kernels, exchange(): pl.pallas_call(functools.partial(exchange_body, len(gathers), len(scatter...  142 us
    pallas_call x1, Pallas kernels, open_exchange(): pl.pallas_call(open_body, out_shape=[jax.ShapeDtypeStruct(shape, jnp.floa...  83.7 us
    unnamed x149, local copies, waits for them, and re-layouts  43 us
    dot_general x5, matrix products, dot(): return jnp.dot(left, right, precision=FAST)  42.2 us
    pallas_call x1, Pallas kernels, close_exchange(): pl.pallas_call(close_body, out_shape=[jax.ShapeDtypeStruct(shape, jnp.flo...  40 us
    dot_general x4, matrix products, dot_t(): lax.dot_general(left, right, (((1,), (1,)), ((), ())), precision=FAST)  21.3 us
  transfers between devices with their start and end apart: 5, of which 1 were waited for; matrix products, arithmetic and copies ran while one was open for 8% of the time, Pallas kernels for 0%

profile of v5, /device:TPU:16, one launch (start us, length us, event | category | flops | bytes accessed | tf_op | source)
XLA Modules:
  0.0 1008.0 jit_solution(7809992913943396125)
XLA Ops:
  8.5 83.7 %open_exchange.1 = (f32[8,24,1536]{2,1,0:T(8,128)}, f32[4,15,384]{2,1,0:T(8,128)}, f32[19,1280]{1,0:T(8,128)}, f32[1,64]{1,0:T(1,128)}, f32[4,4,96,1536]{3,2,1,0...) custom-call(f32[6,24,1536]{2,1,0:T(8,128)} %bitcast.188, ...), custom_call_target="tpu_custom_call" | custom-call | tf_op jit(solution)/shard_map/open_exchange/pallas_call | solution.py:810
  97.2 5.5 fusion.69
  105.5 3.0 copy-done.1
  108.5 43.9 %exchange.5 = (f32[4,144,1536]{2,1,0:T(8,128)S(1)}, f32[4,1,3072]{2,1,0:T(1,128)S(1)}, f32[3,19,320]{2,1,0:T(8,128)S(1)}, f32[4,384,1152]{2,1,0:T(8,128)S(1)}) custom-call(f32[144,1536]{1,0:T(8,128)S(1)} %subtract_multiply_fusion.1.refs_0_, f32[1,3072]{1,0:T(1,128)S(1)} %fusion.54.refs_1_, ...), custom_call_target="tpu_custom_call", output_to_operand_aliasing={{3}: (3, {})} | custom-call | tf_op jit(solution)/shard_map/exchange/pallas_call | solution.py:579
  155.4 3.6 collective-permute-start
  159.8 14.2 %multiply_reduce_fusion.1 = (f32[1536]{0:T(1024)S(1)}, f32[576,1536]{1,0:T(8,128)}, f32[576,1536]{1,0:T(8,128)}) fusion(f32[1536]{0:T(1024)S(1)} %copy-done.63, f32[576,1536]{1,0:T(8,128)S(1)} %bitcast.148, f32[1536,1536]{1,0:T(8,128)} %bitcast.157), kind=kOutput, calls=%fused_computation.30 | convolution fusion | flops 8164342272 | bytes 20066304 | tf_op jit(solution)/shard_map/dot_general | solution.py:291
  175.3 4.7 exchange.6
  190.3 4.2 multiply_add_fusion.response_ref
  195.2 12.6 %fusion.71 = f32[576,1536]{1,0:T(8,128)S(1)} fusion(f32[576,1536]{1,0:T(8,128)} %multiply_add_fusion.response_ref, f32[1536,1536]{1,0:T(8,128)} %reduce_w_ref.1), kind=kOutput, calls=%fused_computation.189 | convolution fusion | flops 8153726976 | bytes 16515072 | tf_op jit(solution)/shard_map/dot_general | solution.py:291
  208.8 37.0 %exchange.7 = (f32[2,144,1536]{2,1,0:T(8,128)S(1)}, f32[3,19,1536]{2,1,0:T(8,128)S(1)}) custom-call(f32[4,144,1536]{2,1,0:T(8,128)S(1)} %bitcast.146, f32[4,19,1536]{2,1,0:T(8,128)S(1)} %reshape.459.refs_1_), custom_call_target="tpu_custom_call" | custom-call | tf_op jit(solution)/shard_map/exchange/pallas_call | solution.py:579
  256.8 8.6 collective-permute-start.1
  268.2 14.7 %collective-permute-done.1.cot_ref = f32[144,1536]{1,0:T(8,128)} collective-permute-done((f32[144,1536]{1,0:T(8,128)}, f32[144,1536]{1,0:T(8,128)}, u32[]{:S(2)}, u32[]{:S(2)}) %collective-permute-start.1) | collective-permute-done | bytes 884768 | tf_op jit(solution)/shard_map/ppermute | solution.py:2170
  282.9 41.2 %exchange.8 = (f32[4,144,1536]{2,1,0:T(8,128)S(1)}, f32[4,19,1536]{2,1,0:T(8,128)S(1)}) custom-call(f32[144,1536]{1,0:T(8,128)S(1)} %subtract_multiply_fusion.refs_0_, f32[19,1536]{1,0:T(8,128)S(1)} %fusion.48.refs_1_), custom_call_target="tpu_custom_call" | custom-call | tf_op jit(solution)/shard_map/exchange/pallas_call | solution.py:579
  327.6 5.5 fusion.22
  335.5 9.0 fusion.4
  348.6 5.7 multiply_reduce_fusion
  369.0 3.0 fusion.72
  372.0 7.7 bitcast_reduce_fusion
  379.7 5.2 fusion.42
  384.9 7.0 multiply_multiply_fusion
  392.0 5.2 bitcast_reduce_fusion.1
  397.1 6.1 fusion.73
  408.4 5.5 fusion.2
  428.2 6.8 fusion.13.output_ref
  436.3 3.5 pad_maximum_fusion.qkv_ref
  439.8 10.7 %fusion.15.two_ref = f32[4,144,1536]{2,1,0:T(8,128)} fusion(f32[1536,1152,1]{1,0,2:T(8,128)} %bitcast.141, f32[4,144,768]{2,1,0:T(8,128)S(1)} %bitcast.169, f32[4,144,384]{2,1,0:T(8,128)S(1)} %copy-done.24), kind=kOutput, calls=%fused_computation.34 | convolution fusion | flops 6115958784 | bytes 13271040 | tf_op jit(solution)/shard_map/dot_general | solution.py:295
  451.2 451.2 %backward_sums.1 = (f32[2,192,1536]{2,1,0:T(8,128)}, f32[2,192,4608]{2,1,0:T(8,128)}, f32[2,160,1536]{2,1,0:T(8,128)}, f32[2,768,1536]{2,1,0:T(8,128)}, f32[2,32...) custom-call(f32[2,192,1536]{2,1,0:T(8,128)} %fusion.13.output_ref, ...), custom_call_target="tpu_custom_call" | custom-call | tf_op jit(solution)/shard_map/backward_sums/pallas_call | solution.py:1903
  915.3 15.0 %exchange.9 = (f32[3,10,384]{2,1,0:T(8,128)S(1)}, f32[3,19,320]{2,1,0:T(8,128)S(1)}) custom-call(f32[4,10,384]{2,1,0:T(8,128)S(1)} %pad_maximum_fusion.5.refs_0_, f32[4,19,320]{2,1,0:T(8,128)S(1)} %reshape.483.refs_1_), custom_call_target="tpu_custom_call" | custom-call | tf_op jit(solution)/shard_map/exchange/pallas_call | solution.py:579
  936.9 40.0 %close_exchange.1 = (f32[144,1536]{1,0:T(8,128)}, f32[19,1280]{1,0:T(8,128)}, f32[8,10,384]{2,1,0:T(8,128)}, f32[24,1536]{1,0:T(8,128)}, f32[24,1536]{1,0:T(8,128)}) custom-call(f32[144,1536]{1,0:T(8,128)} %bitcast.174, f32[19,1280]{1,0:T(8,128)} %reshape.484.token_in, f32[10,384]{1,0:T(8,128)} %dynamic-slice_add_fusion.conv_in, ...), custom_call_target="tpu_custom_call" | custom-call | tf_op jit(solution)/shard_map/close_exchange/pallas_call | solution.py:2051
  986.5 9.3 copy.86
  995.9 4.2 copy.87
  1003.0 3.2 copy.89
  (296 shorter events, 124.5 us)
Async XLA Ops:
  0.7 185.0 %copy-start = (f32[320,1536]{1,0:T(8,128)S(1)}, f32[320,1536]{1,0:T(8,128)}, u32[]{:S(2)}) copy-start(f32[320,1536]{1,0:T(8,128)} %param.39) | copy-start | bytes 5898244
  94.0 10.9 %copy-start.32 = (f32[1536]{0:T(1024)}, f32[1536]{0:T(1024)S(1)}, u32[]{:S(2)}) copy-start(f32[1536]{0:T(1024)S(1)} %get-tuple-element.185) | copy-start | bytes 18436
  94.0 10.9 %copy-start.34 = (f32[1536]{0:T(1024)}, f32[1536]{0:T(1024)S(1)}, u32[]{:S(2)}) copy-start(f32[1536]{0:T(1024)S(1)} %get-tuple-element.186) | copy-start | bytes 18436
  94.0 10.9 %copy-start.36 = (f32[1536]{0:T(1024)}, f32[1536]{0:T(1024)S(1)}, u32[]{:S(2)}) copy-start(f32[1536]{0:T(1024)S(1)} %get-tuple-element.187) | copy-start | bytes 18436
  94.0 10.9 %copy-start.38 = (f32[1536]{0:T(1024)}, f32[1536]{0:T(1024)S(1)}, u32[]{:S(2)}) copy-start(f32[1536]{0:T(1024)S(1)} %get-tuple-element.188) | copy-start | bytes 18436
  94.0 10.9 %copy-start.39 = (f32[1536]{0:T(1024)}, f32[1536]{0:T(1024)S(1)}, u32[]{:S(2)}) copy-start(f32[1536]{0:T(1024)S(1)} %get-tuple-element.189) | copy-start | bytes 18436
  94.0 10.9 %copy-start.40 = (f32[1536]{0:T(1024)}, f32[1536]{0:T(1024)S(1)}, u32[]{:S(2)}) copy-start(f32[1536]{0:T(1024)S(1)} %get-tuple-element.190) | copy-start | bytes 18436
  94.0 10.9 %copy-start.41 = (f32[1536]{0:T(1024)}, f32[1536]{0:T(1024)S(1)}, u32[]{:S(2)}) copy-start(f32[1536]{0:T(1024)S(1)} %get-tuple-element.191) | copy-start | bytes 18436
  108.5 51.3 %copy-start.63 = (f32[1536]{0:T(1024)S(1)}, f32[1536]{0:T(1024)}, u32[]{:S(2)}) copy-start(f32[1536]{0:T(1024)} %param.32) | copy-start | bytes 18436
  155.4 18.6 %copy-start.5 = (f32[4,144,1536]{2,1,0:T(8,128)}, f32[4,144,1536]{2,1,0:T(8,128)S(1)}, u32[]{:S(2)}) copy-start(f32[4,144,1536]{2,1,0:T(8,128)S(1)} %get-tuple-element.88) | copy-start | bytes 10616836
  155.4 52.5 %collective-permute-start = (f32[144,1536]{1,0:T(8,128)}, f32[144,1536]{1,0:T(8,128)}, u32[]{:S(2)}, u32[]{:S(2)}) collective-permute-start(f32[144,1536]{1,0:T(8,128)} %bitcast), channel_id=1, source_target_pairs={{0,0},{1,1},{2,2},{3,3},{4,6},{5,7},{6,4},{7,5},{8,9},{9,8},{10,11... | collective-permute-start | bytes 2654216 | tf_op jit(solution)/shard_map/ppermute | solution.py:2150
  159.8 22.7 %copy-start.43 = (f32[1536]{0:T(1024)S(1)}, f32[1536]{0:T(1024)}, u32[]{:S(2)}) copy-start(f32[1536]{0:T(1024)} %param.33) | copy-start | bytes 18436
  174.0 12.5 %copy-start.45 = (f32[4,384]{1,0:T(4,128)S(1)}, f32[4,384]{1,0:T(4,128)}, u32[]{:S(2)}) copy-start(f32[4,384]{1,0:T(4,128)} %get-tuple-element.181) | copy-start | bytes 18436
  174.0 12.5 %copy-start.44 = (f32[4,384]{1,0:T(4,128)S(1)}, f32[4,384]{1,0:T(4,128)}, u32[]{:S(2)}) copy-start(f32[4,384]{1,0:T(4,128)} %get-tuple-element.179) | copy-start | bytes 18436
  254.1 13.9 %copy-start.25 = (f32[19,1536]{1,0:T(8,128)S(1)}, f32[19,1536]{1,0:T(8,128)}, u32[]{:S(2)}) copy-start(f32[19,1536]{1,0:T(8,128)} %reduce_sum.255) | copy-start | bytes 350212
  256.1 11.9 %copy-start.51 = (f32[144]{0:T(256)S(1)}, f32[144]{0:T(256)}, u32[]{:S(2)}) copy-start(f32[144]{0:T(256)} %div.124) | copy-start | bytes 1732
  256.8 11.3 %copy-start.52 = (f32[144]{0:T(256)S(1)}, f32[144]{0:T(256)}, u32[]{:S(2)}) copy-start(f32[144]{0:T(256)} %rsqrt.25) | copy-start | bytes 1732
  256.8 26.1 %collective-permute-start.1 = (f32[144,1536]{1,0:T(8,128)}, f32[144,1536]{1,0:T(8,128)}, u32[]{:S(2)}, u32[]{:S(2)}) collective-permute-start(f32[144,1536]{1,0:T(8,128)} %collective-permute-done), channel_id=1, source_target_pairs={{0,0},{1,5},{2,10},{3,15},{4,8},{5,13},{6,2},{7,7},{8,4},{9,1},{10... | collective-permute-start | bytes 2654216 | tf_op jit(solution)/shard_map/ppermute | solution.py:2170
  265.4 62.2 %copy-start.55 = (f32[384]{0:T(512)S(1)}, f32[384]{0:T(512)}, u32[]{:S(2)}) copy-start(f32[384]{0:T(512)} %param.42) | copy-start | bytes 4612
  268.0 56.0 %copy-start.16 = (f32[144,1536]{1,0:T(8,128)}, f32[144,1536]{1,0:T(8,128)S(1)}, u32[]{:S(2)}) copy-start(f32[144,1536]{1,0:T(8,128)S(1)} %get-tuple-element.193.one_ref) | copy-start | bytes 2654212
  324.1 38.9 %collective-permute-start.2 = (f32[144,1536]{1,0:T(8,128)}, f32[144,1536]{1,0:T(8,128)}, u32[]{:S(2)}, u32[]{:S(2)}) collective-permute-start(f32[144,1536]{1,0:T(8,128)} %collective-permute-done.1.cot_ref), channel_id=1, source_target_pairs={{0,1},{1,0},{2,3},{3,2},{4,5},{5,4},{6,7},{7,6},{8,9},{9,8},{10,11... | collective-permute-start | bytes 2654216 | tf_op jit(solution)/shard_map/ppermute | solution.py:2183
  324.2 40.0 %collective-permute-start.3 = (f32[144,1536]{1,0:T(8,128)}, f32[144,1536]{1,0:T(8,128)}, u32[]{:S(2)}, u32[]{:S(2)}) collective-permute-start(f32[144,1536]{1,0:T(8,128)} %collective-permute-done.1.cot_ref), channel_id=1, source_target_pairs={{0,2},{1,3},{2,0},{3,1},{4,6},{5,7},{6,4},{7,5},{8,10},{9,11},{10,... | collective-permute-start | bytes 2654216 | tf_op jit(solution)/shard_map/ppermute | solution.py:2183
  325.3 40.3 %collective-permute-start.4 = (f32[144,1536]{1,0:T(8,128)}, f32[144,1536]{1,0:T(8,128)}, u32[]{:S(2)}, u32[]{:S(2)}) collective-permute-start(f32[144,1536]{1,0:T(8,128)} %collective-permute-done.1.cot_ref), channel_id=1, source_target_pairs={{0,3},{1,2},{2,1},{3,0},{4,7},{5,6},{6,5},{7,4},{8,11},{9,10},{10,... | collective-permute-start | bytes 2654216 | tf_op jit(solution)/shard_map/ppermute | solution.py:2183
  335.5 9.1 copy-start.54
  408.4 8.9 copy-start.53
  439.8 10.7 %copy-start.56 = (f32[32]{0:T(128)S(1)}, f32[32]{0:T(128)}, u32[]{:S(2)}) copy-start(f32[32]{0:T(128)} %broadcast_in_dim.119) | copy-start | bytes 388
  931.7 51.7 %copy-start.57 = (f32[6]{0:T(128)S(1)}, f32[6]{0:T(128)}, u32[]{:S(2)}) copy-start(f32[6]{0:T(128)} %pad.32.clone) | copy-start | bytes 76
  936.9 48.7 %copy-start.23 = (f32[144,1536]{1,0:T(8,128)S(1)}, f32[144,1536]{1,0:T(8,128)}, u32[]{:S(2)}) copy-start(f32[144,1536]{1,0:T(8,128)} %get-tuple-element.105) | copy-start | bytes 2654212
  985.6 10.2 %slice-start = ((s8[9437184]{0:T(1024)(128)(4,1)}), s8[4194304]{0:T(1024)(128)(4,1)S(1)}, s32[]{:S(2)}) async-start(s8[9437184]{0:T(1024)(128)(4,1)} %bitcast.153), calls=%async_computation | async-start | bytes 8388608
  986.5 9.3 slice-start.1
  986.5 9.3 slice-start.2
  986.5 16.4 %slice-start.3 = ((s8[7077888]{0:T(1024)(128)(4,1)}), s8[4194304]{0:T(1024)(128)(4,1)S(1)}, s32[]{:S(2)}) async-start(s8[7077888]{0:T(1024)(128)(4,1)} %bitcast.166), calls=%async_computation.3 | async-start | bytes 8388608
  (42 other events, 187.1 us)

commit v6 on v5

--- a/solution.py
+++ b/solution.py
@@ -1181,14 +1181,14 @@
 
     stages = (
         (0, start),
-        (3, combine),
-        (5, depart),
-        (8, relay),
-        (11, root),
-        (14, spread),
-        (17, landed),
-        (20, arrived),
-        (23, finish),
+        (2, combine),
+        (3, depart),
+        (6, relay),
+        (9, root),
+        (12, spread),
+        (15, landed),
+        (18, arrived),
+        (21, finish),
     )
 
     def step(t, carry):
@@ -1203,7 +1203,7 @@
             pl.when(jnp.logical_and(t >= low, t < high))(lambda hook=hook, low=low: hook(t - low))
         return carry
 
-    lax.fori_loop(0, total + 23, step, 0)
+    lax.fori_loop(0, total + 21, step, 0)
 
 
 def stream_scratch(total, most, width):
@@ -2059,6 +2059,39 @@
     )(grad, tokens, conv, up, down)
 
 
+def deliver_body(count, *refs):
+    ins, outs, holds = refs[:count], refs[count : 2 * count], refs[2 * count : 3 * count]
+    load, store = refs[3 * count :]
+    loads, stores = [], []
+    for i in range(count):
+        rows = ins[i].shape[0] // 8
+        for k in range(8):
+            part = pl.ds(k * rows, rows)
+            loads.append(pltpu.make_async_copy(ins[i].at[part], holds[i].at[part], load.at[i, k]))
+            stores.append(pltpu.make_async_copy(holds[i].at[part], outs[i].at[part], store.at[i, k]))
+    for copy in loads:
+        copy.start()
+    for first, then in zip(loads, stores):
+        first.wait()
+        then.start()
+    for copy in stores:
+        copy.wait()
+
+
+def deliver(*arrays):
+    count = len(arrays)
+    return pl.pallas_call(
+        functools.partial(deliver_body, count),
+        out_shape=[jax.ShapeDtypeStruct(item.shape, item.dtype) for item in arrays],
+        in_specs=[ANY] * count,
+        out_specs=[ANY] * count,
+        scratch_shapes=[pltpu.VMEM(item.shape, item.dtype) for item in arrays]
+        + [DMA((count, 8)), DMA((count, 8))],
+        compiler_params=pltpu.CompilerParams(vmem_limit_bytes=48 * 2**20),
+        name="deliver",
+    )(*arrays)
+
+
 def plane_body(
     latents,
     ratio_embed,
@@ -2291,6 +2324,7 @@
     reduce_sum = reduce_sum.reshape(wide, chan)
     expand_sum = expand_sum.reshape(part, hid)
     layer_output = layer_output.reshape(latents.shape)
+    mapper_sum, expand_sum = deliver(mapper_sum, expand_sum)
     grad_mapped_all = grad_mapped_all[:, :texts].reshape(size * texts, chan)
     gate = 1.0 / (1.0 + jnp.exp(-near_tokens))
     tokens_near = dot_t(grad_mapped_all, text_weight) * (

time: 1010 us -> 1010 us (level)
    pallas_call x0 -> x1, Pallas kernels: none -> 11.3 us  [deliver(): pl.pallas_call(functools.partial(deliver_body, count), out_shape=[jax.Sha...]
    unnamed x149 -> x155, local copies, waits for them, and re-layouts: 43 us -> 34.2 us
where the time goes in v6:
time: 1010 us
  Pallas kernels  726 us (72%)
  matrix products  107 us (11%)
  local copies, waits for them, and re-layouts  87.9 us (9%)
  other arithmetic  51.9 us (5%)
  starting transfers between devices  15.7 us (2%)
  waiting for transfers between devices  14.7 us (1%)
    pallas_call x1, Pallas kernels, backward_sums(): pl.pallas_call(backward_body, out_shape=[shape(2, half, chan), shape(2, h...  446 us
    pallas_call x5, Pallas kernels, exchange(): pl.pallas_call(functools.partial(exchange_body, len(gathers), len(scatter...  144 us
    pallas_call x1, Pallas kernels, open_exchange(): pl.pallas_call(open_body, out_shape=[jax.ShapeDtypeStruct(shape, jnp.floa...  83.7 us
    dot_general x5, matrix products, dot(): return jnp.dot(left, right, precision=FAST)  42.2 us
    pallas_call x1, Pallas kernels, close_exchange(): pl.pallas_call(close_body, out_shape=[jax.ShapeDtypeStruct(shape, jnp.flo...  40.1 us
    unnamed x155, local copies, waits for them, and re-layouts  34.2 us
    dot_general x4, matrix products, dot_t(): lax.dot_general(left, right, (((1,), (1,)), ((), ())), precision=FAST)  21.3 us
  transfers between devices with their start and end apart: 5, of which 1 were waited for; matrix products, arithmetic and copies ran while one was open for 8% of the time, Pallas kernels for 0%

profile of v6, /device:TPU:16, one launch (start us, length us, event | category | flops | bytes accessed | tf_op | source)
XLA Modules:
  0.0 1006.5 jit_solution(13724133475749002900)
XLA Ops:
  8.5 83.7 %open_exchange.1 = (f32[8,24,1536]{2,1,0:T(8,128)}, f32[4,15,384]{2,1,0:T(8,128)}, f32[19,1280]{1,0:T(8,128)}, f32[1,64]{1,0:T(1,128)}, f32[4,4,96,1536]{3,2,1,0...) custom-call(f32[6,24,1536]{2,1,0:T(8,128)} %bitcast.188, ...), custom_call_target="tpu_custom_call" | custom-call | tf_op jit(solution)/shard_map/open_exchange/pallas_call | solution.py:810
  97.2 5.5 fusion.69
  105.5 3.0 copy-done.1
  108.5 43.9 %exchange.5 = (f32[4,144,1536]{2,1,0:T(8,128)S(1)}, f32[4,1,3072]{2,1,0:T(1,128)S(1)}, f32[3,19,320]{2,1,0:T(8,128)S(1)}, f32[4,384,1152]{2,1,0:T(8,128)S(1)}) custom-call(f32[144,1536]{1,0:T(8,128)S(1)} %subtract_multiply_fusion.1.refs_0_, f32[1,3072]{1,0:T(1,128)S(1)} %fusion.54.refs_1_, ...), custom_call_target="tpu_custom_call", output_to_operand_aliasing={{3}: (3, {})} | custom-call | tf_op jit(solution)/shard_map/exchange/pallas_call | solution.py:579
  155.4 3.6 collective-permute-start
  159.8 14.2 %multiply_reduce_fusion.1 = (f32[1536]{0:T(1024)S(1)}, f32[576,1536]{1,0:T(8,128)}, f32[576,1536]{1,0:T(8,128)}) fusion(f32[1536]{0:T(1024)S(1)} %copy-done.67, f32[576,1536]{1,0:T(8,128)S(1)} %bitcast.148, f32[1536,1536]{1,0:T(8,128)} %bitcast.158), kind=kOutput, calls=%fused_computation.30 | convolution fusion | flops 8164342272 | bytes 20066304 | tf_op jit(solution)/shard_map/dot_general | solution.py:291
  175.3 4.7 exchange.6
  190.3 4.2 multiply_add_fusion.response_ref
  195.3 12.6 %fusion.71 = f32[576,1536]{1,0:T(8,128)S(1)} fusion(f32[576,1536]{1,0:T(8,128)} %multiply_add_fusion.response_ref, f32[1536,1536]{1,0:T(8,128)} %reduce_w_ref.1), kind=kOutput, calls=%fused_computation.189 | convolution fusion | flops 8153726976 | bytes 16515072 | tf_op jit(solution)/shard_map/dot_general | solution.py:291
  208.9 37.0 %exchange.7 = (f32[2,144,1536]{2,1,0:T(8,128)S(1)}, f32[3,19,1536]{2,1,0:T(8,128)S(1)}) custom-call(f32[4,144,1536]{2,1,0:T(8,128)S(1)} %bitcast.146, f32[4,19,1536]{2,1,0:T(8,128)S(1)} %reshape.459.refs_1_), custom_call_target="tpu_custom_call" | custom-call | tf_op jit(solution)/shard_map/exchange/pallas_call | solution.py:579
  256.9 8.6 collective-permute-start.1
  268.3 14.7 %collective-permute-done.1.cot_ref = f32[144,1536]{1,0:T(8,128)} collective-permute-done((f32[144,1536]{1,0:T(8,128)}, f32[144,1536]{1,0:T(8,128)}, u32[]{:S(2)}, u32[]{:S(2)}) %collective-permute-start.1) | collective-permute-done | bytes 884768 | tf_op jit(solution)/shard_map/ppermute | solution.py:2203
  283.0 41.1 %exchange.8 = (f32[4,144,1536]{2,1,0:T(8,128)S(1)}, f32[4,19,1536]{2,1,0:T(8,128)S(1)}) custom-call(f32[144,1536]{1,0:T(8,128)S(1)} %subtract_multiply_fusion.refs_0_, f32[19,1536]{1,0:T(8,128)S(1)} %fusion.48.refs_1_), custom_call_target="tpu_custom_call" | custom-call | tf_op jit(solution)/shard_map/exchange/pallas_call | solution.py:579
  327.7 5.5 fusion.22
  335.6 9.0 fusion.4
  348.6 5.7 multiply_reduce_fusion
  369.0 3.0 fusion.72
  372.1 7.7 bitcast_reduce_fusion
  379.8 5.2 fusion.42
  385.0 7.0 multiply_multiply_fusion
  392.0 5.2 bitcast_reduce_fusion.1
  397.2 6.1 fusion.73
  408.4 5.5 fusion.2
  428.2 6.8 fusion.13.output_ref
  436.3 3.5 pad_maximum_fusion.qkv_ref
  439.9 10.7 %fusion.15.two_ref = f32[4,144,1536]{2,1,0:T(8,128)} fusion(f32[1536,1152,1]{1,0,2:T(8,128)} %bitcast.141, f32[4,144,768]{2,1,0:T(8,128)S(1)} %bitcast.170, f32[4,144,384]{2,1,0:T(8,128)S(1)} %copy-done.26), kind=kOutput, calls=%fused_computation.34 | convolution fusion | flops 6115958784 | bytes 13271040 | tf_op jit(solution)/shard_map/dot_general | solution.py:295
  451.3 446.4 %backward_sums.1 = (f32[2,192,1536]{2,1,0:T(8,128)}, f32[2,192,4608]{2,1,0:T(8,128)}, f32[2,160,1536]{2,1,0:T(8,128)}, f32[2,768,1536]{2,1,0:T(8,128)}, f32[2,32...) custom-call(f32[2,192,1536]{2,1,0:T(8,128)} %fusion.13.output_ref, ...), custom_call_target="tpu_custom_call" | custom-call | tf_op jit(solution)/shard_map/backward_sums/pallas_call | solution.py:1903
  910.6 17.7 %exchange.9 = (f32[3,10,384]{2,1,0:T(8,128)S(1)}, f32[3,19,320]{2,1,0:T(8,128)S(1)}) custom-call(f32[4,10,384]{2,1,0:T(8,128)S(1)} %pad_maximum_fusion.5.refs_0_, f32[4,19,320]{2,1,0:T(8,128)S(1)} %reshape.483.refs_1_), custom_call_target="tpu_custom_call" | custom-call | tf_op jit(solution)/shard_map/exchange/pallas_call | solution.py:579
  934.9 40.1 %close_exchange.1 = (f32[144,1536]{1,0:T(8,128)}, f32[19,1280]{1,0:T(8,128)}, f32[8,10,384]{2,1,0:T(8,128)}, f32[24,1536]{1,0:T(8,128)}, f32[24,1536]{1,0:T(8,128)}) custom-call(f32[144,1536]{1,0:T(8,128)} %bitcast.175, f32[19,1280]{1,0:T(8,128)} %reshape.484.token_in, f32[10,384]{1,0:T(8,128)} %dynamic-slice_add_fusion.conv_in, ...), custom_call_target="tpu_custom_call" | custom-call | tf_op jit(solution)/shard_map/close_exchange/pallas_call | solution.py:2051
  982.1 11.3 %deliver.1 = (f32[320,1536]{1,0:T(8,128)}, f32[384,6144]{1,0:T(8,128)}) custom-call(f32[320,1536]{1,0:T(8,128)S(1)} %bitcast.150, f32[384,6144]{1,0:T(8,128)} %bitcast.157), custom_call_target="tpu_custom_call" | custom-call | tf_op jit(solution)/shard_map/deliver/pallas_call | solution.py:2083
  995.4 4.8 copy.84
  1001.5 3.2 copy.85
  (303 shorter events, 122.3 us)
Async XLA Ops:
  0.7 185.0 %copy-start = (f32[320,1536]{1,0:T(8,128)S(1)}, f32[320,1536]{1,0:T(8,128)}, u32[]{:S(2)}) copy-start(f32[320,1536]{1,0:T(8,128)} %param.39) | copy-start | bytes 5898244
  94.0 10.9 %copy-start.36 = (f32[1536]{0:T(1024)}, f32[1536]{0:T(1024)S(1)}, u32[]{:S(2)}) copy-start(f32[1536]{0:T(1024)S(1)} %get-tuple-element.189) | copy-start | bytes 18436
  94.0 10.9 %copy-start.38 = (f32[1536]{0:T(1024)}, f32[1536]{0:T(1024)S(1)}, u32[]{:S(2)}) copy-start(f32[1536]{0:T(1024)S(1)} %get-tuple-element.190) | copy-start | bytes 18436
  94.0 10.9 %copy-start.40 = (f32[1536]{0:T(1024)}, f32[1536]{0:T(1024)S(1)}, u32[]{:S(2)}) copy-start(f32[1536]{0:T(1024)S(1)} %get-tuple-element.191) | copy-start | bytes 18436
  94.0 10.9 %copy-start.42 = (f32[1536]{0:T(1024)}, f32[1536]{0:T(1024)S(1)}, u32[]{:S(2)}) copy-start(f32[1536]{0:T(1024)S(1)} %get-tuple-element.192) | copy-start | bytes 18436
  94.0 10.9 %copy-start.43 = (f32[1536]{0:T(1024)}, f32[1536]{0:T(1024)S(1)}, u32[]{:S(2)}) copy-start(f32[1536]{0:T(1024)S(1)} %get-tuple-element.193) | copy-start | bytes 18436
  94.0 10.9 %copy-start.44 = (f32[1536]{0:T(1024)}, f32[1536]{0:T(1024)S(1)}, u32[]{:S(2)}) copy-start(f32[1536]{0:T(1024)S(1)} %get-tuple-element.194) | copy-start | bytes 18436
  94.0 10.9 %copy-start.45 = (f32[1536]{0:T(1024)}, f32[1536]{0:T(1024)S(1)}, u32[]{:S(2)}) copy-start(f32[1536]{0:T(1024)S(1)} %get-tuple-element.195) | copy-start | bytes 18436
  108.5 51.3 %copy-start.67 = (f32[1536]{0:T(1024)S(1)}, f32[1536]{0:T(1024)}, u32[]{:S(2)}) copy-start(f32[1536]{0:T(1024)} %param.32) | copy-start | bytes 18436
  155.4 18.6 %copy-start.5 = (f32[4,144,1536]{2,1,0:T(8,128)}, f32[4,144,1536]{2,1,0:T(8,128)S(1)}, u32[]{:S(2)}) copy-start(f32[4,144,1536]{2,1,0:T(8,128)S(1)} %get-tuple-element.90) | copy-start | bytes 10616836
  155.4 52.5 %collective-permute-start = (f32[144,1536]{1,0:T(8,128)}, f32[144,1536]{1,0:T(8,128)}, u32[]{:S(2)}, u32[]{:S(2)}) collective-permute-start(f32[144,1536]{1,0:T(8,128)} %bitcast), channel_id=1, source_target_pairs={{0,0},{1,1},{2,2},{3,3},{4,6},{5,7},{6,4},{7,5},{8,9},{9,8},{10,11... | collective-permute-start | bytes 2654216 | tf_op jit(solution)/shard_map/ppermute | solution.py:2183
  159.8 22.7 %copy-start.47 = (f32[1536]{0:T(1024)S(1)}, f32[1536]{0:T(1024)}, u32[]{:S(2)}) copy-start(f32[1536]{0:T(1024)} %param.33) | copy-start | bytes 18436
  174.0 12.5 %copy-start.49 = (f32[4,384]{1,0:T(4,128)S(1)}, f32[4,384]{1,0:T(4,128)}, u32[]{:S(2)}) copy-start(f32[4,384]{1,0:T(4,128)} %get-tuple-element.185) | copy-start | bytes 18436
  174.0 12.5 %copy-start.48 = (f32[4,384]{1,0:T(4,128)S(1)}, f32[4,384]{1,0:T(4,128)}, u32[]{:S(2)}) copy-start(f32[4,384]{1,0:T(4,128)} %get-tuple-element.183) | copy-start | bytes 18436
  254.2 13.9 %copy-start.27 = (f32[19,1536]{1,0:T(8,128)S(1)}, f32[19,1536]{1,0:T(8,128)}, u32[]{:S(2)}) copy-start(f32[19,1536]{1,0:T(8,128)} %reduce_sum.255) | copy-start | bytes 350212
  256.2 11.9 %copy-start.55 = (f32[144]{0:T(256)S(1)}, f32[144]{0:T(256)}, u32[]{:S(2)}) copy-start(f32[144]{0:T(256)} %div.124) | copy-start | bytes 1732
  256.9 11.3 %copy-start.56 = (f32[144]{0:T(256)S(1)}, f32[144]{0:T(256)}, u32[]{:S(2)}) copy-start(f32[144]{0:T(256)} %rsqrt.25) | copy-start | bytes 1732
  256.9 26.1 %collective-permute-start.1 = (f32[144,1536]{1,0:T(8,128)}, f32[144,1536]{1,0:T(8,128)}, u32[]{:S(2)}, u32[]{:S(2)}) collective-permute-start(f32[144,1536]{1,0:T(8,128)} %collective-permute-done), channel_id=1, source_target_pairs={{0,0},{1,5},{2,10},{3,15},{4,8},{5,13},{6,2},{7,7},{8,4},{9,1},{10... | collective-permute-start | bytes 2654216 | tf_op jit(solution)/shard_map/ppermute | solution.py:2203
  265.5 62.2 %copy-start.59 = (f32[384]{0:T(512)S(1)}, f32[384]{0:T(512)}, u32[]{:S(2)}) copy-start(f32[384]{0:T(512)} %param.42) | copy-start | bytes 4612
  268.1 56.0 %copy-start.17 = (f32[144,1536]{1,0:T(8,128)}, f32[144,1536]{1,0:T(8,128)S(1)}, u32[]{:S(2)}) copy-start(f32[144,1536]{1,0:T(8,128)S(1)} %get-tuple-element.197.one_ref) | copy-start | bytes 2654212
  324.1 38.9 %collective-permute-start.2 = (f32[144,1536]{1,0:T(8,128)}, f32[144,1536]{1,0:T(8,128)}, u32[]{:S(2)}, u32[]{:S(2)}) collective-permute-start(f32[144,1536]{1,0:T(8,128)} %collective-permute-done.1.cot_ref), channel_id=1, source_target_pairs={{0,1},{1,0},{2,3},{3,2},{4,5},{5,4},{6,7},{7,6},{8,9},{9,8},{10,11... | collective-permute-start | bytes 2654216 | tf_op jit(solution)/shard_map/ppermute | solution.py:2216
  324.2 40.0 %collective-permute-start.3 = (f32[144,1536]{1,0:T(8,128)}, f32[144,1536]{1,0:T(8,128)}, u32[]{:S(2)}, u32[]{:S(2)}) collective-permute-start(f32[144,1536]{1,0:T(8,128)} %collective-permute-done.1.cot_ref), channel_id=1, source_target_pairs={{0,2},{1,3},{2,0},{3,1},{4,6},{5,7},{6,4},{7,5},{8,10},{9,11},{10,... | collective-permute-start | bytes 2654216 | tf_op jit(solution)/shard_map/ppermute | solution.py:2216
  325.4 40.3 %collective-permute-start.4 = (f32[144,1536]{1,0:T(8,128)}, f32[144,1536]{1,0:T(8,128)}, u32[]{:S(2)}, u32[]{:S(2)}) collective-permute-start(f32[144,1536]{1,0:T(8,128)} %collective-permute-done.1.cot_ref), channel_id=1, source_target_pairs={{0,3},{1,2},{2,1},{3,0},{4,7},{5,6},{6,5},{7,4},{8,11},{9,10},{10,... | collective-permute-start | bytes 2654216 | tf_op jit(solution)/shard_map/ppermute | solution.py:2216
  439.9 10.7 %copy-start.60 = (f32[32]{0:T(128)S(1)}, f32[32]{0:T(128)}, u32[]{:S(2)}) copy-start(f32[32]{0:T(128)} %broadcast_in_dim.119) | copy-start | bytes 388
  934.9 60.5 %slice-start = ((s8[9437184]{0:T(1024)(128)(4,1)}), s8[1048576]{0:T(1024)(128)(4,1)S(1)}, s32[]{:S(2)}) async-start(s8[9437184]{0:T(1024)(128)(4,1)} %bitcast.154), calls=%async_computation | async-start | bytes 2097152
  982.0 11.3 %copy-start.31 = (f32[24,1536]{1,0:T(8,128)S(1)}, f32[24,1536]{1,0:T(8,128)}, u32[]{:S(2)}) copy-start(f32[24,1536]{1,0:T(8,128)} %get-tuple-element.115) | copy-start | bytes 442372
  982.0 11.3 %copy-start.32 = (f32[24,1536]{1,0:T(8,128)S(1)}, f32[24,1536]{1,0:T(8,128)}, u32[]{:S(2)}) copy-start(f32[24,1536]{1,0:T(8,128)} %get-tuple-element.114) | copy-start | bytes 442372
  982.0 11.4 %copy-start.25 = (f32[144,1536]{1,0:T(8,128)S(1)}, f32[144,1536]{1,0:T(8,128)}, u32[]{:S(2)}) copy-start(f32[144,1536]{1,0:T(8,128)} %get-tuple-element.113) | copy-start | bytes 2654212
  982.0 11.4 %copy-start.61 = (f32[6]{0:T(128)S(1)}, f32[6]{0:T(128)}, u32[]{:S(2)}) copy-start(f32[6]{0:T(128)} %pad.32.clone) | copy-start | bytes 76
  982.0 12.5 %copy-start.24 = (f32[144,1536]{1,0:T(8,128)S(1)}, f32[144,1536]{1,0:T(8,128)}, u32[]{:S(2)}) copy-start(f32[144,1536]{1,0:T(8,128)} %get-tuple-element.107) | copy-start | bytes 2654212
  982.0 13.4 %slice-start.1 = ((s8[9437184]{0:T(1024)(128)(4,1)}), s8[4194304]{0:T(1024)(128)(4,1)S(1)}, s32[]{:S(2)}) async-start(s8[9437184]{0:T(1024)(128)(4,1)} %bitcast.154), calls=%async_computation.1 | async-start | bytes 8388608
  982.1 13.4 %slice-start.2 = ((s8[9437184]{0:T(1024)(128)(4,1)}), s8[4194304]{0:T(1024)(128)(4,1)S(1)}, s32[]{:S(2)}) async-start(s8[9437184]{0:T(1024)(128)(4,1)} %bitcast.154), calls=%async_computation.2 | async-start | bytes 8388608
  (46 other events, 211.3 us)
